TPU v7x, 32 devices: a whole 2x2x4 slice. The times are simulated.
32 devices in a mesh: wide: 8 (over y, x, core), narrow: 4 (over z).
Axes of the slice: x: 2, y: 2, z: 4, core: 2. Of those that a mesh axis runs over, the one named last changes fastest.
Arguments:
- block_in: bfloat16 [2, 4096, 1280], P(None, ('wide', 'narrow')), may hold values from -6 to 6
- cotangent: bfloat16 [2, 4096, 1280], P(None, ('wide', 'narrow')), may hold values from -6 to 6
- routes: int32 [2, 4096, 7], P(None, ('wide', 'narrow')), may hold values from 0 to 14, all different within a row; in each aligned block of 128 rows (0 to 127, 128 to 255, ..., all dimensions but the last counted through in order) at most 64 rows name the same one
- seq_ids: int32 [2, 4096], P(None, ('wide', 'narrow')), may hold values from 0 to 127, as said below
- slot_order: int32 [16], replicated, may hold values from 0 to 15, each once
- attention_in: float32 [1280, 3840], P(('wide', 'narrow')), may hold values from -0.15625 to 0.15625
- attention_in_moment: float32 [1280, 3840], P(('wide', 'narrow'))
- attention_in_average: float32 [1280, 3840], P(('wide', 'narrow')), may hold values from -0.15625 to 0.15625
- attention_out: float32 [1280, 1280], P(('wide', 'narrow')), may hold values from -0.625 to 0.625
- attention_out_moment: float32 [1280, 1280], P(('wide', 'narrow'))
- attention_out_average: float32 [1280, 1280], P(('wide', 'narrow')), may hold values from -0.625 to 0.625
- shared_in: float32 [1280, 1792], P(('wide', 'narrow')), may hold values from -0.15625 to 0.15625
- shared_in_moment: float32 [1280, 1792], P(('wide', 'narrow'))
- shared_in_average: float32 [1280, 1792], P(('wide', 'narrow')), may hold values from -0.15625 to 0.15625
- shared_out: float32 [896, 1280], P(None, ('wide', 'narrow')), may hold values from -0.1875 to 0.1875
- shared_out_moment: float32 [896, 1280], P(None, ('wide', 'narrow'))
- shared_out_average: float32 [896, 1280], P(None, ('wide', 'narrow')), may hold values from -0.1875 to 0.1875
- router: float32 [1280, 15], P(('wide', 'narrow')), may hold values from -0.078125 to 0.078125
- router_moment: float32 [1280, 15], P(('wide', 'narrow'))
- router_average: float32 [1280, 15], P(('wide', 'narrow')), may hold values from -0.078125 to 0.078125
- gains: float32 [2, 1280], P(None, ('wide', 'narrow')), may hold values from 0.5 to 1.5
- gains_moment: float32 [2, 1280], P(None, ('wide', 'narrow'))
- gains_average: float32 [2, 1280], P(None, ('wide', 'narrow')), may hold values from 0.5 to 1.5
- experts_in: float32 [16, 1280, 1792], P('narrow', 'wide'), may hold values from -0.15625 to 0.15625
- experts_in_moment: float32 [16, 1280, 1792], P('narrow', 'wide')
- experts_in_average: float32 [16, 1280, 1792], P('narrow', 'wide'), may hold values from -0.15625 to 0.15625
- experts_out: float32 [16, 896, 1280], P('narrow', None, 'wide'), may hold values from -2 to 2
- experts_out_moment: float32 [16, 896, 1280], P('narrow', None, 'wide')
- experts_out_average: float32 [16, 896, 1280], P('narrow', None, 'wide'), may hold values from -2 to 2
Outputs:
- block_out: bfloat16 [2, 4096, 1280], P(None, ('wide', 'narrow'))
- input_grad: bfloat16 [2, 4096, 1280], P(None, ('wide', 'narrow'))
- attention_in_momentum: float32 [1280, 3840], P(('wide', 'narrow'))
- attention_out_momentum: float32 [1280, 1280], P(('wide', 'narrow'))
- shared_in_momentum: float32 [1280, 1792], P(('wide', 'narrow'))
- shared_out_momentum: float32 [896, 1280], P(None, ('wide', 'narrow'))
- router_momentum: float32 [1280, 15], P(('wide', 'narrow'))
- gains_momentum: float32 [2, 1280], P(None, ('wide', 'narrow'))
- experts_in_momentum: float32 [16, 1280, 1792], P('narrow', 'wide')
- experts_out_momentum: float32 [16, 896, 1280], P('narrow', None, 'wide')
- attention_in_state: float32 [2, 1280, 3840], P(None, ('wide', 'narrow'))
- attention_out_state: float32 [2, 1280, 1280], P(None, ('wide', 'narrow'))
- shared_in_state: float32 [2, 1280, 1792], P(None, ('wide', 'narrow'))
- shared_out_state: float32 [2, 896, 1280], P(None, None, ('wide', 'narrow'))
- router_state: float32 [2, 1280, 15], P(None, ('wide', 'narrow'))
- gains_state: float32 [2, 2, 1280], P(None, None, ('wide', 'narrow'))
- experts_in_state: float32 [2, 16, 1280, 1792], P(None, 'narrow', 'wide')
- experts_out_state: float32 [2, 16, 896, 1280], P(None, 'narrow', None, 'wide')
Inputs may be any that keep to these rules, and one draw needn't show every extreme that they name: `routes`: each row names 7 different routed experts; among the rows of one device in one microbatch (aligned blocks of 128) no expert is named by more than 64 rows, a bound that some block reaches. A permutation of the slots: routed expert e sits in slot slot_order[e]; the slot in the last entry holds no expert. `seq_ids`: within each row of 128 tokens, a token's entry is the index in that row of the first token of its sequence; the first token of a row has 0, and in the first row of each microbatch the last token starts a sequence of its own.
All inputs are finite; a program needn't handle non-finite values.
Results may differ from a plain program's by a relative error of at most 0.018.
Values may be sent and summed in bfloat16 or wider, within the bound.
No kernel may reach another device: no remote copies, remote signals or barrier semaphores. Data moves between devices by JAX's collectives and lax.ppermute only.
A program may use at most 320 MiB of HBM per device.

v0:
```python
import math

import jax
import jax.numpy as jnp
from jax import lax
from jax.sharding import PartitionSpec as P

D = 1280
HEADS = 10
HEAD_DIM = 128
TOPK = 7
EXP_DEV = 4
MB = 2
MB_TOK = 128


HIGHEST = lax.Precision.HIGHEST
EPSILON = 1e-06
MOMENTUM_DECAY = 0.9
AVERAGE_DECAY = 0.99
STEP_RATES = (0.006, 0.1, 0.009, 0.0125, 0.0002, 0.011, 0.027, 8.0)
MASKED = -1e30


def rms_scale(rows_in):
    return lax.rsqrt(jnp.mean(rows_in * rows_in, axis=-1, keepdims=True) + EPSILON)


def norm_back(rows_in, scale_rows, gain_row, grad_norm):
    normed = rows_in * scale_rows
    weighted = grad_norm * gain_row
    grad_rows = scale_rows * (
        weighted - normed * jnp.mean(weighted * normed, axis=-1, keepdims=True)
    )
    return (grad_rows, jnp.sum(grad_norm * normed, axis=0))


def rotary_tables(positions):
    half_dim = HEAD_DIM // 2
    freqs = jnp.exp(jnp.arange(half_dim, dtype=jnp.float32) * (-2.0 * math.log(10000.0) / HEAD_DIM))
    angles = positions.astype(jnp.float32)[..., None] * freqs
    return (jnp.cos(angles)[..., None, :], jnp.sin(angles)[..., None, :])


def rotate(vectors, cosines, sines):
    half_dim = vectors.shape[-1] // 2
    first_half = vectors[..., :half_dim]
    second_half = vectors[..., half_dim:]
    return jnp.concatenate(
        [first_half * cosines - second_half * sines, second_half * cosines + first_half * sines],
        axis=-1,
    )


def unrotate(grads_in, cosines, sines):
    half_dim = grads_in.shape[-1] // 2
    first_half = grads_in[..., :half_dim]
    second_half = grads_in[..., half_dim:]
    return jnp.concatenate(
        [first_half * cosines + second_half * sines, second_half * cosines - first_half * sines],
        axis=-1,
    )


def swiglu_parts(pre_act):
    half_width = pre_act.shape[-1] // 2
    gate_pre = pre_act[..., :half_width]
    up_pre = pre_act[..., half_width:]
    return (gate_pre, up_pre, jax.nn.sigmoid(gate_pre))


def swiglu(pre_act):
    gate_pre, up_pre, sigmoid_gate = swiglu_parts(pre_act)
    return gate_pre * sigmoid_gate * up_pre


def swiglu_back(pre_act, grad_act):
    gate_pre, up_pre, sigmoid_gate = swiglu_parts(pre_act)
    grad_gate = grad_act * up_pre * sigmoid_gate * (1.0 + gate_pre * (1.0 - sigmoid_gate))
    grad_up = grad_act * gate_pre * sigmoid_gate
    return jnp.concatenate([grad_gate, grad_up], axis=-1)


def masked_scores(queries, keys_rot, allowed):
    scores = jnp.einsum(
        "qhd,khd->hqk", queries, keys_rot, preferred_element_type=jnp.float32
    ) * HEAD_DIM ** (-0.5)
    return jnp.where(allowed[None], scores, MASKED)


def local(
    block_in,
    cotangent,
    routes,
    seq_ids,
    slot_order,
    attention_in,
    attention_in_moment,
    attention_in_average,
    attention_out,
    attention_out_moment,
    attention_out_average,
    shared_in,
    shared_in_moment,
    shared_in_average,
    shared_out,
    shared_out_moment,
    shared_out_average,
    router,
    router_moment,
    router_average,
    gains,
    gains_moment,
    gains_average,
    experts_in,
    experts_in_moment,
    experts_in_average,
    experts_out,
    experts_out_moment,
    experts_out_average,
):
    wide_count = lax.axis_size("wide")
    narrow_count = lax.axis_size("narrow")
    slots = EXP_DEV * narrow_count
    routed = slots - 1
    capacity = (MB_TOK * TOPK * 8 // (7 * slots) + 7) // 8 * 8
    tokens = MB * MB_TOK * wide_count * narrow_count
    route_count = MB_TOK * TOPK
    bfloat = jnp.bfloat16
    single = jnp.float32
    w_attn_in, w_attn_out, w_shared_in, w_shared_out, w_router, w_gains = (
        lax.all_gather(attention_in.astype(bfloat), ("wide", "narrow"), axis=0, tiled=True),
        lax.all_gather(attention_out.astype(bfloat), ("wide", "narrow"), axis=0, tiled=True),
        lax.all_gather(shared_in.astype(bfloat), ("wide", "narrow"), axis=0, tiled=True),
        lax.all_gather(shared_out.astype(bfloat), ("wide", "narrow"), axis=1, tiled=True),
        lax.all_gather(router.astype(bfloat), ("wide", "narrow"), axis=0, tiled=True),
        lax.all_gather(gains.astype(bfloat), ("wide", "narrow"), axis=1, tiled=True),
    )
    w_experts_in, w_experts_out = (
        lax.all_gather(experts_in.astype(bfloat), "wide", axis=1, tiled=True),
        lax.all_gather(experts_out.astype(bfloat), "wide", axis=2, tiled=True),
    )
    gain_rows = w_gains.astype(single)
    router_full = w_router.astype(single)
    owner_slots = slot_order[:routed]
    expert_ids = jnp.arange(routed, dtype=jnp.int32)
    slot_ids = jnp.arange(slots, dtype=jnp.int32)
    positions = jnp.arange(MB_TOK, dtype=jnp.int32)
    block_parts = []
    grad_parts = []
    local_sums = None
    for micro_index in range(MB):
        rows_in = block_in[micro_index].astype(single)
        grad_out = cotangent[micro_index]
        grad_rows_out = grad_out.astype(single)
        route_rows = routes[micro_index]
        doc_starts = seq_ids[micro_index]
        scale_one = rms_scale(rows_in)
        first_norm = (rows_in * scale_one * gain_rows[0]).astype(bfloat)
        projected = jnp.dot(first_norm, w_attn_in, preferred_element_type=single).reshape(
            MB_TOK, 3, HEADS, HEAD_DIM
        )
        cosines, sines = rotary_tables(positions - doc_starts)
        queries = rotate(projected[:, 0], cosines, sines).astype(bfloat)
        keys_rot = rotate(projected[:, 1], cosines, sines).astype(bfloat)
        values = projected[:, 2].astype(bfloat)
        allowed = (doc_starts[:, None] == doc_starts[None, :]) & (
            positions[None, :] <= positions[:, None]
        )
        scores = masked_scores(queries, keys_rot, allowed)
        top_score = jnp.max(scores, axis=-1, keepdims=True)
        exp_scores = jnp.exp(scores - top_score)
        totals = jnp.sum(exp_scores, axis=-1, keepdims=True)
        log_totals = top_score + jnp.log(totals)
        attended = (
            jnp.einsum(
                "hqk,khd->qhd",
                (exp_scores / totals).astype(bfloat),
                values,
                preferred_element_type=single,
            )
            .astype(bfloat)
            .reshape(MB_TOK, D)
        )
        hidden = rows_in + jnp.dot(attended, w_attn_out, preferred_element_type=single)
        scale_two = rms_scale(hidden)
        second_norm = (hidden * scale_two * gain_rows[1]).astype(bfloat)
        shared_pre = jnp.dot(second_norm, w_shared_in, preferred_element_type=single)
        shared_act = swiglu(shared_pre).astype(bfloat)
        shared_branch = jnp.dot(shared_act, w_shared_out, preferred_element_type=single)
        logits = jnp.dot(second_norm, w_router, preferred_element_type=single)
        router_probs = jax.nn.softmax(logits, axis=-1)
        route_hot = (route_rows[:, :, None] == expert_ids).astype(jnp.int32)
        hot_float = route_hot.astype(single)
        gates = jnp.sum(hot_float * router_probs[:, None, :], axis=-1)
        route_slots = jnp.sum(route_hot * owner_slots, axis=-1).reshape(route_count)
        slot_hot = (route_slots[:, None] == slot_ids).astype(jnp.int32)
        ranks = jnp.sum((jnp.cumsum(slot_hot, axis=0) - 1) * slot_hot, axis=1)
        targets = route_slots * capacity + ranks
        route_table = (
            jnp.full((slots * capacity,), route_count, jnp.int32)
            .at[targets]
            .set(jnp.arange(route_count, dtype=jnp.int32))
        )
        padded_norm = jnp.concatenate([second_norm, jnp.zeros((1, D), bfloat)], axis=0)
        outgoing = padded_norm[route_table // TOPK].reshape(narrow_count, EXP_DEV, capacity, D)
        arrived = lax.all_to_all(outgoing, "narrow", split_axis=0, concat_axis=0, tiled=True)
        expert_pre = jnp.einsum(
            "aecd,edf->aecf", arrived, w_experts_in, preferred_element_type=single
        )
        expert_act = swiglu(expert_pre).astype(bfloat)
        produced = jnp.einsum(
            "aecf,efd->aecd", expert_act, w_experts_out, preferred_element_type=single
        ).astype(bfloat)
        returned = lax.all_to_all(produced, "narrow", split_axis=0, concat_axis=0, tiled=True)
        route_out = (
            returned.reshape(slots * capacity, D)[targets].reshape(MB_TOK, TOPK, D).astype(single)
        )
        block_rows = hidden + shared_branch + jnp.sum(route_out * gates[:, :, None], axis=1)
        grad_gates = jnp.sum(route_out * grad_rows_out[:, None, :], axis=-1)
        route_grads = (
            (gates[:, :, None] * grad_rows_out[:, None, :]).astype(bfloat).reshape(route_count, D)
        )
        padded_grads = jnp.concatenate([route_grads, jnp.zeros((1, D), bfloat)], axis=0)
        grad_outgoing = padded_grads[route_table].reshape(narrow_count, EXP_DEV, capacity, D)
        grad_arrived = lax.all_to_all(
            grad_outgoing, "narrow", split_axis=0, concat_axis=0, tiled=True
        )
        grad_act = jnp.einsum(
            "aecd,efd->aecf", grad_arrived, w_experts_out, preferred_element_type=single
        )
        grad_pre = swiglu_back(expert_pre, grad_act).astype(bfloat)
        grad_experts_out = jnp.einsum(
            "aecf,aecd->efd", expert_act, grad_arrived, preferred_element_type=single
        )
        grad_experts_in = jnp.einsum(
            "aecd,aecf->edf", arrived, grad_pre, preferred_element_type=single
        )
        grad_sent = jnp.einsum(
            "aecf,edf->aecd", grad_pre, w_experts_in, preferred_element_type=single
        ).astype(bfloat)
        grad_back = lax.all_to_all(grad_sent, "narrow", split_axis=0, concat_axis=0, tiled=True)
        grad_norm_experts = jnp.sum(
            grad_back.reshape(slots * capacity, D)[targets].reshape(MB_TOK, TOPK, D).astype(single),
            axis=1,
        )
        grad_probs = jnp.sum(hot_float * grad_gates[:, :, None], axis=1)
        grad_logits = router_probs * (
            grad_probs - jnp.sum(router_probs * grad_probs, axis=-1, keepdims=True)
        )
        grad_router = jnp.einsum(
            "td,te->de", second_norm.astype(single), grad_logits, precision=HIGHEST
        )
        grad_norm_router = jnp.einsum("te,de->td", grad_logits, router_full, precision=HIGHEST)
        grad_shared_out = jnp.einsum(
            "tf,td->fd", shared_act, grad_out, preferred_element_type=single
        )
        grad_shared_act = jnp.einsum(
            "td,fd->tf", grad_out, w_shared_out, preferred_element_type=single
        )
        grad_shared_pre = swiglu_back(shared_pre, grad_shared_act).astype(bfloat)
        grad_shared_in = jnp.einsum(
            "td,tf->df", second_norm, grad_shared_pre, preferred_element_type=single
        )
        grad_norm_shared = jnp.einsum(
            "tf,df->td", grad_shared_pre, w_shared_in, preferred_element_type=single
        )
        grad_second = grad_norm_shared + grad_norm_router + grad_norm_experts
        grad_hidden_norm, grad_gain_two = norm_back(hidden, scale_two, gain_rows[1], grad_second)
        grad_hidden = grad_rows_out + grad_hidden_norm
        grad_branch = grad_hidden.astype(bfloat)
        grad_attn_out = jnp.einsum(
            "td,te->de", attended, grad_branch, preferred_element_type=single
        )
        grad_attended = (
            jnp.einsum("te,de->td", grad_branch, w_attn_out, preferred_element_type=single)
            .astype(bfloat)
            .reshape(MB_TOK, HEADS, HEAD_DIM)
        )
        probs_again = jnp.exp(masked_scores(queries, keys_rot, allowed) - log_totals)
        grad_values = jnp.einsum(
            "hqk,qhd->khd", probs_again.astype(bfloat), grad_attended, preferred_element_type=single
        )
        grad_probs_attn = jnp.einsum(
            "qhd,khd->hqk", grad_attended, values, preferred_element_type=single
        )
        grad_scores = (
            probs_again
            * (grad_probs_attn - jnp.sum(probs_again * grad_probs_attn, axis=-1, keepdims=True))
        ).astype(bfloat)
        grad_queries = jnp.einsum(
            "hqk,khd->qhd", grad_scores, keys_rot, preferred_element_type=single
        ) * HEAD_DIM ** (-0.5)
        grad_keys = jnp.einsum(
            "hqk,qhd->khd", grad_scores, queries, preferred_element_type=single
        ) * HEAD_DIM ** (-0.5)
        grad_projected = (
            jnp.stack(
                [
                    unrotate(grad_queries, cosines, sines),
                    unrotate(grad_keys, cosines, sines),
                    grad_values,
                ],
                axis=1,
            )
            .astype(bfloat)
            .reshape(MB_TOK, 3 * D)
        )
        grad_attn_in = jnp.einsum(
            "td,te->de", first_norm, grad_projected, preferred_element_type=single
        )
        grad_first = jnp.einsum(
            "te,de->td", grad_projected, w_attn_in, preferred_element_type=single
        )
        grad_rows_norm, grad_gain_one = norm_back(rows_in, scale_one, gain_rows[0], grad_first)
        grad_rows_in = (grad_hidden + grad_rows_norm).astype(bfloat)
        micro_grads_local = (
            grad_attn_in,
            grad_attn_out,
            grad_shared_in,
            grad_shared_out,
            grad_router,
            jnp.stack([grad_gain_one, grad_gain_two]),
            grad_experts_in,
            grad_experts_out,
        )
        block_rows, grad_rows, grads_local = (
            block_rows.astype(bfloat),
            grad_rows_in,
            micro_grads_local,
        )
        block_parts.append(block_rows)
        grad_parts.append(grad_rows)
        local_sums = (
            grads_local
            if local_sums is None
            else tuple((earlier + latest for earlier, latest in zip(local_sums, grads_local)))
        )
    dense_shares = (
        lax.psum_scatter(local_sums[0], ("wide", "narrow"), scatter_dimension=0, tiled=True),
        lax.psum_scatter(local_sums[1], ("wide", "narrow"), scatter_dimension=0, tiled=True),
        lax.psum_scatter(local_sums[2], ("wide", "narrow"), scatter_dimension=0, tiled=True),
        lax.psum_scatter(local_sums[3], ("wide", "narrow"), scatter_dimension=1, tiled=True),
        lax.psum_scatter(local_sums[4], ("wide", "narrow"), scatter_dimension=0, tiled=True),
        lax.psum_scatter(local_sums[5], ("wide", "narrow"), scatter_dimension=1, tiled=True),
    )
    expert_shares = (
        lax.psum_scatter(
            local_sums[6].astype(jnp.bfloat16), "wide", scatter_dimension=1, tiled=True
        ).astype(jnp.float32),
        lax.psum_scatter(
            local_sums[7].astype(jnp.bfloat16), "wide", scatter_dimension=2, tiled=True
        ).astype(jnp.float32),
    )
    summed = tuple(dense_shares) + tuple(expert_shares)
    masters = (
        attention_in,
        attention_out,
        shared_in,
        shared_out,
        router,
        gains,
        experts_in,
        experts_out,
    )
    moments = (
        attention_in_moment,
        attention_out_moment,
        shared_in_moment,
        shared_out_moment,
        router_moment,
        gains_moment,
        experts_in_moment,
        experts_out_moment,
    )
    averages = (
        attention_in_average,
        attention_out_average,
        shared_in_average,
        shared_out_average,
        router_average,
        gains_average,
        experts_in_average,
        experts_out_average,
    )
    base_rate = 1.0 / math.sqrt(tokens)
    moment_outs = []
    states = []
    for master, moment, average, grad_share, step_rate in zip(
        masters, moments, averages, summed, STEP_RATES
    ):
        moment_new = MOMENTUM_DECAY * moment + grad_share
        master_new = master - step_rate * base_rate * (grad_share + MOMENTUM_DECAY * moment_new)
        average_new = AVERAGE_DECAY * average + (1.0 - AVERAGE_DECAY) * master_new
        moment_outs.append(moment_new)
        states.append(jnp.stack([average_new, master_new]))
    block_out = jnp.stack(block_parts)
    input_grad = jnp.stack(grad_parts)
    return (
        block_out,
        input_grad,
        moment_outs[0],
        moment_outs[1],
        moment_outs[2],
        moment_outs[3],
        moment_outs[4],
        moment_outs[5],
        moment_outs[6],
        moment_outs[7],
        states[0],
        states[1],
        states[2],
        states[3],
        states[4],
        states[5],
        states[6],
        states[7],
    )


def solution(mesh):
    in_specs = (
        P(None, ("wide", "narrow"), None),
        P(None, ("wide", "narrow"), None),
        P(None, ("wide", "narrow"), None),
        P(None, ("wide", "narrow")),
        P(),
        P(("wide", "narrow"), None),
        P(("wide", "narrow"), None),
        P(("wide", "narrow"), None),
        P(("wide", "narrow"), None),
        P(("wide", "narrow"), None),
        P(("wide", "narrow"), None),
        P(("wide", "narrow"), None),
        P(("wide", "narrow"), None),
        P(("wide", "narrow"), None),
        P(None, ("wide", "narrow")),
        P(None, ("wide", "narrow")),
        P(None, ("wide", "narrow")),
        P(("wide", "narrow"), None),
        P(("wide", "narrow"), None),
        P(("wide", "narrow"), None),
        P(None, ("wide", "narrow")),
        P(None, ("wide", "narrow")),
        P(None, ("wide", "narrow")),
        P("narrow", "wide", None),
        P("narrow", "wide", None),
        P("narrow", "wide", None),
        P("narrow", None, "wide"),
        P("narrow", None, "wide"),
        P("narrow", None, "wide"),
    )
    out_specs = (
        P(None, ("wide", "narrow"), None),
        P(None, ("wide", "narrow"), None),
        P(("wide", "narrow"), None),
        P(("wide", "narrow"), None),
        P(("wide", "narrow"), None),
        P(None, ("wide", "narrow")),
        P(("wide", "narrow"), None),
        P(None, ("wide", "narrow")),
        P("narrow", "wide", None),
        P("narrow", None, "wide"),
        P(None, ("wide", "narrow"), None),
        P(None, ("wide", "narrow"), None),
        P(None, ("wide", "narrow"), None),
        P(None, None, ("wide", "narrow")),
        P(None, ("wide", "narrow"), None),
        P(None, None, ("wide", "narrow")),
        P(None, "narrow", "wide", None),
        P(None, "narrow", None, "wide"),
    )
    return jax.shard_map(local, mesh=mesh, in_specs=in_specs, out_specs=out_specs, check_vma=False)
```

profile of v0, /device:TPU:0, one launch (start us, length us, event | category | flops | bytes accessed | tf_op | source)
XLA Modules:
  0.0 1896.4 jit_solution(1152674261958745614)
XLA Ops:
  17.3 69.9 %all-gather = bf16[32,40,2]{1,2,0:T(2,128)(2,1)S(1)} all-gather(bf16[1,40,2]{1,2,0:T(2,128)(2,1)S(1)} %convert_bitcast_fusion.3), channel_id=1, replica_groups=mesh['wide'=8,'narrow'=4] {'wide','narrow'}, dimensions={0}, use_global_device_ids=true | all-gather | bytes 5280 | tf_op jit(solution)/shard_map/all_gather | solution.py:137
  98.0 13.8 copy.240
  119.7 39.6 %all-gather.11.cloned.1.call-done = bf16[1280,1280]{1,0:T(8,128)(2,1)} async-done(((bf16[40,1280]{1,0:T(8,128)(2,1)}), bf16[1280,1280]{1,0:T(8,128)(2,1)}) %all-gather.11.cloned.1.call-update) | async-done | bytes 3276816 | tf_op jit(solution)/shard_map/all_gather | solution.py:133
  173.2 119.1 %all-gather.1 = bf16[32,40,15]{1,2,0:T(8,128)(2,1)S(1)} all-gather(bf16[1,40,15]{1,2,0:T(8,128)(2,1)S(1)} %convert_bitcast_fusion.2), channel_id=1, replica_groups=mesh['wide'=8,'narrow'=4] {'wide','narrow'}, dimensions={0}, use_global_device_ids=true | all-gather | bytes 39600 | tf_op jit(solution)/shard_map/all_gather | solution.py:136
  317.3 15.0 fusion.20
  332.3 46.6 %all-to-all-done.4 = bf16[4,4,64,1280]{3,2,1,0:T(8,128)(2,1)S(1)} async-done(((bf16[4,4,64,1280]{3,2,1,0:T(8,128)(2,1)}), bf16[4,4,64,1280]{3,2,1,0:T(8,128)(2,1)S(1)}, u32[]{:S(2)}, u32[]{:S(2)}) %all-to-all-start.4) | async-done | bytes 2621472 | tf_op jit(solution)/shard_map/all_to_all | solution.py:226
  419.2 48.7 %all-to-all-done.5 = bf16[4,4,64,1280]{3,2,1,0:T(8,128)(2,1)S(1)} async-done(((bf16[4,4,64,1280]{3,2,1,0:T(8,128)(2,1)}), bf16[4,4,64,1280]{3,2,1,0:T(8,128)(2,1)S(1)}, u32[]{:S(2)}, u32[]{:S(2)}) %all-to-all-start.5) | async-done | bytes 2621472 | tf_op jit(solution)/shard_map/all_to_all | solution.py:242
  511.3 26.1 %all-to-all-done.1 = bf16[4,4,64,1280]{3,2,1,0:T(8,128)(2,1)} async-done(((bf16[4,4,64,1280]{3,2,1,0:T(8,128)(2,1)}), bf16[4,4,64,1280]{3,2,1,0:T(8,128)(2,1)}, u32[]{:S(2)}, u32[]{:S(2)}) %all-to-all-start.1) | async-done | bytes 2621472 | tf_op jit(solution)/shard_map/all_to_all | solution.py:215
  592.1 40.1 %all-to-all-done.2 = bf16[4,4,64,1280]{3,2,1,0:T(8,128)(2,1)} async-done(((bf16[4,4,64,1280]{3,2,1,0:T(8,128)(2,1)}), bf16[4,4,64,1280]{3,2,1,0:T(8,128)(2,1)}, u32[]{:S(2)}, u32[]{:S(2)}) %all-to-all-start.2) | async-done | bytes 2621472 | tf_op jit(solution)/shard_map/all_to_all | solution.py:207
  635.9 15.0 fusion.23
  650.9 43.9 %all-to-all-done.6 = bf16[4,4,64,1280]{3,2,1,0:T(8,128)(2,1)S(1)} async-done(((bf16[4,4,64,1280]{3,2,1,0:T(8,128)(2,1)}), bf16[4,4,64,1280]{3,2,1,0:T(8,128)(2,1)S(1)}, u32[]{:S(2)}, u32[]{:S(2)}) %all-to-all-start.6) | async-done | bytes 2621472 | tf_op jit(solution)/shard_map/all_to_all | solution.py:226
  732.5 48.1 %all-to-all-done.3 = bf16[4,4,64,1280]{3,2,1,0:T(8,128)(2,1)S(1)} async-done(((bf16[4,4,64,1280]{3,2,1,0:T(8,128)(2,1)}), bf16[4,4,64,1280]{3,2,1,0:T(8,128)(2,1)S(1)}, u32[]{:S(2)}, u32[]{:S(2)}) %all-to-all-start.3) | async-done | bytes 2621472 | tf_op jit(solution)/shard_map/all_to_all | solution.py:215
  814.0 14.0 fusion.1
  858.5 53.2 %all-to-all-done.7 = bf16[4,4,64,1280]{3,2,1,0:T(8,128)(2,1)S(1)} async-done(((bf16[4,4,64,1280]{3,2,1,0:T(8,128)(2,1)}), bf16[4,4,64,1280]{3,2,1,0:T(8,128)(2,1)S(1)}, u32[]{:S(2)}, u32[]{:S(2)}) %all-to-all-start.7) | async-done | bytes 2621472 | tf_op jit(solution)/shard_map/all_to_all | solution.py:242
  934.4 19.3 %fusion.49 = f32[4,1280,1792,1]{2,1,0,3:T(8,128)} fusion(bf16[4,4,64,1280]{3,2,1,0:T(8,128)(2,1)} %all-to-all-done, bf16[4,4,64,896]{3,2,0,1:T(8,128)(2,1)} %get-tuple-element.165, bf16[4,4,64,896]{3,2,0,1:T(8,128)(2,1)S(1)} %copy-done.181), kind=kOutput, calls=%fused_computation.70 | convolution fusion | flops 4704960512 | bytes 42991616 | tf_op jit(solution)/shard_map/aecd,aecf->edf/dot_general | solution.py:236
  953.8 20.7 %fusion = bf16[4,1280,1792]{2,1,0:T(8,128)(2,1)} fusion(f32[4,1280,1792,1]{2,1,0,3:T(8,128)} %fusion.49, bf16[4,4,64,1280]{3,2,1,0:T(8,128)(2,1)} %all-to-all-done.2, bf16[4,4,64,896]{3,2,0,1:T(8,128)(2,1)} %get-tuple-element.167, bf16[4,4,64,896]{3,2,0,1:T(8,128)(2,1)} %get-tuple-element.166), kind=kOutput, calls=%fused_computation.11 | convolution fusion | flops 4723310592 | bytes 61341696 | tf_op jit(solution)/shard_map/aecd,aecf->edf/dot_general | solution.py:236
  1002.9 12.5 convolution_add_fusion
  1035.5 40.8 %all-reduce.6 = f32[2,1280]{1,0:T(2,128)S(1)} all-reduce(f32[2,1280]{1,0:T(2,128)S(1)} %maximum_add_fusion), channel_id=7, replica_groups=mesh['wide'=8,'narrow'=4] {'wide','narrow'}, use_global_device_ids=true, to_apply=%region_49.50.clone | all-reduce | flops 2560 | bytes 20480
  1085.8 15.3 reduce-scatter.22.cloned.1.call-done
  1103.9 74.1 %reduce-scatter.20.cloned.1.call-done = bf16[4,896,160]{1,2,0:T(8,128)(2,1)} async-done(((bf16[4,896,1280]{1,2,0:T(8,128)(2,1)}), bf16[4,896,160]{1,2,0:T(8,128)(2,1)}) %reduce-scatter.20.cloned.1.call-update) | async-done | bytes 1146896 | tf_op jit(solution)/shard_map/reduce_scatter | solution.py:351
  1185.5 197.5 %reduce-scatter.16.cloned.1.call-done = f32[40,1792]{1,0:T(8,128)} async-done(((f32[1280,1792]{1,0:T(8,128)}), f32[40,1792]{1,0:T(8,128)}) %reduce-scatter.16.cloned.1.call-update) | async-done | bytes 286736 | tf_op jit(solution)/shard_map/reduce_scatter | solution.py:342
  1386.1 157.1 %reduce-scatter.14.cloned.1.call-done = f32[40,1280]{1,0:T(8,128)} async-done(((f32[1280,1280]{1,0:T(8,128)}), f32[40,1280]{1,0:T(8,128)}) %reduce-scatter.14.cloned.1.call-update) | async-done | bytes 204816 | tf_op jit(solution)/shard_map/reduce_scatter | solution.py:341
  1546.1 122.8 %reduce-scatter.18.cloned.1.call-done = bf16[4,160,1792]{2,1,0:T(8,128)(2,1)} async-done(((bf16[4,1280,1792]{2,1,0:T(8,128)(2,1)}), bf16[4,160,1792]{2,1,0:T(8,128)(2,1)}) %reduce-scatter.18.cloned.1.call-update) | async-done | bytes 2293776 | tf_op jit(solution)/shard_map/reduce_scatter | solution.py:348
  1688.8 197.9 %reduce-scatter.12.cloned.1.call-done = f32[40,3840]{1,0:T(8,128)} async-done(((f32[1280,3840]{1,0:T(8,128)}), f32[40,3840]{1,0:T(8,128)}) %reduce-scatter.12.cloned.1.call-update) | async-done | bytes 614416 | tf_op jit(solution)/shard_map/reduce_scatter | solution.py:340
  (614 shorter events, 428.1 us)
Async XLA Ops:
  7.2 90.8 %all-gather.9.cloned.1.call-start = ((), (), s32[]{:S(2)}) async-start(), calls=%async_computation.14 | async-start | bytes 10137600 | tf_op jit(solution)/shard_map/all_gather | solution.py:132
  9.1 150.2 %all-gather.11.cloned.1.call-start = ((), (), s32[]{:S(2)}) async-start(), calls=%async_computation.15 | async-start | bytes 3379200 | tf_op jit(solution)/shard_map/all_gather | solution.py:133
  10.8 306.5 %all-gather.17.cloned.1.call-start = ((), (), s32[]{:S(2)}) async-start(), calls=%async_computation.18 | async-start | bytes 20643840 | tf_op jit(solution)/shard_map/all_gather | solution.py:140
  14.9 317.4 %all-gather.19.cloned.1.call-start = ((), (), s32[]{:S(2)}) async-start(), calls=%async_computation.19 | async-start | bytes 10321920 | tf_op jit(solution)/shard_map/all_gather | solution.py:141
  95.5 384.4 %copy-start.74 = (f32[1280]{0:T(1024)}, f32[1280]{0:T(1024)S(1)}, u32[]{:S(2)}) copy-start(f32[1280]{0:T(1024)S(1)} %get-tuple-element.143) | copy-start | bytes 15364
  168.5 143.2 %all-to-all-start = ((bf16[4,4,64,1280]{3,2,1,0:T(8,128)(2,1)}), bf16[4,4,64,1280]{3,2,1,0:T(8,128)(2,1)}, u32[]{:S(2)}, u32[]{:S(2)}) async-start(bf16[4,4,64,1280]{3,2,1,0:T(8,128)(2,1)} %bitcast.420), calls=%async_computation | async-start | bytes 5242880 | tf_op jit(solution)/shard_map/all_to_all | solution.py:207
  311.7 67.2 %all-to-all-start.4 = ((bf16[4,4,64,1280]{3,2,1,0:T(8,128)(2,1)}), bf16[4,4,64,1280]{3,2,1,0:T(8,128)(2,1)S(1)}, u32[]{:S(2)}, u32[]{:S(2)}) async-start(bf16[4,4,64,1280]{3,2,1,0:T(8,128)(2,1)} %bitcast.421), calls=%async_computation.4 | async-start | bytes 5242880 | tf_op jit(solution)/shard_map/all_to_all | solution.py:226
  315.4 175.3 %all-gather.13.cloned.1.call-start = ((), (), s32[]{:S(2)}) async-start(), calls=%async_computation.16 | async-start | bytes 4730880 | tf_op jit(solution)/shard_map/all_gather | solution.py:134
  403.0 64.9 %all-to-all-start.5 = ((bf16[4,4,64,1280]{3,2,1,0:T(8,128)(2,1)}), bf16[4,4,64,1280]{3,2,1,0:T(8,128)(2,1)S(1)}, u32[]{:S(2)}, u32[]{:S(2)}) async-start(bf16[4,4,64,1280]{3,2,1,0:T(8,128)(2,1)} %copy.267), calls=%async_computation.5 | async-start | bytes 5242880 | tf_op jit(solution)/shard_map/all_to_all | solution.py:242
  406.8 94.5 %all-gather.15.cloned.1.call-start = ((), (), s32[]{:S(2)}) async-start(), calls=%async_computation.17 | async-start | bytes 2365440 | tf_op jit(solution)/shard_map/all_gather | solution.py:135
  467.9 69.6 %all-to-all-start.1 = ((bf16[4,4,64,1280]{3,2,1,0:T(8,128)(2,1)}), bf16[4,4,64,1280]{3,2,1,0:T(8,128)(2,1)}, u32[]{:S(2)}, u32[]{:S(2)}) async-start(bf16[4,4,64,1280]{3,2,1,0:T(8,128)(2,1)} %copy.250), calls=%async_computation.1 | async-start | bytes 5242880 | tf_op jit(solution)/shard_map/all_to_all | solution.py:215
  568.6 63.7 %all-to-all-start.2 = ((bf16[4,4,64,1280]{3,2,1,0:T(8,128)(2,1)}), bf16[4,4,64,1280]{3,2,1,0:T(8,128)(2,1)}, u32[]{:S(2)}, u32[]{:S(2)}) async-start(bf16[4,4,64,1280]{3,2,1,0:T(8,128)(2,1)} %bitcast.422), calls=%async_computation.2 | async-start | bytes 5242880 | tf_op jit(solution)/shard_map/all_to_all | solution.py:207
  632.3 62.5 %all-to-all-start.6 = ((bf16[4,4,64,1280]{3,2,1,0:T(8,128)(2,1)}), bf16[4,4,64,1280]{3,2,1,0:T(8,128)(2,1)S(1)}, u32[]{:S(2)}, u32[]{:S(2)}) async-start(bf16[4,4,64,1280]{3,2,1,0:T(8,128)(2,1)} %bitcast.423), calls=%async_computation.6 | async-start | bytes 5242880 | tf_op jit(solution)/shard_map/all_to_all | solution.py:226
  718.0 62.5 %all-to-all-start.3 = ((bf16[4,4,64,1280]{3,2,1,0:T(8,128)(2,1)}), bf16[4,4,64,1280]{3,2,1,0:T(8,128)(2,1)S(1)}, u32[]{:S(2)}, u32[]{:S(2)}) async-start(bf16[4,4,64,1280]{3,2,1,0:T(8,128)(2,1)} %copy.262), calls=%async_computation.3 | async-start | bytes 5242880 | tf_op jit(solution)/shard_map/all_to_all | solution.py:215
  721.7 362.1 %all-reduce.9.cloned.1.call-start = ((), (), s32[]{:S(2)}) async-start(), calls=%async_computation.25 | async-start | bytes 163840
  796.1 304.9 %reduce-scatter.22.cloned.1.call-start = ((), (), s32[]{:S(2)}) async-start(), calls=%async_computation.26 | async-start | bytes 4730880
  801.5 376.6 %reduce-scatter.20.cloned.1.call-start = ((), (), s32[]{:S(2)}) async-start(), calls=%async_computation.24 | async-start | bytes 10321920 | tf_op jit(solution)/shard_map/reduce_scatter | solution.py:351
  828.1 555.0 %reduce-scatter.16.cloned.1.call-start = ((), (), s32[]{:S(2)}) async-start(), calls=%async_computation.22 | async-start | bytes 9461760 | tf_op jit(solution)/shard_map/reduce_scatter | solution.py:342
  848.6 63.1 %all-to-all-start.7 = ((bf16[4,4,64,1280]{3,2,1,0:T(8,128)(2,1)}), bf16[4,4,64,1280]{3,2,1,0:T(8,128)(2,1)S(1)}, u32[]{:S(2)}, u32[]{:S(2)}) async-start(bf16[4,4,64,1280]{3,2,1,0:T(8,128)(2,1)} %copy.276), calls=%async_computation.7 | async-start | bytes 5242880 | tf_op jit(solution)/shard_map/all_to_all | solution.py:242
  852.3 691.0 %reduce-scatter.14.cloned.1.call-start = ((), (), s32[]{:S(2)}) async-start(), calls=%async_computation.21 | async-start | bytes 6758400 | tf_op jit(solution)/shard_map/reduce_scatter | solution.py:341
  932.9 736.0 %reduce-scatter.18.cloned.1.call-start = ((), (), s32[]{:S(2)}) async-start(), calls=%async_computation.23 | async-start | bytes 20643840 | tf_op jit(solution)/shard_map/reduce_scatter | solution.py:348
  974.5 912.2 %reduce-scatter.12.cloned.1.call-start = ((), (), s32[]{:S(2)}) async-start(), calls=%async_computation.20 | async-start | bytes 20275200 | tf_op jit(solution)/shard_map/reduce_scatter | solution.py:340
  1185.5 357.8 %copy-start.110 = (f32[40,1280]{1,0:T(8,128)S(1)}, f32[40,1280]{1,0:T(8,128)}, u32[]{:S(2)}) copy-start(f32[40,1280]{1,0:T(8,128)} %param.39) | copy-start | bytes 614404
  1185.5 357.8 %copy-start.111 = (f32[40,1280]{1,0:T(8,128)S(1)}, f32[40,1280]{1,0:T(8,128)}, u32[]{:S(2)}) copy-start(f32[40,1280]{1,0:T(8,128)} %param.38) | copy-start | bytes 614404
  (179 other events, 4319.6 us)
Sparse Core Ops, SparseCore 0:
  11.4 86.5 all-gather.8
  101.4 57.9 all-gather.10
  161.8 95.6 all-gather.16
  259.9 57.8 all-gather.18
  321.0 84.8 all-gather.12
  410.7 90.5 all-gather.14
  796.3 148.4 all-reduce.8
  947.6 153.3 reduce-scatter.21
  1104.7 73.3 reduce-scatter.19
  1180.9 202.0 reduce-scatter.15
  1385.4 157.7 reduce-scatter.13
  1547.3 121.6 reduce-scatter.17
  1675.4 211.2 reduce-scatter.11
where the time goes:
time: 1910 us; the launch traced here: 1900 us
  waiting for transfers between devices  1120 us (59%)
  matrix products  273 us (14%)
  blocking collectives  230 us (12%)
  local copies, waits for them, and re-layouts  128 us (7%)
  other arithmetic  96.5 us (5%)
  starting transfers between devices  33.8 us (2%)
    reduce_scatter x1, waiting for transfers between devices, local(): lax.psum_scatter(local_sums[0], ('wide', 'narrow'), scatter_dimension=0,...  198 us
    reduce_scatter x1, waiting for transfers between devices, local(): lax.psum_scatter(local_sums[2], ('wide', 'narrow'), scatter_dimension=0,...  198 us
    reduce_scatter x1, waiting for transfers between devices, local(): lax.psum_scatter(local_sums[1], ('wide', 'narrow'), scatter_dimension=0,...  157 us
    reduce_scatter x1, waiting for transfers between devices, local(): lax.psum_scatter(local_sums[6].astype(jnp.bfloat16), 'wide', scatter_dime...  123 us
    all_gather x1, blocking collectives, local(): lax.all_gather(router.astype(bfloat), ('wide', 'narrow'), axis=0, tiled=T...  119 us
    all_to_all x2, waiting for transfers between devices, local(): lax.all_to_all(grad_sent, 'narrow', split_axis=0, concat_axis=0, tiled=True)  102 us
    all_to_all x2, waiting for transfers between devices, local(): lax.all_to_all(grad_outgoing, 'narrow', split_axis=0, concat_axis=0, tile...  90.5 us
    all_to_all x2, waiting for transfers between devices, local(): lax.all_to_all(produced, 'narrow', split_axis=0, concat_axis=0, tiled=True)  74.2 us
  transfers between devices with their start and end apart: 21, of which 15 were waited for; matrix products, arithmetic and copies ran while one was open for 22% of the time, Pallas kernels for 0%

commit v1 on v0

v1 whole, which is shorter than its diff:
```python
import math

import jax
import jax.numpy as jnp
from jax import lax
from jax.sharding import PartitionSpec as P

D = 1280
HEADS = 10
HEAD_DIM = 128
FF = 896
TOPK = 7
EXP_DEV = 4
MB = 2
MB_TOK = 128
LANES = 128

HIGHEST = lax.Precision.HIGHEST
EPSILON = 1e-06
MOMENTUM_DECAY = 0.9
AVERAGE_DECAY = 0.99
STEP_RATES = (0.006, 0.1, 0.009, 0.0125, 0.0002, 0.011, 0.027, 8.0)
MASKED = -1e30

ECOLS = 3 * FF
ACOLS = 4 * D + LANES
bfloat = jnp.bfloat16
single = jnp.float32


def split_cols(cols):
    return (cols // LANES + 1) // 2 * LANES


def dot(a, b, dims=(((1,), (0,)), ((), ()))):
    return lax.dot_general(a, b, dims, preferred_element_type=single)


NT = (((1,), (1,)), ((), ()))
TN = (((0,), (0,)), ((), ()))


def rms_scale(rows_in):
    return lax.rsqrt(jnp.mean(rows_in * rows_in, axis=-1, keepdims=True) + EPSILON)


def norm_back(rows_in, scale_rows, gain_row, grad_norm):
    normed = rows_in * scale_rows
    weighted = grad_norm * gain_row
    grad_rows = scale_rows * (
        weighted - normed * jnp.mean(weighted * normed, axis=-1, keepdims=True)
    )
    return (grad_rows, jnp.sum(grad_norm * normed, axis=0))


def rotary_tables(positions):
    half_dim = HEAD_DIM // 2
    freqs = jnp.exp(jnp.arange(half_dim, dtype=jnp.float32) * (-2.0 * math.log(10000.0) / HEAD_DIM))
    angles = positions.astype(jnp.float32)[..., None] * freqs
    return (jnp.cos(angles)[..., None, :], jnp.sin(angles)[..., None, :])


def rotate(vectors, cosines, sines):
    half_dim = vectors.shape[-1] // 2
    first_half = vectors[..., :half_dim]
    second_half = vectors[..., half_dim:]
    return jnp.concatenate(
        [first_half * cosines - second_half * sines, second_half * cosines + first_half * sines],
        axis=-1,
    )


def swiglu(gate_pre, up_pre):
    return gate_pre * jax.nn.sigmoid(gate_pre) * up_pre


def swiglu_back(gate_pre, up_pre, grad_act):
    sigmoid_gate = jax.nn.sigmoid(gate_pre)
    grad_gate = grad_act * up_pre * sigmoid_gate * (1.0 + gate_pre * (1.0 - sigmoid_gate))
    grad_up = grad_act * gate_pre * sigmoid_gate
    return (grad_gate, grad_up)


def wide_xor(piece, bit):
    count = lax.axis_size("wide")
    return lax.ppermute(piece, "wide", [(i, i ^ bit) for i in range(count)])


def ring(piece):
    count = lax.axis_size("narrow")
    return lax.ppermute(piece, "narrow", [(i, (i + 1) % count) for i in range(count)])


def chip_bits():
    bits, bit = [], 2
    while bit < lax.axis_size("wide"):
        bits.append(bit)
        bit *= 2
    return bits


def gather_plane(shard):
    cut = split_cols(shard.shape[1])
    halves = []
    for part, order in (
        (shard[:, :cut], chip_bits()),
        (shard[:, cut:], chip_bits()[::-1]),
    ):
        pieces = {0: part}
        for bit in order:
            pieces.update({r | bit: wide_xor(p, bit) for r, p in list(pieces.items())})
        pieces.update({r | 1: wide_xor(p, 1) for r, p in list(pieces.items())})
        halves.append(pieces)
    return [(halves[0][r], halves[1][r]) for r in range(lax.axis_size("wide"))]


def assemble(pieces):
    me = lax.axis_index("wide")
    rows, cut = pieces[0][0].shape
    full = jnp.zeros((len(pieces) * rows, cut + pieces[0][1].shape[1]), bfloat)
    for r, (left, right) in enumerate(pieces):
        full = lax.dynamic_update_slice(full, left, ((me ^ r) * rows, 0))
        full = lax.dynamic_update_slice(full, right, ((me ^ r) * rows, cut))
    return full


def place(pieces):
    level = lax.axis_index("narrow")
    count = len(pieces)
    full = jnp.zeros((count, *pieces[0].shape), pieces[0].dtype)
    for s, piece in enumerate(pieces):
        full = lax.dynamic_update_index_in_dim(full, piece, (level - s) % count, 0)
    return full


def scatter_plane(full):
    wide_count = lax.axis_size("wide")
    me = lax.axis_index("wide")
    rows = full.shape[0] // wide_count
    view = full.astype(bfloat).reshape(wide_count // 2, 2, rows, full.shape[1])
    core = me & 1
    give = lax.dynamic_index_in_dim(view, 1 - core, axis=1, keepdims=False)
    keep = lax.dynamic_index_in_dim(view, core, axis=1, keepdims=False)
    total = keep.astype(single) + wide_xor(give, 1).astype(single)
    cut = split_cols(full.shape[1])
    parts = []
    bit_count = len(chip_bits())
    for part, order in (
        (total[..., :cut], list(range(bit_count))[::-1]),
        (total[..., cut:], list(range(bit_count))),
    ):
        blocks = part.astype(bfloat)
        present = list(range(bit_count))
        for bit_index in order:
            give, keep = halves(blocks, present.index(bit_index), (me >> (bit_index + 1)) & 1)
            present.remove(bit_index)
            summed = keep.astype(single) + wide_xor(give, 2 << bit_index).astype(single)
            blocks = summed.astype(bfloat)
        parts.append(summed[0])
    return jnp.concatenate(parts, axis=1)


def halves(blocks, place, own):
    count = blocks.shape[0]
    low = 1 << place
    view = blocks.reshape(count // (2 * low), 2, low, *blocks.shape[1:])
    give = lax.dynamic_index_in_dim(view, 1 - own, axis=1, keepdims=False)
    keep = lax.dynamic_index_in_dim(view, own, axis=1, keepdims=False)
    shape = (count // 2, *blocks.shape[1:])
    return give.reshape(shape), keep.reshape(shape)


def ring_gather(piece):
    pieces = [piece]
    for _ in range(lax.axis_size("narrow") - 1):
        pieces.append(ring(pieces[-1]))
    return pieces


def ring_scatter(block_of):
    count = lax.axis_size("narrow")
    total = block_of(1).astype(bfloat)
    for step in range(1, count):
        arrived = ring(total)
        last = step == count - 1
        total = arrived.astype(single) + block_of((step + 1) % count).astype(single)
        if not last:
            total = total.astype(bfloat)
    return total


def local(
    block_in,
    cotangent,
    routes,
    seq_ids,
    slot_order,
    attention_in,
    attention_in_moment,
    attention_in_average,
    attention_out,
    attention_out_moment,
    attention_out_average,
    shared_in,
    shared_in_moment,
    shared_in_average,
    shared_out,
    shared_out_moment,
    shared_out_average,
    router,
    router_moment,
    router_average,
    gains,
    gains_moment,
    gains_average,
    experts_in,
    experts_in_moment,
    experts_in_average,
    experts_out,
    experts_out_moment,
    experts_out_average,
):
    wide_count = lax.axis_size("wide")
    narrow_count = lax.axis_size("narrow")
    level = lax.axis_index("narrow")
    slots = EXP_DEV * narrow_count
    routed = slots - 1
    capacity = (MB_TOK * TOPK * 8 // (7 * slots) + 7) // 8 * 8
    tokens = MB * MB_TOK * wide_count * narrow_count
    own_tokens = MB * MB_TOK
    rows_dense = D // (wide_count * narrow_count)
    rows_plane = D // wide_count
    blocks = MB * narrow_count
    quarter = FF // narrow_count
    shared_width = (quarter + LANES - 1) // LANES * LANES

    pad_small = jnp.zeros((rows_dense, LANES - routed - 2), bfloat)
    attention_pack = jnp.concatenate(
        [
            attention_in.astype(bfloat),
            attention_out.astype(bfloat),
            router.astype(bfloat),
            gains.T.astype(bfloat),
            pad_small,
        ],
        axis=1,
    )
    shared_pack = jnp.concatenate([shared_in, shared_out.T], axis=1).astype(bfloat)
    shared_pack = shared_pack.reshape(rows_dense, 3, narrow_count, quarter)
    shared_pack = jnp.pad(shared_pack, ((0, 0), (0, 0), (0, 0), (0, shared_width - quarter)))
    shared_pack = shared_pack.transpose(2, 0, 1, 3).reshape(
        narrow_count, rows_dense, 3 * shared_width
    )
    shared_piece = lax.all_to_all(
        shared_pack, "narrow", split_axis=0, concat_axis=0, tiled=True
    ).reshape(rows_plane, 3 * shared_width)
    expert_pack = jnp.concatenate(
        [experts_in, experts_out.transpose(0, 2, 1)], axis=2
    ).astype(bfloat)
    expert_piece = jnp.concatenate(
        [expert_pack[e] for e in range(EXP_DEV)] + [shared_piece], axis=1
    )

    route_hot = (routes[..., None] == jnp.arange(routed, dtype=jnp.int32)).astype(single).sum(axis=2)
    slot_hot_of_expert = (
        slot_order[:routed, None] == jnp.arange(slots, dtype=jnp.int32)
    ).astype(single)
    chosen = jnp.dot(route_hot.reshape(own_tokens, routed), slot_hot_of_expert)
    grad_out = cotangent.reshape(own_tokens, D)
    token_pack = jnp.concatenate(
        [grad_out, jnp.pad(chosen.astype(bfloat), ((0, 0), (0, LANES - slots)))], axis=1
    )
    token_parts = ring_gather(token_pack)

    attention_parts = ring_gather(attention_pack)
    attention_piece = place(attention_parts).reshape(rows_plane, ACOLS)
    attention_full = assemble(gather_plane(attention_piece))
    expert_full = assemble(gather_plane(expert_piece))

    w_attn_in = attention_full[:, : 3 * D]
    w_attn_out = attention_full[:, 3 * D : 4 * D]
    w_router = attention_full[:, 4 * D : 4 * D + routed]
    gain_rows = attention_full[:, 4 * D + routed : 4 * D + routed + 2].T.astype(single)
    router_slots = jnp.dot(w_router, slot_hot_of_expert.astype(bfloat))
    empty = jnp.sum(slot_hot_of_expert, axis=0) == 0.0

    rows_in = block_in.reshape(own_tokens, D).astype(single)
    grad_rows_out = grad_out.astype(single)
    positions = jnp.arange(MB_TOK, dtype=jnp.int32)
    scale_one = rms_scale(rows_in)
    first_norm = (rows_in * scale_one * gain_rows[0]).astype(bfloat)
    projected = dot(first_norm, w_attn_in).reshape(MB, MB_TOK, 3, HEADS, HEAD_DIM)
    cosines, sines = rotary_tables(positions - seq_ids)
    queries = rotate(projected[:, :, 0], cosines, sines).astype(bfloat)
    keys_rot = rotate(projected[:, :, 1], cosines, sines).astype(bfloat)
    values = projected[:, :, 2].astype(bfloat)
    allowed = (seq_ids[:, :, None] == seq_ids[:, None, :]) & (
        positions[None, None, :] <= positions[None, :, None]
    )
    scores = jnp.einsum(
        "bqhd,bkhd->bhqk", queries, keys_rot, preferred_element_type=single
    ) * HEAD_DIM ** (-0.5)
    scores = jnp.where(allowed[:, None], scores, MASKED)
    probs = jax.nn.softmax(scores, axis=-1)
    probs_low = probs.astype(bfloat)
    attended = (
        jnp.einsum("bhqk,bkhd->bqhd", probs_low, values, preferred_element_type=single)
        .astype(bfloat)
        .reshape(own_tokens, D)
    )
    hidden = rows_in + dot(attended, w_attn_out)
    scale_two = rms_scale(hidden)
    second_norm = (hidden * scale_two * gain_rows[1]).astype(bfloat)
    router_probs = jax.nn.softmax(
        jnp.where(empty, MASKED, dot(second_norm, router_slots)), axis=-1
    )

    norm_parts = ring_gather(second_norm)
    norm_all = jnp.concatenate(norm_parts, axis=0)
    token_all = jnp.concatenate(token_parts, axis=0)
    dy_all = token_all[:, :D]
    chosen_all = token_all[:, D : D + slots].astype(single)
    gates_all = chosen_all * jax.nn.softmax(
        jnp.where(empty, MASKED, dot(norm_all, router_slots)), axis=-1
    )
    chosen_mine = lax.dynamic_slice_in_dim(chosen_all, level * EXP_DEV, EXP_DEV, axis=1)
    gates_mine = lax.dynamic_slice_in_dim(gates_all, level * EXP_DEV, EXP_DEV, axis=1)
    chosen_mine = chosen_mine.reshape(blocks, MB_TOK, EXP_DEV)
    gates_mine = gates_mine.reshape(blocks, MB_TOK, EXP_DEV)
    below = (positions[:, None] > positions[None, :]).astype(single)
    ranks = jnp.einsum("tu,bue->bte", below, chosen_mine)
    select = (
        (ranks[:, :, :, None] == jnp.arange(capacity, dtype=single))
        & (chosen_mine[:, :, :, None] > 0.5)
    ).transpose(2, 0, 3, 1)
    select_low = select.astype(bfloat)
    count_rows = blocks * capacity
    norm_blocks = norm_all.reshape(blocks, MB_TOK, D)
    dy_blocks = dy_all.reshape(blocks, MB_TOK, D)

    out_sum = jnp.zeros((blocks, MB_TOK, D), single)
    grad_sum = jnp.zeros((blocks, MB_TOK, D), single)
    q_cols = []
    expert_grads = []
    for e in range(EXP_DEV):
        w_in = expert_full[:, e * ECOLS : e * ECOLS + 2 * FF]
        w_out = expert_full[:, e * ECOLS + 2 * FF : (e + 1) * ECOLS]
        sel = select_low[e]
        rows = jnp.einsum("brt,btd->brd", sel, norm_blocks, preferred_element_type=single)
        rows = rows.astype(bfloat).reshape(count_rows, D)
        dy_rows = jnp.einsum("brt,btd->brd", sel, dy_blocks, preferred_element_type=single)
        dy_rows = dy_rows.reshape(count_rows, D)
        gate_rows = jnp.sum(
            jnp.where(select[e], gates_mine[:, None, :, e], 0.0), axis=-1
        ).reshape(count_rows, 1)
        pre = dot(rows, w_in)
        gate_pre, up_pre = pre[:, :FF], pre[:, FF:]
        act = swiglu(gate_pre, up_pre).astype(bfloat)
        out = dot(act, w_out, NT).astype(bfloat).astype(single)
        q_rows = jnp.sum(out * dy_rows, axis=-1)
        q_cols.append(
            jnp.sum(
                jnp.where(select[e], q_rows.reshape(blocks, capacity, 1), 0.0), axis=1
            )
        )
        grad_rows_exp = (gate_rows * dy_rows).astype(bfloat)
        grad_act = dot(grad_rows_exp, w_out)
        grad_gate, grad_up = swiglu_back(gate_pre, up_pre, grad_act)
        grad_pre = jnp.concatenate([grad_gate, grad_up], axis=1).astype(bfloat)
        expert_grads.append(dot(rows, grad_pre, TN))
        expert_grads.append(dot(grad_rows_exp, act, TN))
        back = dot(grad_pre, w_in, NT).astype(bfloat).reshape(blocks, capacity, D)
        weighted = (gate_rows * out).astype(bfloat).reshape(blocks, capacity, D)
        out_sum += jnp.einsum("brt,brd->btd", sel, weighted, preferred_element_type=single)
        grad_sum += jnp.einsum("brt,brd->btd", sel, back, preferred_element_type=single)
    base = EXP_DEV * ECOLS
    w_gate = expert_full[:, base : base + shared_width]
    w_up = expert_full[:, base + shared_width : base + 2 * shared_width]
    w_down = expert_full[:, base + 2 * shared_width :]
    gate_pre, up_pre = dot(norm_all, w_gate), dot(norm_all, w_up)
    act = swiglu(gate_pre, up_pre).astype(bfloat)
    out_sum += dot(act, w_down, NT).reshape(blocks, MB_TOK, D)
    grad_gate, grad_up = swiglu_back(gate_pre, up_pre, dot(dy_all, w_down))
    grad_gate, grad_up = grad_gate.astype(bfloat), grad_up.astype(bfloat)
    grad_sum += (dot(grad_gate, w_gate, NT) + dot(grad_up, w_up, NT)).reshape(
        blocks, MB_TOK, D
    )
    expert_grads += [dot(norm_all, grad_gate, TN), dot(norm_all, grad_up, TN), dot(dy_all, act, TN)]
    expert_grads = [g.astype(bfloat) for g in expert_grads]

    out_parts = out_sum.reshape(narrow_count, own_tokens, D)
    grad_parts = grad_sum.reshape(narrow_count, own_tokens, D)
    q_sent = jnp.stack(q_cols, axis=-1).reshape(narrow_count, own_tokens, EXP_DEV)
    q_sent = place([q_sent[s] for s in range(narrow_count)])
    q_back = lax.all_to_all(q_sent, "narrow", split_axis=0, concat_axis=0, tiled=True)
    q_slots = q_back.transpose(1, 0, 2).reshape(own_tokens, slots)

    grad_second = ring_scatter(lambda s: grad_parts[s])
    grad_logits = router_probs * (
        q_slots - jnp.sum(router_probs * q_slots, axis=-1, keepdims=True)
    )
    grad_router = jnp.dot(
        jnp.dot(second_norm.astype(single).T, grad_logits, precision=HIGHEST),
        slot_hot_of_expert.T,
        precision=HIGHEST,
    )
    grad_second = grad_second + lax.dot_general(
        grad_logits, router_slots.astype(single), NT, precision=HIGHEST
    )
    grad_hidden_norm, grad_gain_two = norm_back(hidden, scale_two, gain_rows[1], grad_second)
    grad_hidden = grad_rows_out + grad_hidden_norm
    grad_branch = grad_hidden.astype(bfloat)
    grad_attn_out = dot(attended, grad_branch, TN)
    grad_attended = (
        dot(grad_branch, w_attn_out, NT).astype(bfloat).reshape(MB, MB_TOK, HEADS, HEAD_DIM)
    )
    grad_values = jnp.einsum(
        "bhqk,bqhd->bkhd", probs_low, grad_attended, preferred_element_type=single
    )
    grad_probs = jnp.einsum(
        "bqhd,bkhd->bhqk", grad_attended, values, preferred_element_type=single
    )
    grad_scores = (
        probs * (grad_probs - jnp.sum(probs * grad_probs, axis=-1, keepdims=True))
    ).astype(bfloat)
    grad_queries = jnp.einsum(
        "bhqk,bkhd->bqhd", grad_scores, keys_rot, preferred_element_type=single
    ) * HEAD_DIM ** (-0.5)
    grad_keys = jnp.einsum(
        "bhqk,bqhd->bkhd", grad_scores, queries, preferred_element_type=single
    ) * HEAD_DIM ** (-0.5)
    grad_projected = (
        jnp.stack(
            [rotate(grad_queries, cosines, -sines), rotate(grad_keys, cosines, -sines), grad_values],
            axis=2,
        )
        .astype(bfloat)
        .reshape(own_tokens, 3 * D)
    )
    grad_attn_in = dot(first_norm, grad_projected, TN)
    grad_first = dot(grad_projected, w_attn_in, NT)
    grad_rows_norm, grad_gain_one = norm_back(rows_in, scale_one, gain_rows[0], grad_first)
    input_grad = (grad_hidden + grad_rows_norm).astype(bfloat).reshape(MB, MB_TOK, D)

    routed_sum = ring_scatter(lambda s: out_parts[s])
    block_out = (hidden + routed_sum).astype(bfloat).reshape(MB, MB_TOK, D)

    attention_grads = jnp.concatenate(
        [
            grad_attn_in.astype(bfloat),
            grad_attn_out.astype(bfloat),
            grad_router.astype(bfloat),
            jnp.stack([grad_gain_one, grad_gain_two], axis=1).astype(bfloat),
            jnp.zeros((D, LANES - routed - 2), bfloat),
        ],
        axis=1,
    )
    expert_share = scatter_plane(jnp.concatenate(expert_grads, axis=1))
    attention_share = scatter_plane(attention_grads).reshape(narrow_count, rows_dense, ACOLS)
    attention_share = ring_scatter(
        lambda s: lax.dynamic_index_in_dim(
            attention_share, (level - s) % narrow_count, axis=0, keepdims=False
        )
    )
    shared_share = expert_share[:, base:].astype(bfloat).reshape(
        narrow_count, rows_dense, 3 * shared_width
    )
    shared_share = lax.all_to_all(
        shared_share, "narrow", split_axis=0, concat_axis=0, tiled=True
    ).reshape(narrow_count, rows_dense, 3, shared_width)[..., :quarter]
    shared_share = shared_share.transpose(1, 2, 0, 3).reshape(rows_dense, 3 * FF).astype(single)

    summed = (
        attention_share[:, : 3 * D],
        attention_share[:, 3 * D : 4 * D],
        shared_share[:, : 2 * FF],
        shared_share[:, 2 * FF :].T,
        attention_share[:, 4 * D : 4 * D + routed],
        attention_share[:, 4 * D + routed : 4 * D + routed + 2].T,
        jnp.stack([expert_share[:, e * ECOLS : e * ECOLS + 2 * FF] for e in range(EXP_DEV)]),
        jnp.stack(
            [expert_share[:, e * ECOLS + 2 * FF : (e + 1) * ECOLS].T for e in range(EXP_DEV)]
        ),
    )
    masters = (
        attention_in,
        attention_out,
        shared_in,
        shared_out,
        router,
        gains,
        experts_in,
        experts_out,
    )
    moments = (
        attention_in_moment,
        attention_out_moment,
        shared_in_moment,
        shared_out_moment,
        router_moment,
        gains_moment,
        experts_in_moment,
        experts_out_moment,
    )
    averages = (
        attention_in_average,
        attention_out_average,
        shared_in_average,
        shared_out_average,
        router_average,
        gains_average,
        experts_in_average,
        experts_out_average,
    )
    base_rate = 1.0 / math.sqrt(tokens)
    moment_outs = []
    states = []
    for master, moment, average, grad_share, step_rate in zip(
        masters, moments, averages, summed, STEP_RATES
    ):
        moment_new = MOMENTUM_DECAY * moment + grad_share
        master_new = master - step_rate * base_rate * (grad_share + MOMENTUM_DECAY * moment_new)
        average_new = AVERAGE_DECAY * average + (1.0 - AVERAGE_DECAY) * master_new
        moment_outs.append(moment_new)
        states.append(jnp.stack([average_new, master_new]))
    return (block_out, input_grad, *moment_outs, *states)


def solution(mesh):
    both = ("wide", "narrow")
    token = P(None, both, None)
    rows = P(both, None)
    cols = P(None, both)
    weight_specs = [rows, rows, rows, cols, rows, cols, P("narrow", "wide", None), P("narrow", None, "wide")]
    in_specs = (token, token, token, P(None, both), P()) + tuple(
        spec for spec in weight_specs for _ in range(3)
    )
    out_specs = (token, token, *weight_specs, *(P(None, *spec) for spec in weight_specs))
    return jax.shard_map(local, mesh=mesh, in_specs=in_specs, out_specs=out_specs, check_vma=False)
```

time: 1910 us -> 1270 us (0.66)
  waiting for transfers between devices: 1120 us -> 335 us
  local copies, waits for them, and re-layouts: 128 us -> 506 us
  blocking collectives: 230 us -> 0 us
  matrix products: 273 us -> 200 us
  other arithmetic: 96.5 us -> 156 us
  starting transfers between devices: 33.8 us -> 57.2 us
    reduce_scatter x5 -> x0, waiting for transfers between devices: 749 us -> none  [the longest x1 198 us: local(): lax.psum_scatter(local_sums[0], ('wide', 'narrow'), scatter_dimension=0,...]
    ppermute x0 -> x56, waiting for transfers between devices: none -> 335 us  [the longest x38 197 us: wide_xor(): return lax.ppermute(piece, 'wide', [(i, i ^ bit) for i in range(count)])]
    all_to_all x8 -> x3, waiting for transfers between devices: 307 us -> 0.01 us  [the longest x1 0.01 us: local(): lax.all_to_all(q_sent, 'narrow', split_axis=0, concat_axis=0, tiled=True)]
    dynamic_update_slice x0 -> x38, local copies, waits for them, and re-layouts: none -> 287 us  [the longest x15 144 us: assemble(): full = lax.dynamic_update_slice(full, left, ((me ^ r) * rows, 0))]
    all_gather x2 -> x0, blocking collectives: 189 us -> none  [the longest x1 119 us: local(): lax.all_gather(router.astype(bfloat), ('wide', 'narrow'), axis=0, tiled=T...]
    dot_general x54 -> x68, matrix products: 273 us -> 196 us  [the longest x41 145 us: dot(): return lax.dot_general(a, b, dims, preferred_element_type=single)]
    ppermute x0 -> x56, starting transfers between devices: none -> 46.4 us  [the longest x38 28.5 us: wide_xor(): return lax.ppermute(piece, 'wide', [(i, i ^ bit) for i in range(count)])]
    all_gather x6 -> x0, waiting for transfers between devices: 46.2 us -> none  [the longest x1 39.6 us: local(): lax.all_gather(attention_out.astype(bfloat), ('wide', 'narrow'), axis=0,...]
  transfers between devices with their start and end apart: 21 -> 59, of which waited for: 15 -> 22; matrix products, arithmetic and copies ran while one was open for 22% -> 47% of each run, Pallas kernels for 0% -> 0%
where the time goes in v1:
time: 1270 us; the launch traced here: 1260 us
  local copies, waits for them, and re-layouts  506 us (40%)
  waiting for transfers between devices  335 us (26%)
  matrix products  200 us (16%)
  other arithmetic  156 us (12%)
  starting transfers between devices  57.2 us (5%)
    ppermute x38, waiting for transfers between devices, wide_xor(): return lax.ppermute(piece, 'wide', [(i, i ^ bit) for i in range(count)])  197 us
    dot_general x41, matrix products, dot(): return lax.dot_general(a, b, dims, preferred_element_type=single)  145 us
    dynamic_update_slice x15, local copies, waits for them, and re-layouts, assemble(): full = lax.dynamic_update_slice(full, left, ((me ^ r) * rows, 0))  144 us
    dynamic_update_slice x15, local copies, waits for them, and re-layouts, assemble(): full = lax.dynamic_update_slice(full, right, ((me ^ r) * rows, cut))  139 us
    ppermute x18, waiting for transfers between devices, ring(): lax.ppermute(piece, 'narrow', [(i, (i + 1) % count) for i in range(count)])  138 us
    unnamed x393, local copies, waits for them, and re-layouts  56.8 us
    another operation x24, other arithmetic, local(): states.append(jnp.stack([average_new, master_new]))  35.9 us
    ppermute x14, local copies, waits for them, and re-layouts, wide_xor(): return lax.ppermute(piece, 'wide', [(i, i ^ bit) for i in range(count)])  32.6 us
  transfers between devices with their start and end apart: 59, of which 22 were waited for; matrix products, arithmetic and copies ran while one was open for 47% of the time, Pallas kernels for 0%

profile of v1, /device:TPU:0, one launch (start us, length us, event | category | flops | bytes accessed | tf_op | source)
XLA Modules:
  0.0 1257.1 jit_solution(6989296849202437983)
XLA Ops:
  56.6 24.1 %collective-permute-done.2 = bf16[40,5248]{1,0:T(8,128)(2,1)S(1)} collective-permute-done((bf16[40,5248]{1,0:T(8,128)(2,1)S(1)}, bf16[40,5248]{1,0:T(8,128)(2,1)S(1)}, u32[]{:S(2)}, u32[]{:S(2)}) %collective-permute-start.2) | collective-permute-done | bytes 419872 | tf_op jit(solution)/shard_map/ppermute | solution.py:91
  149.3 15.5 %dynamic_update_slice.128 = bf16[1280,5248]{0,1:T(8,128)(2,1)} dynamic-update-slice(bf16[1280,5248]{0,1:T(8,128)(2,1)} %dynamic_update_slice.127, bf16[160,2688]{0,1:T(8,128)(2,1)S(1)} %copy.415, s32[]{:T(128)S(6)} %select_n.198, s32[]{:T(128)} %constant.221.clone.1) | dynamic-update-slice | bytes 1720324 | tf_op jit(solution)/shard_map/dynamic_update_slice | solution.py:122
  164.8 15.3 %dynamic_update_slice.129 = bf16[1280,5248]{0,1:T(8,128)(2,1)} dynamic-update-slice(bf16[1280,5248]{0,1:T(8,128)(2,1)} %dynamic_update_slice.128, bf16[160,2560]{0,1:T(8,128)(2,1)} %copy.416, s32[]{:T(128)S(6)} %select_n.198, s32[]{:T(128)} %constant.231.clone.1) | dynamic-update-slice | bytes 1638404 | tf_op jit(solution)/shard_map/dynamic_update_slice | solution.py:123
  182.3 15.5 %dynamic_update_slice.130 = bf16[1280,5248]{0,1:T(8,128)(2,1)} dynamic-update-slice(bf16[1280,5248]{0,1:T(8,128)(2,1)} %dynamic_update_slice.129, bf16[160,2688]{0,1:T(8,128)(2,1)S(1)} %copy.417, s32[]{:T(128)S(6)} %select_n.199, s32[]{:T(128)} %constant.221.clone.1) | dynamic-update-slice | bytes 1720324 | tf_op jit(solution)/shard_map/dynamic_update_slice | solution.py:122
  197.8 15.3 %dynamic_update_slice.131 = bf16[1280,5248]{0,1:T(8,128)(2,1)} dynamic-update-slice(bf16[1280,5248]{0,1:T(8,128)(2,1)} %dynamic_update_slice.130, bf16[160,2560]{0,1:T(8,128)(2,1)} %copy.418, s32[]{:T(128)S(6)} %select_n.199, s32[]{:T(128)} %constant.231.clone.1) | dynamic-update-slice | bytes 1638404 | tf_op jit(solution)/shard_map/dynamic_update_slice | solution.py:123
  231.0 25.5 %collective-permute-done.26 = bf16[160,5760]{1,0:T(8,128)(2,1)} collective-permute-done((bf16[160,5760]{1,0:T(8,128)(2,1)}, bf16[160,5760]{1,0:T(8,128)(2,1)}, u32[]{:S(2)}, u32[]{:S(2)}) %collective-permute-start.26) | collective-permute-done | bytes 1843232 | tf_op jit(solution)/shard_map/ppermute | solution.py:86
  291.6 16.2 %dynamic_update_slice.132 = bf16[1280,5248]{0,1:T(8,128)(2,1)} dynamic-update-slice(bf16[1280,5248]{0,1:T(8,128)(2,1)} %dynamic_update_slice.131, bf16[160,2688]{0,1:T(8,128)(2,1)} %copy.419, s32[]{:T(128)S(6)} %select_n.200, s32[]{:T(128)} %constant.221.clone.1) | dynamic-update-slice | bytes 1720324 | tf_op jit(solution)/shard_map/dynamic_update_slice | solution.py:122
  307.8 15.3 %dynamic_update_slice.133 = bf16[1280,5248]{0,1:T(8,128)(2,1)} dynamic-update-slice(bf16[1280,5248]{0,1:T(8,128)(2,1)} %dynamic_update_slice.132, bf16[160,2560]{0,1:T(8,128)(2,1)} %copy.420, s32[]{:T(128)S(6)} %select_n.200, s32[]{:T(128)} %constant.231.clone.1) | dynamic-update-slice | bytes 1638404 | tf_op jit(solution)/shard_map/dynamic_update_slice | solution.py:123
  323.1 14.3 %dynamic_update_slice.134 = bf16[1280,5248]{0,1:T(8,128)(2,1)} dynamic-update-slice(bf16[1280,5248]{0,1:T(8,128)(2,1)} %dynamic_update_slice.133, bf16[160,2688]{0,1:T(8,128)(2,1)} %copy.421, s32[]{:T(128)S(6)} %select_n.201, s32[]{:T(128)} %constant.221.clone.1) | dynamic-update-slice | bytes 1720324 | tf_op jit(solution)/shard_map/dynamic_update_slice | solution.py:122
  353.2 16.1 %dynamic_update_slice.136 = bf16[1280,5248]{0,1:T(8,128)(2,1)} dynamic-update-slice(bf16[1280,5248]{0,1:T(8,128)(2,1)} %dynamic_update_slice.135, bf16[160,2688]{0,1:T(8,128)(2,1)} %copy.423, s32[]{:T(128)S(6)} %select_n.202, s32[]{:T(128)} %constant.221.clone.1) | dynamic-update-slice | bytes 1720324 | tf_op jit(solution)/shard_map/dynamic_update_slice | solution.py:122
  369.3 15.3 %dynamic_update_slice.137 = bf16[1280,5248]{0,1:T(8,128)(2,1)} dynamic-update-slice(bf16[1280,5248]{0,1:T(8,128)(2,1)} %dynamic_update_slice.136, bf16[160,2560]{0,1:T(8,128)(2,1)} %copy.424, s32[]{:T(128)S(6)} %select_n.202, s32[]{:T(128)} %constant.231.clone.1) | dynamic-update-slice | bytes 1638404 | tf_op jit(solution)/shard_map/dynamic_update_slice | solution.py:123
  387.0 16.5 %dynamic_update_slice.138 = bf16[1280,5248]{0,1:T(8,128)(2,1)} dynamic-update-slice(bf16[1280,5248]{0,1:T(8,128)(2,1)} %dynamic_update_slice.137, bf16[160,2688]{0,1:T(8,128)(2,1)} %copy.425, s32[]{:T(128)S(6)} %select_n.203, s32[]{:T(128)} %constant.221.clone.1) | dynamic-update-slice | bytes 1720324 | tf_op jit(solution)/shard_map/dynamic_update_slice | solution.py:122
  403.5 15.2 %dynamic_update_slice.139 = bf16[1280,5248]{0,1:T(8,128)(2,1)} dynamic-update-slice(bf16[1280,5248]{0,1:T(8,128)(2,1)} %dynamic_update_slice.138, bf16[160,2560]{0,1:T(8,128)(2,1)} %copy.426, s32[]{:T(128)S(6)} %select_n.203, s32[]{:T(128)} %constant.231.clone.1) | dynamic-update-slice | bytes 1638404 | tf_op jit(solution)/shard_map/dynamic_update_slice | solution.py:123
  427.6 15.4 %dynamic_update_slice.140 = bf16[1280,5248]{0,1:T(8,128)(2,1)} dynamic-update-slice(bf16[1280,5248]{0,1:T(8,128)(2,1)} %dynamic_update_slice.139, bf16[160,2688]{0,1:T(8,128)(2,1)} %copy.427, s32[]{:T(128)S(6)} %select_n.204, s32[]{:T(128)} %constant.221.clone.1) | dynamic-update-slice | bytes 1720324 | tf_op jit(solution)/shard_map/dynamic_update_slice | solution.py:122
  443.0 15.2 %dynamic_update_slice.141 = bf16[1280,5248]{0,1:T(8,128)(2,1)} dynamic-update-slice(bf16[1280,5248]{0,1:T(8,128)(2,1)} %dynamic_update_slice.140, bf16[160,2560]{0,1:T(8,128)(2,1)} %copy.428, s32[]{:T(128)S(6)} %select_n.204, s32[]{:T(128)} %constant.231.clone.1) | dynamic-update-slice | bytes 1638404 | tf_op jit(solution)/shard_map/dynamic_update_slice | solution.py:123
  512.7 14.3 %collective-permute-done.21 = bf16[256,1280]{1,0:T(8,128)(2,1)S(1)} collective-permute-done((bf16[256,1280]{1,0:T(8,128)(2,1)S(1)}, bf16[256,1280]{1,0:T(8,128)(2,1)S(1)}, u32[]{:S(2)}, u32[]{:S(2)}) %collective-permute-start.21) | collective-permute-done | bytes 655392 | tf_op jit(solution)/shard_map/ppermute | solution.py:91
  530.0 14.8 %collective-permute-done.22 = bf16[256,1280]{1,0:T(8,128)(2,1)S(1)} collective-permute-done((bf16[256,1280]{1,0:T(8,128)(2,1)S(1)}, bf16[256,1280]{1,0:T(8,128)(2,1)S(1)}, u32[]{:S(2)}, u32[]{:S(2)}) %collective-permute-start.22) | collective-permute-done | bytes 655392 | tf_op jit(solution)/shard_map/ppermute | solution.py:91
  774.4 14.7 %collective-permute-done.37 = bf16[256,1280]{1,0:T(8,128)(2,1)} collective-permute-done((bf16[256,1280]{1,0:T(8,128)(2,1)}, bf16[256,1280]{1,0:T(8,128)(2,1)}, u32[]{:S(2)}, u32[]{:S(2)}) %collective-permute-start.37) | collective-permute-done | bytes 655392 | tf_op jit(solution)/shard_map/ppermute | solution.py:91
  871.1 18.8 %concatenate.91 = bf16[1280,5248]{1,0:T(8,128)(2,1)} concatenate(bf16[1280,3840]{1,0:T(8,128)(2,1)} %convolution_convert_fusion, bf16[1280,1280]{1,0:T(8,128)(2,1)S(1)} %convolution_convert_fusion.5, bf16[1280,15]{1,0:T(8,128)(2,1)} %copy.449, bf16[1280,1]{1,0:T(8,128)(2,1)} %stack.184, bf16[1280,1]{1,0:T(8,128)(2,1)} %stack.185, bf16[1280,111]{1,0:T(8,128)(2,1)} %broadcast_in_dim.200), dimensions={1} | concatenate | bytes 26869760 | tf_op jit(solution)/shard_map/concatenate | solution.py:448
  954.9 31.6 %collective-permute-done.46 = bf16[2,160,2560]{2,1,0:T(8,128)(2,1)} collective-permute-done((bf16[2,160,2560]{2,1,0:T(8,128)(2,1)}, bf16[2,160,2560]{2,1,0:T(8,128)(2,1)}, u32[]{:S(2)}, u32[]{:S(2)}) %collective-permute-start.46) | collective-permute-done | bytes 1638432 | tf_op jit(solution)/shard_map/ppermute | solution.py:86
  996.5 14.2 %collective-permute-done.47 = bf16[1,160,2560]{2,1,0:T(8,128)(2,1)S(1)} collective-permute-done((bf16[1,160,2560]{2,1,0:T(8,128)(2,1)S(1)}, bf16[1,160,2560]{2,1,0:T(8,128)(2,1)S(1)}, u32[]{:S(2)}, u32[]{:S(2)}) %collective-permute-start.47) | collective-permute-done | bytes 819232 | tf_op jit(solution)/shard_map/ppermute | solution.py:86
  1112.8 54.2 %collective-permute-done.52 = bf16[2,160,5760]{2,1,0:T(8,128)(2,1)} collective-permute-done((bf16[2,160,5760]{2,1,0:T(8,128)(2,1)}, bf16[2,160,5760]{2,1,0:T(8,128)(2,1)}, u32[]{:S(2)}, u32[]{:S(2)}) %collective-permute-start.52) | collective-permute-done | bytes 3686432 | tf_op jit(solution)/shard_map/ppermute | solution.py:86
  1171.3 18.3 %collective-permute-done.54 = bf16[2,160,5760]{2,1,0:T(8,128)(2,1)S(1)} collective-permute-done((bf16[2,160,5760]{2,1,0:T(8,128)(2,1)S(1)}, bf16[2,160,5760]{2,1,0:T(8,128)(2,1)S(1)}, u32[]{:S(2)}, u32[]{:S(2)}) %collective-permute-start.54) | collective-permute-done | bytes 3686432 | tf_op jit(solution)/shard_map/ppermute | solution.py:86
  1192.0 31.0 %collective-permute-done.53 = bf16[1,160,5760]{2,1,0:T(8,128)(2,1)S(1)} collective-permute-done((bf16[1,160,5760]{2,1,0:T(8,128)(2,1)S(1)}, bf16[1,160,5760]{2,1,0:T(8,128)(2,1)S(1)}, u32[]{:S(2)}, u32[]{:S(2)}) %collective-permute-start.53) | collective-permute-done | bytes 1843232 | tf_op jit(solution)/shard_map/ppermute | solution.py:86
  (794 shorter events, 791.3 us)
Async XLA Ops:
  17.6 72.3 %all-to-all-start = ((bf16[4,40,768]{2,1,0:T(8,128)(2,1)}), bf16[4,40,768]{2,1,0:T(8,128)(2,1)}, u32[]{:S(2)}, u32[]{:S(2)}) async-start(bf16[4,40,768]{2,1,0:T(8,128)(2,1)} %reshape.422), calls=%async_computation | async-start | bytes 491520 | tf_op jit(solution)/shard_map/all_to_all | solution.py:254
  39.6 49.2 %collective-permute-start.23 = (bf16[160,5760]{1,0:T(8,128)(2,1)}, bf16[160,5760]{1,0:T(8,128)(2,1)}, u32[]{:S(2)}, u32[]{:S(2)}) collective-permute-start(bf16[160,5760]{1,0:T(8,128)(2,1)} %get-tuple-element.182), channel_id=1, source_target_pairs={{0,4},{4,0},{8,12},{12,8},{16,20},{20,16},{24,28},{28,24},{1,5},{5... | collective-permute-start | bytes 5529608 | tf_op jit(solution)/shard_map/ppermute | solution.py:86
  85.9 49.9 %collective-permute-start.10 = (bf16[160,2560]{1,0:T(8,128)(2,1)}, bf16[160,2560]{1,0:T(8,128)(2,1)}, u32[]{:S(2)}, u32[]{:S(2)}) collective-permute-start(bf16[160,2560]{1,0:T(8,128)(2,1)} %slice.393), channel_id=1, source_target_pairs={{0,16},{4,20},{8,24},{12,28},{16,0},{20,4},{24,8},{28,12},{1,17},{... | collective-permute-start | bytes 2457608 | tf_op jit(solution)/shard_map/ppermute | solution.py:86
  88.9 57.1 %collective-permute-start.3 = (bf16[160,2688]{1,0:T(8,128)(2,1)}, bf16[160,2688]{1,0:T(8,128)(2,1)}, u32[]{:S(2)}, u32[]{:S(2)}) collective-permute-start(bf16[160,2688]{1,0:T(8,128)(2,1)} %slice.392), channel_id=1, source_target_pairs={{0,4},{4,0},{8,12},{12,8},{16,20},{20,16},{24,28},{28,24},{1,5},{5... | collective-permute-start | bytes 2580488 | tf_op jit(solution)/shard_map/ppermute | solution.py:86
  88.9 91.2 %collective-permute-start.5 = (bf16[160,2688]{1,0:T(8,128)(2,1)}, bf16[160,2688]{1,0:T(8,128)(2,1)}, u32[]{:S(2)}, u32[]{:S(2)}) collective-permute-start(bf16[160,2688]{1,0:T(8,128)(2,1)} %slice.392), channel_id=1, source_target_pairs={{0,8},{4,12},{8,0},{12,4},{16,24},{20,28},{24,16},{28,20},{1,9},{5... | collective-permute-start | bytes 2580488 | tf_op jit(solution)/shard_map/ppermute | solution.py:86
  89.5 123.5 %collective-permute-start.9 = (bf16[160,2688]{1,0:T(8,128)(2,1)}, bf16[160,2688]{1,0:T(8,128)(2,1)}, u32[]{:S(2)}, u32[]{:S(2)}) collective-permute-start(bf16[160,2688]{1,0:T(8,128)(2,1)} %slice.392), channel_id=1, source_target_pairs={{0,16},{4,20},{8,24},{12,28},{16,0},{20,4},{24,8},{28,12},{1,17},{... | collective-permute-start | bytes 2580488 | tf_op jit(solution)/shard_map/ppermute | solution.py:86
  130.5 92.4 %collective-permute-start.25 = (bf16[160,5760]{1,0:T(8,128)(2,1)}, bf16[160,5760]{1,0:T(8,128)(2,1)}, u32[]{:S(2)}, u32[]{:S(2)}) collective-permute-start(bf16[160,5760]{1,0:T(8,128)(2,1)} %get-tuple-element.182), channel_id=1, source_target_pairs={{0,8},{4,12},{8,0},{12,4},{16,24},{20,28},{24,16},{28,20},{1,9},{5... | collective-permute-start | bytes 5529608 | tf_op jit(solution)/shard_map/ppermute | solution.py:86
  135.8 79.8 %collective-permute-start.19 = (bf16[256,1408]{1,0:T(8,128)(2,1)}, bf16[256,1408]{1,0:T(8,128)(2,1)S(1)}, u32[]{:S(2)}, u32[]{:S(2)}) collective-permute-start(bf16[256,1408]{1,0:T(8,128)(2,1)} %collective-permute-done.18), channel_id=1, source_target_pairs={{0,1},{1,2},{2,3},{3,0},{4,5},{5,6},{6,7},{7,4},{8,9},{9,10},{10,1... | collective-permute-start | bytes 2162696 | tf_op jit(solution)/shard_map/ppermute | solution.py:91
  146.0 81.1 %collective-permute-start.29 = (bf16[160,5760]{1,0:T(8,128)(2,1)}, bf16[160,5760]{1,0:T(8,128)(2,1)}, u32[]{:S(2)}, u32[]{:S(2)}) collective-permute-start(bf16[160,5760]{1,0:T(8,128)(2,1)} %get-tuple-element.182), channel_id=1, source_target_pairs={{0,16},{4,20},{8,24},{12,28},{16,0},{20,4},{24,8},{28,12},{1,17},{... | collective-permute-start | bytes 5529608 | tf_op jit(solution)/shard_map/ppermute | solution.py:86
  256.4 162.3 %collective-permute-start.27 = (bf16[160,5760]{1,0:T(8,128)(2,1)}, bf16[160,5760]{1,0:T(8,128)(2,1)}, u32[]{:S(2)}, u32[]{:S(2)}) collective-permute-start(bf16[160,5760]{1,0:T(8,128)(2,1)} %collective-permute-done.25), channel_id=1, source_target_pairs={{0,4},{4,0},{8,12},{12,8},{16,20},{20,16},{24,28},{28,24},{1,5},{5... | collective-permute-start | bytes 5529608 | tf_op jit(solution)/shard_map/ppermute | solution.py:86
  273.6 148.1 %collective-permute-start.30 = (bf16[160,5760]{1,0:T(8,128)(2,1)}, bf16[160,5760]{1,0:T(8,128)(2,1)}, u32[]{:S(2)}, u32[]{:S(2)}) collective-permute-start(bf16[160,5760]{1,0:T(8,128)(2,1)} %get-tuple-element.180), channel_id=1, source_target_pairs={{0,16},{4,20},{8,24},{12,28},{16,0},{20,4},{24,8},{28,12},{1,17},{... | collective-permute-start | bytes 5529608 | tf_op jit(solution)/shard_map/ppermute | solution.py:86
  273.6 151.0 %collective-permute-start.33 = (bf16[160,5760]{1,0:T(8,128)(2,1)}, bf16[160,5760]{1,0:T(8,128)(2,1)}, u32[]{:S(2)}, u32[]{:S(2)}) collective-permute-start(bf16[160,5760]{1,0:T(8,128)(2,1)} %collective-permute-done.25), channel_id=1, source_target_pairs={{0,16},{4,20},{8,24},{12,28},{16,0},{20,4},{24,8},{28,12},{1,17},{... | collective-permute-start | bytes 5529608 | tf_op jit(solution)/shard_map/ppermute | solution.py:86
  278.5 143.7 %collective-permute-start.16 = (bf16[160,2560]{1,0:T(8,128)(2,1)}, bf16[160,2560]{1,0:T(8,128)(2,1)}, u32[]{:S(2)}, u32[]{:S(2)}) collective-permute-start(bf16[160,2560]{1,0:T(8,128)(2,1)} %collective-permute-done.14), channel_id=1, source_target_pairs={{0,4},{4,0},{8,12},{12,8},{16,20},{20,16},{24,28},{28,24},{1,5},{5... | collective-permute-start | bytes 2457608 | tf_op jit(solution)/shard_map/ppermute | solution.py:86
  279.3 145.4 %collective-permute-start.15 = (bf16[160,2688]{1,0:T(8,128)(2,1)}, bf16[160,2688]{1,0:T(8,128)(2,1)}, u32[]{:S(2)}, u32[]{:S(2)}) collective-permute-start(bf16[160,2688]{1,0:T(8,128)(2,1)} %collective-permute-done.13), channel_id=1, source_target_pairs={{0,4},{4,0},{8,12},{12,8},{16,20},{20,16},{24,28},{28,24},{1,5},{5... | collective-permute-start | bytes 2580488 | tf_op jit(solution)/shard_map/ppermute | solution.py:86
  418.7 80.9 %collective-permute-start.31 = (bf16[160,5760]{1,0:T(8,128)(2,1)}, bf16[160,5760]{1,0:T(8,128)(2,1)}, u32[]{:S(2)}, u32[]{:S(2)}) collective-permute-start(bf16[160,5760]{1,0:T(8,128)(2,1)} %collective-permute-done.29), channel_id=1, source_target_pairs={{0,4},{4,0},{8,12},{12,8},{16,20},{20,16},{24,28},{28,24},{1,5},{5... | collective-permute-start | bytes 5529608 | tf_op jit(solution)/shard_map/ppermute | solution.py:86
  421.7 67.4 %collective-permute-start.28 = (bf16[160,5760]{1,0:T(8,128)(2,1)}, bf16[160,5760]{1,0:T(8,128)(2,1)}, u32[]{:S(2)}, u32[]{:S(2)}) collective-permute-start(bf16[160,5760]{1,0:T(8,128)(2,1)} %collective-permute-done.26), channel_id=1, source_target_pairs={{0,4},{4,0},{8,12},{12,8},{16,20},{20,16},{24,28},{28,24},{1,5},{5... | collective-permute-start | bytes 5529608 | tf_op jit(solution)/shard_map/ppermute | solution.py:86
  422.2 80.3 %collective-permute-start.32 = (bf16[160,5760]{1,0:T(8,128)(2,1)}, bf16[160,5760]{1,0:T(8,128)(2,1)}, u32[]{:S(2)}, u32[]{:S(2)}) collective-permute-start(bf16[160,5760]{1,0:T(8,128)(2,1)} %collective-permute-done.30), channel_id=1, source_target_pairs={{0,4},{4,0},{8,12},{12,8},{16,20},{20,16},{24,28},{28,24},{1,5},{5... | collective-permute-start | bytes 5529608 | tf_op jit(solution)/shard_map/ppermute | solution.py:86
  424.6 65.9 %collective-permute-start.34 = (bf16[160,5760]{1,0:T(8,128)(2,1)}, bf16[160,5760]{1,0:T(8,128)(2,1)}, u32[]{:S(2)}, u32[]{:S(2)}) collective-permute-start(bf16[160,5760]{1,0:T(8,128)(2,1)} %collective-permute-done.30), channel_id=1, source_target_pairs={{0,8},{4,12},{8,0},{12,4},{16,24},{20,28},{24,16},{28,20},{1,9},{5... | collective-permute-start | bytes 5529608 | tf_op jit(solution)/shard_map/ppermute | solution.py:86
  424.6 102.4 %collective-permute-start.35 = (bf16[160,5760]{1,0:T(8,128)(2,1)}, bf16[160,5760]{1,0:T(8,128)(2,1)}, u32[]{:S(2)}, u32[]{:S(2)}) collective-permute-start(bf16[160,5760]{1,0:T(8,128)(2,1)} %collective-permute-done.33), channel_id=1, source_target_pairs={{0,4},{4,0},{8,12},{12,8},{16,20},{20,16},{24,28},{28,24},{1,5},{5... | collective-permute-start | bytes 5529608 | tf_op jit(solution)/shard_map/ppermute | solution.py:86
  490.5 71.1 %collective-permute-start.36 = (bf16[160,5760]{1,0:T(8,128)(2,1)}, bf16[160,5760]{1,0:T(8,128)(2,1)}, u32[]{:S(2)}, u32[]{:S(2)}) collective-permute-start(bf16[160,5760]{1,0:T(8,128)(2,1)} %collective-permute-done.34), channel_id=1, source_target_pairs={{0,4},{4,0},{8,12},{12,8},{16,20},{20,16},{24,28},{28,24},{1,5},{5... | collective-permute-start | bytes 5529608 | tf_op jit(solution)/shard_map/ppermute | solution.py:86
  932.3 138.0 %collective-permute-start.51 = (bf16[4,160,11520]{2,1,0:T(8,128)(2,1)}, bf16[4,160,11520]{2,1,0:T(8,128)(2,1)}, u32[]{:S(2)}, u32[]{:S(2)}) collective-permute-start(bf16[4,160,11520]{2,1,0:T(8,128)(2,1)} %dynamic-slice_bitcast_fusion), channel_id=1, source_target_pairs={{0,4},{4,0},{8,12},{12,8},{16,20},{20,16},{24,28},{28,24},{1,5},{5... | collective-permute-start | bytes 44236808 | tf_op jit(solution)/shard_map/ppermute | solution.py:86
  1090.4 76.6 %collective-permute-start.52 = (bf16[2,160,5760]{2,1,0:T(8,128)(2,1)}, bf16[2,160,5760]{2,1,0:T(8,128)(2,1)}, u32[]{:S(2)}, u32[]{:S(2)}) collective-permute-start(bf16[2,160,5760]{2,1,0:T(8,128)(2,1)} %dynamic-slice_bitcast_fusion.3), channel_id=1, source_target_pairs={{0,8},{4,12},{8,0},{12,4},{16,24},{20,28},{24,16},{28,20},{1,9},{5... | collective-permute-start | bytes 11059208 | tf_op jit(solution)/shard_map/ppermute | solution.py:86
  1106.9 82.7 %collective-permute-start.54 = (bf16[2,160,5760]{2,1,0:T(8,128)(2,1)S(1)}, bf16[2,160,5760]{2,1,0:T(8,128)(2,1)S(1)}, u32[]{:S(2)}, u32[]{:S(2)}) collective-permute-start(bf16[2,160,5760]{2,1,0:T(8,128)(2,1)S(1)} %dynamic-slice_bitcast_fusion.2), channel_id=1, source_target_pairs={{0,16},{4,20},{8,24},{12,28},{16,0},{20,4},{24,8},{28,12},{1,17},{... | collective-permute-start | bytes 11059208 | tf_op jit(solution)/shard_map/ppermute | solution.py:86
  1170.1 52.9 %collective-permute-start.53 = (bf16[1,160,5760]{2,1,0:T(8,128)(2,1)S(1)}, bf16[1,160,5760]{2,1,0:T(8,128)(2,1)S(1)}, u32[]{:S(2)}, u32[]{:S(2)}) collective-permute-start(bf16[1,160,5760]{2,1,0:T(8,128)(2,1)S(1)} %constant_dynamic-slice_fusion.1), channel_id=1, source_target_pairs={{0,16},{4,20},{8,24},{12,28},{16,0},{20,4},{24,8},{28,12},{1,17},{... | collective-permute-start | bytes 5529608 | tf_op jit(solution)/shard_map/ppermute | solution.py:86
  (224 other events, 2988.1 us)

commit v2 on v1

v2 whole, which is shorter than its diff:
```python
import functools
import math

import jax
import jax.numpy as jnp
from jax import lax
from jax.experimental import pallas as pl
from jax.experimental.pallas import tpu as pltpu
from jax.sharding import PartitionSpec as P

D = 1280
HEADS = 10
HEAD_DIM = 128
FF = 896
TOPK = 7
EXP_DEV = 4
MB = 2
MB_TOK = 128
LANES = 128

EPSILON = 1e-06
MOMENTUM_DECAY = 0.9
AVERAGE_DECAY = 0.99
STEP_RATES = (0.006, 0.1, 0.009, 0.0125, 0.0002, 0.011, 0.027, 8.0)
MASKED = -1e30

ECOLS = 3 * FF
ACOLS = 4 * D + LANES
bfloat = jnp.bfloat16
single = jnp.float32


def split_cols(cols):
    return (cols // LANES + 1) // 2 * LANES


def dot(a, b, dims=(((1,), (0,)), ((), ()))):
    return lax.dot_general(a, b, dims, preferred_element_type=single)


NT = (((1,), (1,)), ((), ()))
TN = (((0,), (0,)), ((), ()))


def rms_scale(rows_in):
    return lax.rsqrt(jnp.mean(rows_in * rows_in, axis=-1, keepdims=True) + EPSILON)


def wide_xor(piece, bit):
    count = lax.axis_size("wide")
    return lax.ppermute(piece, "wide", [(i, i ^ bit) for i in range(count)])


def ring(piece):
    count = lax.axis_size("narrow")
    return lax.ppermute(piece, "narrow", [(i, (i + 1) % count) for i in range(count)])


def chip_bits():
    bits, bit = [], 2
    while bit < lax.axis_size("wide"):
        bits.append(bit)
        bit *= 2
    return bits


def gather_plane(left, right):
    halves = []
    for part, order in ((left, chip_bits()), (right, chip_bits()[::-1])):
        pieces = {0: part}
        for bit in order:
            pieces.update({r | bit: wide_xor(p, bit) for r, p in list(pieces.items())})
        pieces.update({r | 1: wide_xor(p, 1) for r, p in list(pieces.items())})
        halves.append([pieces[r] for r in range(lax.axis_size("wide"))])
    return halves


def place(pieces):
    level = lax.axis_index("narrow")
    count = len(pieces)
    full = jnp.zeros((count, *pieces[0].shape), pieces[0].dtype)
    for s, piece in enumerate(pieces):
        full = lax.dynamic_update_index_in_dim(full, piece, (level - s) % count, 0)
    return full


def scatter_half(keep, give, order):
    arrived = wide_xor(give, 1)
    terms = {i: [keep[i], arrived[i]] for i in range(keep.shape[0])}
    for bit in order:
        sent = [i for i in terms if i & (bit >> 1)]
        kept = [i for i in terms if not i & (bit >> 1)]
        outgoing = jnp.stack([sum(t.astype(single) for t in terms[i]).astype(bfloat) for i in sent])
        incoming = wide_xor(outgoing, bit)
        terms = {
            i: [*terms[i], incoming[sent.index(i | (bit >> 1))]]
            for i in kept
        }
    return sum(t.astype(single) for t in terms[0])


def scatter_plane(left, right):
    order = chip_bits()
    return (
        scatter_half(*left, order[::-1]),
        scatter_half(*right, order),
    )


TILE = 256


def col_tiles(width):
    return [(at, min(TILE, width - at)) for at in range(0, width, TILE)]


def expert_body(
    wide_count, narrow_count, capacity, width, first, buffers, idx, *refs
):
    refs = list(refs)
    take = lambda count: [refs.pop(0) for _ in range(count)]
    lefts, rights = take(wide_count), take(wide_count)
    norm_parts, dy_parts = take(narrow_count), take(narrow_count)
    rank_parts, gate_parts = take(narrow_count), take(narrow_count)
    sums_in = [] if first else take(2)
    keep_left, give_left, keep_right, give_right, q_ref = take(5)
    sums_out = take(2) if first else take(2 * narrow_count)
    (w, stage, norm, dy, out_acc, grad_acc, rows, dy_rows, grad_rows, pre, act, grad_pre, sel, sel_t, gate, q_acc, turned) = take(17)
    if width:
        sw, s_stage, s_act, s_pre = take(4)
    sems = refs.pop(0)
    assert not refs
    me, slot = idx[0], idx[1]
    part = norm_parts[0].shape[0]
    total = part * narrow_count
    shard = D // wide_count
    blocks = total // MB_TOK
    per_part = part // MB_TOK

    def row_of(r):
        return pl.multiple_of((me ^ r) * shard, 16)

    def slot_row(ref, number, at):
        tile = ref[:, at : at + MB_TOK]
        mine = lax.broadcasted_iota(jnp.int32, tile.shape, 0) == number
        return jnp.sum(jnp.where(mine, tile, 0.0), axis=0, keepdims=True)

    def weight_copies(halves, buffer, sem):
        return [
            pltpu.make_async_copy(
                halves[r].at[:, pl.ds(0, ECOLS)],
                w.at[buffer, pl.ds(row_of(r), shard), :],
                sems.at[sem],
            )
            for r in range(wide_count)
        ]

    token_copies = [
        pltpu.make_async_copy(src, dst.at[pl.ds(s * part, part), :], sems.at[2])
        for parts, dst in ((norm_parts, norm), (dy_parts, dy))
        for s, src in enumerate(parts)
    ]
    sum_copies = [
        pltpu.make_async_copy(src, dst, sems.at[3])
        for src, dst in zip(sums_in, (out_acc, grad_acc))
    ]
    shared_copies = []
    if width:
        for r in range(wide_count):
            shared_copies.append(
                pltpu.make_async_copy(
                    lefts[r].at[:, pl.ds(ECOLS, width)],
                    sw.at[pl.ds(row_of(r), shard), pl.ds(0, width)],
                    sems.at[4],
                )
            )
            shared_copies.append(
                pltpu.make_async_copy(
                    rights[r].at[:, pl.ds(ECOLS, 2 * width)],
                    sw.at[pl.ds(row_of(r), shard), pl.ds(width, 2 * width)],
                    sems.at[4],
                )
            )
    expert_copies = [weight_copies(lefts, 0, 0), weight_copies(rights, buffers - 1, 1)]
    for copy in token_copies + expert_copies[0] + sum_copies:
        copy.start()
    if buffers == 2:
        for copy in expert_copies[1]:
            copy.start()
    for copy in shared_copies:
        copy.start()
    for copy in token_copies:
        copy.wait()

    waiting = []
    for e in range(2):
        buffer = e if buffers == 2 else 0
        if e == 1 and buffers == 1:
            for copy in expert_copies[1]:
                copy.start()
        for b in range(blocks):
            s, at = b // per_part, (b % per_part) * MB_TOK
            rank_row = slot_row(rank_parts[s], slot + e, at)
            gate_row = slot_row(gate_parts[s], slot + e, at)
            place_in = lax.broadcasted_iota(jnp.int32, (capacity, MB_TOK), 0).astype(single)
            hit = jnp.where(place_in == rank_row, 1.0, 0.0)
            here = pl.ds(b * capacity, capacity)
            gate_col = jnp.sum(hit * gate_row, axis=1, keepdims=True)
            gate[here, :] = jnp.broadcast_to(gate_col, (capacity, LANES))
            hit_low = hit.astype(bfloat)
            sel[here, :] = hit_low
            sel_t[pl.ds(b * MB_TOK, MB_TOK), :] = hit.T.astype(bfloat)
            tokens_here = pl.ds(b * MB_TOK, MB_TOK)
            rows[here, :] = dot(hit_low, norm[tokens_here, :]).astype(bfloat)
            picked = dot(hit_low, dy[tokens_here, :])
            dy_rows[here, :] = picked.astype(bfloat)
            grad_rows[here, :] = (gate_col * picked).astype(bfloat)
        for copy in expert_copies[e]:
            copy.wait()

        @pl.loop(0, 2 * FF // TILE)
        def _(j):
            cols = pl.ds(pl.multiple_of(j * TILE, TILE), TILE)
            pre[:, cols] = dot(rows[...], w[buffer, :, cols])

        @pl.loop(0, rows.shape[0] // 32)
        def _(i):
            here = pl.ds(pl.multiple_of(i * 32, 32), 32)
            gate_pre, up_pre = pre[here, :FF], pre[here, FF:]
            sigma = jax.nn.sigmoid(gate_pre)
            silu = gate_pre * sigma
            act[here, :] = (silu * up_pre).astype(bfloat)
            pre[here, :FF] = up_pre * sigma * (1.0 + gate_pre * (1.0 - sigma))
            pre[here, FF:] = silu

        if e == 0:
            for copy in sum_copies:
                copy.wait()
        q_acc[...] = jnp.zeros_like(q_acc)

        def add_up(acc, tile, cols, fresh):
            for b in range(blocks):
                tokens_here = pl.ds(b * MB_TOK, MB_TOK)
                term = dot(sel_t[tokens_here, :], tile[b * capacity : (b + 1) * capacity, :])
                if fresh:
                    acc[tokens_here, cols] = term
                else:
                    acc[tokens_here, cols] += term

        @pl.loop(0, D // TILE)
        def _(j):
            cols = pl.ds(pl.multiple_of(j * TILE, TILE), TILE)
            out = dot(act[...], w[buffer, cols, 2 * FF :], NT).astype(bfloat).astype(single)
            product = out * dy_rows[:, cols].astype(single)
            q_acc[...] += product[:, :LANES] + product[:, LANES:]
            tile = (out * gate[:, :1]).astype(bfloat)
            add_up(out_acc, tile, cols, first and e == 0)

        q_col = jnp.sum(q_acc[...], axis=1, keepdims=True)
        for b in range(blocks):
            here = slice(b * capacity, (b + 1) * capacity)
            q_ref[e : e + 1, b * MB_TOK : (b + 1) * MB_TOK] = jnp.sum(
                sel[here, :].astype(single) * q_col[here], axis=0, keepdims=True
            )
        for at, n in col_tiles(FF):
            grad_act = dot(grad_rows[...], w[buffer, :, 2 * FF + at : 2 * FF + at + n])
            grad_pre[:, at : at + n] = (grad_act * pre[:, at : at + n]).astype(bfloat)
            grad_pre[:, FF + at : FF + at + n] = (
                grad_act * pre[:, FF + at : FF + at + n]
            ).astype(bfloat)

        @pl.loop(0, D // TILE)
        def _(j):
            cols = pl.ds(pl.multiple_of(j * TILE, TILE), TILE)
            tile = dot(grad_pre[...], w[buffer, cols, : 2 * FF], NT).astype(bfloat)
            add_up(grad_acc, tile, cols, first and e == 0)

        for copy in waiting:
            copy.wait()

        @pl.loop(0, D // TILE)
        def _(j):
            cols = pl.ds(pl.multiple_of(j * TILE, TILE), TILE)
            turned[...] = rows[:, cols].T

            @pl.loop(0, 2 * FF // TILE)
            def _(k):
                out_cols = pl.ds(pl.multiple_of(k * TILE, TILE), TILE)
                stage[cols, out_cols] = dot(turned[...], grad_pre[:, out_cols]).astype(bfloat)

            turned[...] = grad_rows[:, cols].T
            for at, n in col_tiles(FF):
                stage[cols, 2 * FF + at : 2 * FF + at + n] = dot(
                    turned[...], act[:, at : at + n]
                ).astype(bfloat)

        keep, give = ((keep_left, give_left), (keep_right, give_right))[e]
        waiting = [
            pltpu.make_async_copy(
                stage.at[pl.ds(row_of(r), shard), :],
                (give if r & 1 else keep).at[r // 2, :, pl.ds(0, ECOLS)],
                sems.at[5],
            )
            for r in range(wide_count)
        ]
        for copy in waiting:
            copy.start()

    if width:
        for copy in shared_copies:
            copy.wait()

        @pl.loop(0, total // TILE)
        def _(i):
            here = pl.ds(pl.multiple_of(i * TILE, TILE), TILE)
            gate_pre = dot(norm[here, :], sw[:, :width])
            up_pre = dot(norm[here, :], sw[:, width : 2 * width])
            sigma = jax.nn.sigmoid(gate_pre)
            silu = gate_pre * sigma
            s_act[here, :] = (silu * up_pre).astype(bfloat)
            grad_act = dot(dy[here, :], sw[:, 2 * width :])
            s_pre[here, :width] = (
                grad_act * up_pre * sigma * (1.0 + gate_pre * (1.0 - sigma))
            ).astype(bfloat)
            s_pre[here, width:] = (grad_act * silu).astype(bfloat)
            for at, n in col_tiles(D):
                cols = slice(at, at + n)
                out_acc[here, cols] += dot(s_act[here, :], sw[cols, 2 * width :], NT)
                grad_acc[here, cols] += dot(s_pre[here, :], sw[cols, : 2 * width], NT)

        @pl.loop(0, D // TILE)
        def _(j):
            cols = pl.ds(pl.multiple_of(j * TILE, TILE), TILE)
            s_stage[cols, : 2 * width] = dot(norm[:, cols], s_pre[...], TN).astype(bfloat)
            s_stage[cols, 2 * width :] = dot(dy[:, cols], s_act[...], TN).astype(bfloat)

        for r in range(wide_count):
            for ref_pair, at, n in (
                ((keep_left, give_left), 0, width),
                ((keep_right, give_right), width, 2 * width),
            ):
                copy = pltpu.make_async_copy(
                    s_stage.at[pl.ds(row_of(r), shard), pl.ds(at, n)],
                    ref_pair[r & 1].at[r // 2, :, pl.ds(ECOLS, n)],
                    sems.at[6],
                )
                copy.start()
                waiting.append(copy)
    if first:
        finals = [
            pltpu.make_async_copy(src, dst, sems.at[7])
            for src, dst in zip((out_acc, grad_acc), sums_out)
        ]
        for copy in finals:
            copy.start()
    else:
        finals = []
        for acc, low, outs in (
            (out_acc, norm, sums_out[:narrow_count]),
            (grad_acc, dy, sums_out[narrow_count:]),
        ):
            finals.append(pltpu.make_async_copy(acc.at[pl.ds(0, part), :], outs[0], sems.at[7]))
            finals[-1].start()
            for s in range(1, narrow_count):

                @pl.loop(0, part // 32)
                def _(i):
                    here = pl.ds(pl.multiple_of(s * part + i * 32, 32), 32)
                    low[here, :] = acc[here, :].astype(bfloat)

                finals.append(
                    pltpu.make_async_copy(low.at[pl.ds(s * part, part), :], outs[s], sems.at[7])
                )
                finals[-1].start()
    for copy in waiting + finals:
        copy.wait()


def expert_pair(lefts, rights, norm_parts, dy_parts, rank_parts, gate_parts, sums, index, capacity, width):
    wide_count, narrow_count = len(lefts), len(norm_parts)
    shard = D // wide_count
    part = norm_parts[0].shape[0]
    total = part * narrow_count
    count_rows = total // MB_TOK * capacity
    first = sums is None
    buffers = 2 if narrow_count <= 4 else 1
    left_cols, right_cols = lefts[0].shape[1], rights[0].shape[1]
    grads = lambda cols: jax.ShapeDtypeStruct((wide_count // 2, shard, cols), bfloat)
    if first:
        sum_shapes = [jax.ShapeDtypeStruct((total, D), single)] * 2
    else:
        sum_shapes = (
            [jax.ShapeDtypeStruct((part, D), single)]
            + [jax.ShapeDtypeStruct((part, D), bfloat)] * (narrow_count - 1)
        ) * 2
    any_space = pl.BlockSpec(memory_space=pl.ANY)
    vmem = pl.BlockSpec(memory_space=pltpu.VMEM)
    operands = [*lefts, *rights, *norm_parts, *dy_parts, *rank_parts, *gate_parts]
    specs = [any_space] * (2 * wide_count + 2 * narrow_count) + [vmem] * (2 * narrow_count)
    if not first:
        operands += list(sums)
        specs += [any_space] * 2
    scratch = [
        pltpu.VMEM((buffers, D, ECOLS), bfloat),
        pltpu.VMEM((D, ECOLS), bfloat),
        pltpu.VMEM((total, D), bfloat),
        pltpu.VMEM((total, D), bfloat),
        pltpu.VMEM((total, D), single),
        pltpu.VMEM((total, D), single),
        pltpu.VMEM((count_rows, D), bfloat),
        pltpu.VMEM((count_rows, D), bfloat),
        pltpu.VMEM((count_rows, D), bfloat),
        pltpu.VMEM((count_rows, 2 * FF), single),
        pltpu.VMEM((count_rows, FF), bfloat),
        pltpu.VMEM((count_rows, 2 * FF), bfloat),
        pltpu.VMEM((count_rows, MB_TOK), bfloat),
        pltpu.VMEM((total, capacity), bfloat),
        pltpu.VMEM((count_rows, LANES), single),
        pltpu.VMEM((count_rows, LANES), single),
        pltpu.VMEM((TILE, count_rows), bfloat),
    ]
    if width:
        scratch += [
            pltpu.VMEM((D, 3 * width), bfloat),
            pltpu.VMEM((D, 3 * width), bfloat),
            pltpu.VMEM((total, width), bfloat),
            pltpu.VMEM((total, 2 * width), bfloat),
        ]
    scratch.append(pltpu.SemaphoreType.DMA((8,)))
    flops = 2 * 2 * count_rows * 9 * D * FF + 6 * 2 * total * D * width
    results = pl.pallas_call(
        functools.partial(
            expert_body, wide_count, narrow_count, capacity, width, first, buffers
        ),
        out_shape=[
            grads(left_cols),
            grads(left_cols),
            grads(right_cols),
            grads(right_cols),
            jax.ShapeDtypeStruct((2, total), single),
            *sum_shapes,
        ],
        in_specs=[pl.BlockSpec(memory_space=pltpu.SMEM)] + specs,
        out_specs=[any_space] * 4 + [vmem] + [any_space] * len(sum_shapes),
        scratch_shapes=scratch,
        compiler_params=pltpu.CompilerParams(vmem_limit_bytes=60 * 2**20),
        cost_estimate=pl.CostEstimate(
            flops=flops, bytes_accessed=4 * D * (left_cols + right_cols), transcendentals=0
        ),
    )(index, *operands)
    return results[:4], results[4], results[5:]


def ring_gather(piece):
    pieces = [piece]
    for _ in range(lax.axis_size("narrow") - 1):
        pieces.append(ring(pieces[-1]))
    return pieces


def ring_scatter(parts):
    count = lax.axis_size("narrow")
    total = parts[1].astype(bfloat)
    for step in range(2, count):
        total = (ring(total).astype(single) + parts[step].astype(single)).astype(bfloat)
    return parts[0], ring(total)


def pack_copies(w, lefts, rights, me, sem):
    shard = lefts[0].shape[0]
    cut = lefts[0].shape[1]
    copies = []
    for r, (left, right) in enumerate(zip(lefts, rights)):
        here = pl.ds(pl.multiple_of((me ^ r) * shard, 16), shard)
        copies.append(pltpu.make_async_copy(left, w.at[here, pl.ds(0, cut)], sem))
        copies.append(pltpu.make_async_copy(right, w.at[here, pl.ds(cut, ACOLS - cut)], sem))
    return copies


def turn(vectors, cosines, sines):
    return vectors * cosines + pltpu.roll(vectors, HEAD_DIM // 2, 1) * sines


def head_cols(part, head):
    return pl.ds(pl.multiple_of(part * D + head * HEAD_DIM, LANES), HEAD_DIM)


def row_probs(queries, keys_rot, bias):
    scores = dot(queries, keys_rot, NT) * HEAD_DIM ** (-0.5) + bias
    exp_scores = jnp.exp(scores - jnp.max(scores, axis=-1, keepdims=True))
    return exp_scores / jnp.sum(exp_scores, axis=-1, keepdims=True)


def attention_forward_body(wide_count, routed, idx, *refs):
    refs = list(refs)
    take = lambda count: [refs.pop(0) for _ in range(count)]
    lefts, rights = take(wide_count), take(wide_count)
    x, cosines, sines, bias, perm, slot_bias = take(6)
    hidden, second_norm, first_norm, qkv, attended, router_probs, gates, gain_rows = take(8)
    w, projected, sem = refs
    copies = pack_copies(w, lefts, rights, idx[0], sem)
    for copy in copies:
        copy.start()
    for copy in copies:
        copy.wait()
    tail = w[:, 4 * D :]
    gain_rows[...] = tail.astype(single).T[routed : routed + 2, :]
    rows_in = x[...].astype(single)
    first_norm[...] = (rows_in * rms_scale(rows_in) * gain_rows[0:1, :]).astype(bfloat)

    @pl.loop(0, 3 * D // TILE)
    def _(j):
        cols = pl.ds(pl.multiple_of(j * TILE, TILE), TILE)
        projected[:, cols] = dot(first_norm[...], w[:, cols])

    @pl.loop(0, HEADS)
    def _(head):
        for part in range(2):
            cols = head_cols(part, head)
            qkv[:, cols] = turn(projected[:, cols], cosines[...], sines[...]).astype(bfloat)
        cols = head_cols(2, head)
        qkv[:, cols] = projected[:, cols].astype(bfloat)
        for b in range(MB):
            here = slice(b * MB_TOK, (b + 1) * MB_TOK)
            probs = row_probs(
                qkv[here, head_cols(0, head)], qkv[here, head_cols(1, head)], bias[here, :]
            ).astype(bfloat)
            attended[here, head_cols(0, head)] = dot(probs, qkv[here, cols]).astype(bfloat)

    for at, n in col_tiles(D):
        hidden[:, at : at + n] = rows_in[:, at : at + n] + dot(
            attended[...], w[:, 3 * D + at : 3 * D + at + n]
        )
    rows_mid = hidden[...]
    second_norm[...] = (rows_mid * rms_scale(rows_mid) * gain_rows[1:2, :]).astype(bfloat)
    router_slots = dot(tail, perm[...]).astype(bfloat)
    logits = dot(second_norm[...], router_slots) + slot_bias[...]
    exp_logits = jnp.exp(logits - jnp.max(logits, axis=-1, keepdims=True))
    probs = exp_logits / jnp.sum(exp_logits, axis=-1, keepdims=True)
    router_probs[...] = probs
    gates[...] = probs.T[: gates.shape[0], :]


def attention_backward_body(wide_count, routed, slots, idx, *refs):
    refs = list(refs)
    take = lambda count: [refs.pop(0) for _ in range(count)]
    lefts, rights = take(wide_count), take(wide_count)
    x, cosines, sines, bias, perm = take(5)
    hidden, second_norm, first_norm, qkv, attended, router_probs, gain_rows = take(7)
    dy, second_own, second_come, q_rows = take(4)
    keep_left, give_left, keep_right, give_right, input_grad = take(5)
    w, stage, grad_second, grad_hidden, grad_branch, grad_attended, grad_projected, turned, tail_rows, sems = refs
    me = idx[0]
    copies = pack_copies(w, lefts, rights, me, sems.at[0])
    for copy in copies:
        copy.start()
    for copy in copies:
        copy.wait()
    probs = router_probs[...]
    pad = jnp.zeros((LANES - slots, q_rows.shape[1]), single)
    q = jnp.concatenate([q_rows[...], pad], axis=0).T
    grad_logits = probs * (q - jnp.sum(probs * q, axis=-1, keepdims=True))
    high = grad_logits.astype(bfloat)
    rest = (grad_logits - high.astype(single)).astype(bfloat)
    router_slots = dot(w[:, 4 * D :], perm[...]).astype(bfloat)
    for at, n in col_tiles(D):
        cols = slice(at, at + n)
        grad_second[:, cols] = (
            second_own[:, cols]
            + second_come[:, cols].astype(single)
            + dot(high, router_slots[cols, :], NT)
            + dot(rest, router_slots[cols, :], NT)
        )
    tail_rows[...] = jnp.zeros_like(tail_rows)
    rows_mid = hidden[...]
    scale = rms_scale(rows_mid)
    normed = rows_mid * scale
    weighted = grad_second[...] * gain_rows[1:2, :]
    tail_rows[1:2, :] = jnp.sum(grad_second[...] * normed, axis=0, keepdims=True)
    grad_hidden[...] = dy[...].astype(single) + scale * (
        weighted - normed * jnp.mean(weighted * normed, axis=-1, keepdims=True)
    )
    grad_branch[...] = grad_hidden[...].astype(bfloat)

    @pl.loop(0, D // TILE)
    def _(j):
        cols = pl.ds(pl.multiple_of(j * TILE, TILE), TILE)
        grad_attended[:, cols] = dot(grad_branch[...], w[cols, 3 * D : 4 * D], NT).astype(bfloat)
        turned[...] = attended[:, cols].T

        for at, n in col_tiles(D):
            stage[cols, 3 * D + at : 3 * D + at + n] = dot(
                turned[...], grad_branch[:, at : at + n]
            ).astype(bfloat)

    @pl.loop(0, HEADS)
    def _(head):
        for b in range(MB):
            here = slice(b * MB_TOK, (b + 1) * MB_TOK)
            queries = qkv[here, head_cols(0, head)]
            keys_rot = qkv[here, head_cols(1, head)]
            values = qkv[here, head_cols(2, head)]
            probs = row_probs(queries, keys_rot, bias[here, :])
            grad_out = grad_attended[here, head_cols(0, head)]
            grad_values = dot(probs.astype(bfloat), grad_out, TN)
            grad_probs = dot(grad_out, values, NT)
            grad_scores = probs * (
                grad_probs - jnp.sum(probs * grad_probs, axis=-1, keepdims=True)
            )
            grad_scores = grad_scores.astype(bfloat)
            grad_queries = dot(grad_scores, keys_rot) * HEAD_DIM ** (-0.5)
            grad_keys = dot(grad_scores, queries, TN) * HEAD_DIM ** (-0.5)
            for part, grad in enumerate((grad_queries, grad_keys)):
                grad_projected[here, head_cols(part, head)] = turn(
                    grad, cosines[here, :], -sines[here, :]
                ).astype(bfloat)
            grad_projected[here, head_cols(2, head)] = grad_values.astype(bfloat)

    @pl.loop(0, D // TILE)
    def _(j):
        cols = pl.ds(pl.multiple_of(j * TILE, TILE), TILE)
        grad_second[:, cols] = dot(grad_projected[...], w[cols, : 3 * D], NT)
        turned[...] = first_norm[:, cols].T

        @pl.loop(0, 3 * D // TILE)
        def _(k):
            out_cols = pl.ds(pl.multiple_of(k * TILE, TILE), TILE)
            stage[cols, out_cols] = dot(turned[...], grad_projected[:, out_cols]).astype(bfloat)

    rows_in = x[...].astype(single)
    scale = rms_scale(rows_in)
    normed = rows_in * scale
    weighted = grad_second[...] * gain_rows[0:1, :]
    tail_rows[0:1, :] = jnp.sum(grad_second[...] * normed, axis=0, keepdims=True)
    input_grad[...] = (
        grad_hidden[...]
        + scale * (weighted - normed * jnp.mean(weighted * normed, axis=-1, keepdims=True))
    ).astype(bfloat)
    high_expert = dot(high, perm[...], NT).astype(bfloat)
    rest_expert = dot(rest, perm[...], NT).astype(bfloat)
    lane = lax.broadcasted_iota(jnp.int32, (TILE, LANES), 1)
    for at, n in col_tiles(D):
        gain_cols = tail_rows[:, at : at + n].T
        router_cols = dot(second_norm[:, at : at + n], high_expert, TN) + dot(
            second_norm[:, at : at + n], rest_expert, TN
        )
        stage[at : at + n, 4 * D :] = (
            router_cols
            + jnp.where(lane == routed, gain_cols[:, 0:1], 0.0)
            + jnp.where(lane == routed + 1, gain_cols[:, 1:2], 0.0)
        ).astype(bfloat)
    shard = D // wide_count
    cut = split_cols(ACOLS)
    copies = []
    for r in range(wide_count):
        here = pl.ds(pl.multiple_of((me ^ r) * shard, 16), shard)
        for refs_out, at, n in (
            ((keep_left, give_left), 0, cut),
            ((keep_right, give_right), cut, ACOLS - cut),
        ):
            copies.append(
                pltpu.make_async_copy(
                    stage.at[here, pl.ds(at, n)], refs_out[r & 1].at[r // 2], sems.at[1]
                )
            )
    for copy in copies:
        copy.start()
    for copy in copies:
        copy.wait()


def attention_forward(lefts, rights, operands, index, routed, slots):
    wide_count = len(lefts)
    part = operands[0].shape[0]
    out = jax.ShapeDtypeStruct
    vmem = pl.BlockSpec(memory_space=pltpu.VMEM)
    any_space = pl.BlockSpec(memory_space=pl.ANY)
    return pl.pallas_call(
        functools.partial(attention_forward_body, wide_count, routed),
        out_shape=[
            out((part, D), single),
            out((part, D), bfloat),
            out((part, D), bfloat),
            out((part, 3 * D), bfloat),
            out((part, D), bfloat),
            out((part, LANES), single),
            out((slots, part), single),
            out((2, D), single),
        ],
        in_specs=[pl.BlockSpec(memory_space=pltpu.SMEM)]
        + [any_space] * (2 * wide_count)
        + [vmem] * len(operands),
        out_specs=[vmem] * 8,
        scratch_shapes=[
            pltpu.VMEM((D, ACOLS), bfloat),
            pltpu.VMEM((part, 3 * D), single),
            pltpu.SemaphoreType.DMA,
        ],
        compiler_params=pltpu.CompilerParams(vmem_limit_bytes=60 * 2**20),
        cost_estimate=pl.CostEstimate(
            flops=8 * part * D * D, bytes_accessed=2 * D * ACOLS, transcendentals=0
        ),
    )(index, *lefts, *rights, *operands)


def attention_backward(lefts, rights, operands, index, routed, slots):
    wide_count = len(lefts)
    part = operands[0].shape[0]
    out = jax.ShapeDtypeStruct
    vmem = pl.BlockSpec(memory_space=pltpu.VMEM)
    any_space = pl.BlockSpec(memory_space=pl.ANY)
    cut = split_cols(ACOLS)
    shard = D // wide_count
    grads = lambda cols: out((wide_count // 2, shard, cols), bfloat)
    return pl.pallas_call(
        functools.partial(attention_backward_body, wide_count, routed, slots),
        out_shape=[
            grads(cut),
            grads(cut),
            grads(ACOLS - cut),
            grads(ACOLS - cut),
            out((part, D), bfloat),
        ],
        in_specs=[pl.BlockSpec(memory_space=pltpu.SMEM)]
        + [any_space] * (2 * wide_count)
        + [vmem] * len(operands),
        out_specs=[any_space] * 4 + [vmem],
        scratch_shapes=[
            pltpu.VMEM((D, ACOLS), bfloat),
            pltpu.VMEM((D, ACOLS), bfloat),
            pltpu.VMEM((part, D), single),
            pltpu.VMEM((part, D), single),
            pltpu.VMEM((part, D), bfloat),
            pltpu.VMEM((part, D), bfloat),
            pltpu.VMEM((part, 3 * D), bfloat),
            pltpu.VMEM((TILE, part), bfloat),
            pltpu.VMEM((8, D), single),
            pltpu.SemaphoreType.DMA((2,)),
        ],
        compiler_params=pltpu.CompilerParams(vmem_limit_bytes=60 * 2**20),
        cost_estimate=pl.CostEstimate(
            flops=16 * part * D * D, bytes_accessed=6 * D * ACOLS, transcendentals=0
        ),
    )(index, *lefts, *rights, *operands)


def local(
    block_in,
    cotangent,
    routes,
    seq_ids,
    slot_order,
    attention_in,
    attention_in_moment,
    attention_in_average,
    attention_out,
    attention_out_moment,
    attention_out_average,
    shared_in,
    shared_in_moment,
    shared_in_average,
    shared_out,
    shared_out_moment,
    shared_out_average,
    router,
    router_moment,
    router_average,
    gains,
    gains_moment,
    gains_average,
    experts_in,
    experts_in_moment,
    experts_in_average,
    experts_out,
    experts_out_moment,
    experts_out_average,
):
    wide_count = lax.axis_size("wide")
    narrow_count = lax.axis_size("narrow")
    level = lax.axis_index("narrow")
    slots = EXP_DEV * narrow_count
    routed = slots - 1
    capacity = (MB_TOK * TOPK * 8 // (7 * slots) + 7) // 8 * 8
    tokens = MB * MB_TOK * wide_count * narrow_count
    own_tokens = MB * MB_TOK
    rows_dense = D // (wide_count * narrow_count)
    rows_plane = D // wide_count
    quarter = FF // narrow_count
    shared_width = (quarter + LANES - 1) // LANES * LANES

    pad_small = jnp.zeros((rows_dense, LANES - routed - 2), bfloat)
    attention_pack = jnp.concatenate(
        [
            attention_in.astype(bfloat),
            attention_out.astype(bfloat),
            router.astype(bfloat),
            gains.T.astype(bfloat),
            pad_small,
        ],
        axis=1,
    )
    shared_pack = jnp.concatenate([shared_in, shared_out.T], axis=1).astype(bfloat)
    shared_pack = shared_pack.reshape(rows_dense, 3, narrow_count, quarter)
    shared_pack = jnp.pad(shared_pack, ((0, 0), (0, 0), (0, 0), (0, shared_width - quarter)))
    shared_pack = shared_pack.transpose(2, 0, 1, 3).reshape(
        narrow_count, rows_dense, 3 * shared_width
    )
    shared_piece = lax.all_to_all(
        shared_pack, "narrow", split_axis=0, concat_axis=0, tiled=True
    ).reshape(rows_plane, 3 * shared_width)
    expert_pack = jnp.concatenate(
        [experts_in, experts_out.transpose(0, 2, 1)], axis=2
    ).astype(bfloat)
    expert_halves = [
        (expert_pack[0], expert_pack[1]),
        (
            jnp.concatenate([expert_pack[2], shared_piece[:, :shared_width]], axis=1),
            jnp.concatenate([expert_pack[3], shared_piece[:, shared_width:]], axis=1),
        ),
    ]

    route_hot = (routes[..., None] == jnp.arange(routed, dtype=jnp.int32)).astype(single).sum(axis=2)
    slot_hot_of_expert = (
        slot_order[:routed, None] == jnp.arange(slots, dtype=jnp.int32)
    ).astype(single)
    chosen = jnp.dot(route_hot.reshape(own_tokens, routed), slot_hot_of_expert)
    positions = jnp.arange(MB_TOK, dtype=jnp.int32)
    below = (positions[:, None] > positions[None, :]).astype(bfloat)
    ranks = jnp.einsum(
        "tu,bue->bte", below, chosen.reshape(MB, MB_TOK, slots).astype(bfloat), preferred_element_type=single
    ).reshape(own_tokens, slots)
    rank_parts = ring_gather(jnp.where(chosen > 0.5, ranks, -1.0).T)
    grad_out = cotangent.reshape(own_tokens, D)
    dy_parts = ring_gather(grad_out)

    attention_parts = ring_gather(attention_pack)
    attention_piece = place(attention_parts).reshape(rows_plane, ACOLS)
    cut = split_cols(ACOLS)
    attention_halves = gather_plane(attention_piece[:, :cut], attention_piece[:, cut:])
    expert_full = [gather_plane(*halves) for halves in expert_halves]

    wide_index = lax.axis_index("wide").reshape(1)
    perm = jnp.pad(
        slot_hot_of_expert, ((0, LANES - routed), (0, LANES - slots))
    ).astype(bfloat)
    slot_bias = jnp.where(jnp.sum(perm.astype(single), axis=0, keepdims=True) > 0.0, 0.0, MASKED)
    half_dim = HEAD_DIM // 2
    freqs = jnp.exp(jnp.arange(half_dim, dtype=single) * (-2.0 * math.log(10000.0) / HEAD_DIM))
    angles = (positions - seq_ids).reshape(own_tokens, 1).astype(single) * freqs
    cosines, sines = jnp.cos(angles), jnp.sin(angles)
    cosines = jnp.concatenate([cosines, cosines], axis=1)
    sines = jnp.concatenate([-sines, sines], axis=1)
    allowed = (seq_ids[:, :, None] == seq_ids[:, None, :]) & (
        positions[None, None, :] <= positions[None, :, None]
    )
    bias = jnp.where(allowed, 0.0, MASKED).reshape(own_tokens, MB_TOK)
    rows_in = block_in.reshape(own_tokens, D)
    tables = (cosines, sines, bias, perm)
    hidden, second_norm, first_norm, qkv, attended, router_probs, gates, gain_rows = attention_forward(
        *attention_halves, (rows_in, *tables, slot_bias), wide_index, routed, slots
    )

    norm_parts = ring_gather(second_norm)
    gate_parts = ring_gather(gates)
    sums = None
    expert_grads, q_rows = [], []
    for pair in range(2):
        index = jnp.stack([lax.axis_index("wide"), level * EXP_DEV + 2 * pair])
        grads, q_pair, sums = expert_pair(
            *expert_full[pair],
            norm_parts,
            dy_parts,
            rank_parts,
            gate_parts,
            sums,
            index,
            capacity,
            shared_width if pair else 0,
        )
        expert_grads.append(grads)
        q_rows.append(q_pair)
    out_parts, grad_parts = sums[:narrow_count], sums[narrow_count:]
    q_sent = jnp.concatenate(q_rows, axis=0).reshape(EXP_DEV, narrow_count, own_tokens)
    q_sent = place([q_sent[:, s] for s in range(narrow_count)])
    q_back = lax.all_to_all(q_sent, "narrow", split_axis=0, concat_axis=0, tiled=True)
    q_back = q_back.reshape(slots, own_tokens)
    second_own, second_come = ring_scatter(grad_parts)
    *attention_grads, input_grad = attention_backward(
        *attention_halves,
        (
            rows_in,
            *tables,
            hidden,
            second_norm,
            first_norm,
            qkv,
            attended,
            router_probs,
            gain_rows,
            grad_out,
            second_own,
            second_come,
            q_back,
        ),
        wide_index,
        routed,
        slots,
    )
    input_grad = input_grad.reshape(MB, MB_TOK, D)

    out_own, out_come = ring_scatter(out_parts)
    block_out = hidden + out_own + out_come.astype(single)
    block_out = block_out.astype(bfloat).reshape(MB, MB_TOK, D)

    shares = [scatter_plane(grads[:2], grads[2:]) for grads in expert_grads]
    attention_share = jnp.concatenate(
        scatter_plane(attention_grads[:2], attention_grads[2:]),
        axis=1,
    ).reshape(narrow_count, rows_dense, ACOLS)
    attention_own, attention_come = ring_scatter(
        [
            lax.dynamic_index_in_dim(attention_share, (level - s) % narrow_count, 0, False)
            for s in range(narrow_count)
        ]
    )
    attention_share = attention_own + attention_come.astype(single)
    shared_share = (
        jnp.concatenate([shares[1][0][:, ECOLS:], shares[1][1][:, ECOLS:]], axis=1)
        .astype(bfloat)
        .reshape(narrow_count, rows_dense, 3 * shared_width)
    )
    expert_shares = [half[:, :ECOLS] for pair in shares for half in pair]
    shared_share = lax.all_to_all(
        shared_share, "narrow", split_axis=0, concat_axis=0, tiled=True
    ).reshape(narrow_count, rows_dense, 3, shared_width)[..., :quarter]
    shared_share = shared_share.transpose(1, 2, 0, 3).reshape(rows_dense, 3 * FF).astype(single)

    summed = (
        attention_share[:, : 3 * D],
        attention_share[:, 3 * D : 4 * D],
        shared_share[:, : 2 * FF],
        shared_share[:, 2 * FF :].T,
        attention_share[:, 4 * D : 4 * D + routed],
        attention_share[:, 4 * D + routed : 4 * D + routed + 2].T,
        jnp.stack([share[:, : 2 * FF] for share in expert_shares]),
        jnp.stack([share[:, 2 * FF :].T for share in expert_shares]),
    )
    masters = (
        attention_in,
        attention_out,
        shared_in,
        shared_out,
        router,
        gains,
        experts_in,
        experts_out,
    )
    moments = (
        attention_in_moment,
        attention_out_moment,
        shared_in_moment,
        shared_out_moment,
        router_moment,
        gains_moment,
        experts_in_moment,
        experts_out_moment,
    )
    averages = (
        attention_in_average,
        attention_out_average,
        shared_in_average,
        shared_out_average,
        router_average,
        gains_average,
        experts_in_average,
        experts_out_average,
    )
    base_rate = 1.0 / math.sqrt(tokens)
    moment_outs = []
    states = []
    for master, moment, average, grad_share, step_rate in zip(
        masters, moments, averages, summed, STEP_RATES
    ):
        moment_new = MOMENTUM_DECAY * moment + grad_share
        master_new = master - step_rate * base_rate * (grad_share + MOMENTUM_DECAY * moment_new)
        average_new = AVERAGE_DECAY * average + (1.0 - AVERAGE_DECAY) * master_new
        moment_outs.append(moment_new)
        states.append(jnp.stack([average_new, master_new]))
    return (block_out, input_grad, *moment_outs, *states)


def solution(mesh):
    both = ("wide", "narrow")
    token = P(None, both, None)
    rows = P(both, None)
    cols = P(None, both)
    weight_specs = [rows, rows, rows, cols, rows, cols, P("narrow", "wide", None), P("narrow", None, "wide")]
    in_specs = (token, token, token, P(None, both), P()) + tuple(
        spec for spec in weight_specs for _ in range(3)
    )
    out_specs = (token, token, *weight_specs, *(P(None, *spec) for spec in weight_specs))
    return jax.shard_map(local, mesh=mesh, in_specs=in_specs, out_specs=out_specs, check_vma=False)
```

time: 1270 us -> 854 us (0.67)
  local copies, waits for them, and re-layouts: 506 us -> 58.4 us
  Pallas kernels: 0 us -> 214 us
  matrix products: 200 us -> 1.05 us
  waiting for transfers between devices: 335 us -> 406 us
  other arithmetic: 156 us -> 104 us
    dynamic_update_slice x30 -> x0, local copies, waits for them, and re-layouts: 282 us -> none  [the longest x15 144 us: assemble(): full = lax.dynamic_update_slice(full, left, ((me ^ r) * rows, 0))]
    pallas_call x0 -> x4, Pallas kernels: none -> 214 us  [the longest x2 139 us: expert_pair(): pl.pallas_call(functools.partial(expert_body, wide_count, narrow_count, c...]
    dot_general x67 -> x1, matrix products: 195 us -> 0.14 us  [local(): jnp.einsum('tu,bue->bte', below, chosen.reshape(MB, MB_TOK, slots).astype...]
    ppermute x18 -> x24, waiting for transfers between devices: 138 us -> 197 us  [ring(): lax.ppermute(piece, 'narrow', [(i, (i + 1) % count) for i in range(count)])]
    slice x20 -> x6, local copies, waits for them, and re-layouts: 37.7 us -> 2.47 us  [the longest x1 1.22 us: local(): attention_piece[:, :cut]]
    ppermute x14 -> x0, local copies, waits for them, and re-layouts: 32.6 us -> none  [wide_xor(): return lax.ppermute(piece, 'wide', [(i, i ^ bit) for i in range(count)])]
    unnamed x393 -> x203, local copies, waits for them, and re-layouts: 56.8 us -> 28.8 us
    broadcast_in_dim x7 -> x0, local copies, waits for them, and re-layouts: 19.6 us -> none  [the longest x2 15.5 us: assemble(): full = jnp.zeros((len(pieces) * rows, cut + pieces[0][1].shape[1]), bfloat)]
  transfers between devices with their start and end apart: 59 -> 87, of which waited for: 22 -> 33; matrix products, arithmetic and copies ran while one was open for 47% -> 14% of each run, Pallas kernels for 0% -> 17%
where the time goes in v2:
time: 854 us; the launch traced here: 844 us
  waiting for transfers between devices  406 us (48%)
  Pallas kernels  214 us (25%)
  other arithmetic  104 us (12%)
  starting transfers between devices  59.3 us (7%)
  local copies, waits for them, and re-layouts  58.4 us (7%)
    ppermute x60, waiting for transfers between devices, wide_xor(): return lax.ppermute(piece, 'wide', [(i, i ^ bit) for i in range(count)])  198 us
    ppermute x24, waiting for transfers between devices, ring(): lax.ppermute(piece, 'narrow', [(i, (i + 1) % count) for i in range(count)])  197 us
    pallas_call x2, Pallas kernels, expert_pair(): pl.pallas_call(functools.partial(expert_body, wide_count, narrow_count, c...  139 us
    pallas_call x1, Pallas kernels, attention_backward(): pl.pallas_call(functools.partial(attention_backward_body, wide_count, rou...  50.8 us
    another operation x24, other arithmetic, local(): states.append(jnp.stack([average_new, master_new]))  37.7 us
    ppermute x60, starting transfers between devices, wide_xor(): return lax.ppermute(piece, 'wide', [(i, i ^ bit) for i in range(count)])  34.7 us
    unnamed x203, local copies, waits for them, and re-layouts  28.8 us
    pallas_call x1, Pallas kernels, attention_forward(): pl.pallas_call(functools.partial(attention_forward_body, wide_count, rout...  23.5 us
  transfers between devices with their start and end apart: 87, of which 33 were waited for; matrix products, arithmetic and copies ran while one was open for 14% of the time, Pallas kernels for 17%

profile of v2, /device:TPU:0, one launch (start us, length us, event | category | flops | bytes accessed | tf_op | source)
XLA Modules:
  0.0 844.5 jit_solution(16944962429364616782)
XLA Ops:
  35.4 13.3 %collective-permute-done.38.refs_26_ = f32[16,256]{1,0:T(8,128)S(1)} collective-permute-done((f32[16,256]{1,0:T(8,128)S(1)}, f32[16,256]{1,0:T(8,128)S(1)}, u32[]{:S(2)}, u32[]{:S(2)}) %collective-permute-start.38) | collective-permute-done | bytes 16416 | tf_op jit(solution)/shard_map/ppermute | solution.py:56
  77.6 19.2 %collective-permute-done.2 = bf16[40,5248]{1,0:T(8,128)(2,1)S(1)} collective-permute-done((bf16[40,5248]{1,0:T(8,128)(2,1)S(1)}, bf16[40,5248]{1,0:T(8,128)(2,1)S(1)}, u32[]{:S(2)}, u32[]{:S(2)}) %collective-permute-start.2) | collective-permute-done | bytes 419872 | tf_op jit(solution)/shard_map/ppermute | solution.py:56
  100.1 17.7 %collective-permute-done.20.refs_4_ = bf16[160,2944]{1,0:T(8,128)(2,1)} collective-permute-done((bf16[160,2944]{1,0:T(8,128)(2,1)S(1)}, bf16[160,2944]{1,0:T(8,128)(2,1)}, u32[]{:S(2)}, u32[]{:S(2)}) %collective-permute-start.20) | collective-permute-done | bytes 942112 | tf_op jit(solution)/shard_map/ppermute | solution.py:51
  123.3 15.7 %collective-permute-done.13.refs_12_ = bf16[160,2560]{1,0:T(8,128)(2,1)S(1)} collective-permute-done((bf16[160,2560]{1,0:T(8,128)(2,1)S(1)}, bf16[160,2560]{1,0:T(8,128)(2,1)S(1)}, u32[]{:S(2)}, u32[]{:S(2)}) %collective-permute-start.13) | collective-permute-done | bytes 819232 | tf_op jit(solution)/shard_map/ppermute | solution.py:51
  141.0 17.3 %collective-permute-done.4.refs_2_ = bf16[160,2688]{1,0:T(8,128)(2,1)S(1)} collective-permute-done((bf16[160,2688]{1,0:T(8,128)(2,1)S(1)}, bf16[160,2688]{1,0:T(8,128)(2,1)S(1)}, u32[]{:S(2)}, u32[]{:S(2)}) %collective-permute-start.4) | collective-permute-done | bytes 860192 | tf_op jit(solution)/shard_map/ppermute | solution.py:51
  178.8 23.5 %shard_map.412 = (f32[256,1280]{1,0:T(8,128)}, bf16[256,1280]{1,0:T(8,128)(2,1)}, bf16[256,1280]{1,0:T(8,128)(2,1)}, bf16[256,3840]{1,0:T(8,128)(2,1)}, bf16[256...) custom-call(s32[1]{0:T(128)} %bitcast.idx, bf16[160,2688]{1,0:T(8,128)(2,1)} %copy-done.12, ...), custom_call_target="tpu_custom_call" | custom-call | flops 3355443200 | bytes 13434880 | tf_op jit(solution)/shard_map/pallas_call | solution.py:678
  205.8 16.1 %collective-permute-done.31.refs_17_ = bf16[256,1280]{1,0:T(8,128)(2,1)S(1)} collective-permute-done((bf16[256,1280]{1,0:T(8,128)(2,1)}, bf16[256,1280]{1,0:T(8,128)(2,1)S(1)}, u32[]{:S(2)}, u32[]{:S(2)}) %collective-permute-start.31) | collective-permute-done | bytes 655392 | tf_op jit(solution)/shard_map/ppermute | solution.py:56
  223.4 12.6 %collective-permute-done.36.refs_23_ = bf16[256,1280]{1,0:T(8,128)(2,1)S(1)} collective-permute-done((bf16[256,1280]{1,0:T(8,128)(2,1)}, bf16[256,1280]{1,0:T(8,128)(2,1)S(1)}, u32[]{:S(2)}, u32[]{:S(2)}) %collective-permute-start.36) | collective-permute-done | bytes 655392 | tf_op jit(solution)/shard_map/ppermute | solution.py:56
  236.5 12.7 %collective-permute-done.32.refs_18_ = bf16[256,1280]{1,0:T(8,128)(2,1)} collective-permute-done((bf16[256,1280]{1,0:T(8,128)(2,1)S(1)}, bf16[256,1280]{1,0:T(8,128)(2,1)}, u32[]{:S(2)}, u32[]{:S(2)}) %collective-permute-start.32) | collective-permute-done | bytes 655392 | tf_op jit(solution)/shard_map/ppermute | solution.py:56
  249.8 17.7 %collective-permute-done.40.refs_29_ = f32[16,256]{1,0:T(8,128)S(1)} collective-permute-done((f32[16,256]{1,0:T(8,128)}, f32[16,256]{1,0:T(8,128)S(1)}, u32[]{:S(2)}, u32[]{:S(2)}) %collective-permute-start.40) | collective-permute-done | bytes 16416 | tf_op jit(solution)/shard_map/ppermute | solution.py:56
  279.1 66.7 %shard_map.413 = (bf16[4,160,2688]{2,1,0:T(8,128)(2,1)}, bf16[4,160,2688]{2,1,0:T(8,128)(2,1)}, bf16[4,160,2688]{2,1,0:T(8,128)(2,1)}, bf16[4,160,2688]{2,1,0:T(...) custom-call(s32[2]{0:T(128)} %pad_add_fusion.1.idx, ...), custom_call_target="tpu_custom_call" | custom-call | flops 21139292160 | bytes 27525120 | tf_op jit(solution)/shard_map/pallas_call | solution.py:431
  345.9 72.6 %shard_map.414 = (bf16[4,160,2944]{2,1,0:T(8,128)(2,1)}, bf16[4,160,2944]{2,1,0:T(8,128)(2,1)}, bf16[4,160,3200]{2,1,0:T(8,128)(2,1)}, bf16[4,160,3200]{2,1,0:T(...) custom-call(s32[2]{0:T(128)} %pad_add_fusion.idx, ...), custom_call_target="tpu_custom_call" | custom-call | flops 25165824000 | bytes 31457280 | tf_op jit(solution)/shard_map/pallas_call | solution.py:431
  421.7 16.4 %collective-permute-done.60 = bf16[256,1280]{1,0:T(8,128)(2,1)S(1)} collective-permute-done((bf16[256,1280]{1,0:T(8,128)(2,1)}, bf16[256,1280]{1,0:T(8,128)(2,1)S(1)}, u32[]{:S(2)}, u32[]{:S(2)}) %collective-permute-start.60) | collective-permute-done | bytes 655392 | tf_op jit(solution)/shard_map/ppermute | solution.py:56
  439.5 12.7 %collective-permute-done.57 = bf16[256,1280]{1,0:T(8,128)(2,1)S(1)} collective-permute-done((bf16[256,1280]{1,0:T(8,128)(2,1)}, bf16[256,1280]{1,0:T(8,128)(2,1)S(1)}, u32[]{:S(2)}, u32[]{:S(2)}) %collective-permute-start.57) | collective-permute-done | bytes 655392 | tf_op jit(solution)/shard_map/ppermute | solution.py:56
  453.0 13.2 %collective-permute-done.61 = bf16[256,1280]{1,0:T(8,128)(2,1)S(1)} collective-permute-done((bf16[256,1280]{1,0:T(8,128)(2,1)S(1)}, bf16[256,1280]{1,0:T(8,128)(2,1)S(1)}, u32[]{:S(2)}, u32[]{:S(2)}) %collective-permute-start.61) | collective-permute-done | bytes 655392 | tf_op jit(solution)/shard_map/ppermute | solution.py:56
  467.2 13.0 %collective-permute-done.58 = bf16[256,1280]{1,0:T(8,128)(2,1)S(1)} collective-permute-done((bf16[256,1280]{1,0:T(8,128)(2,1)S(1)}, bf16[256,1280]{1,0:T(8,128)(2,1)S(1)}, u32[]{:S(2)}, u32[]{:S(2)}) %collective-permute-start.58) | collective-permute-done | bytes 655392 | tf_op jit(solution)/shard_map/ppermute | solution.py:56
  498.3 9.5 %all-to-all-done.1 = f32[4,4,256]{2,1,0:T(4,128)S(1)} async-done(((f32[4,4,256]{2,1,0:T(4,128)}), f32[4,4,256]{2,1,0:T(4,128)S(1)}, u32[]{:S(2)}, u32[]{:S(2)}) %all-to-all-start.1) | async-done | bytes 16416 | tf_op jit(solution)/shard_map/all_to_all | solution.py:885
  508.4 50.8 %shard_map.415 = (bf16[4,160,2688]{2,1,0:T(8,128)(2,1)}, bf16[4,160,2688]{2,1,0:T(8,128)(2,1)}, bf16[4,160,2560]{2,1,0:T(8,128)(2,1)}, bf16[4,160,2560]{2,1,0:T(8,128)(2,1)}, bf16[256,1280]{1,0:T(8,128)(2,1)}) custom-call(s32[1]{0:T(128)} %bitcast.idx, bf16[160,2688]{1,0:T(8,128)(2,1)} %copy-done.12, bf16[160,2688]{1,0:T(8,128)(2,1)} %copy-done.34, ...), custom_call_target="tpu_custom_call" | custom-call | flops 6710886400 | bytes 40304640 | tf_op jit(solution)/shard_map/pallas_call | solution.py:715
  576.2 29.2 %collective-permute-done.79 = bf16[2,160,2688]{2,1,0:T(8,128)(2,1)S(1)} collective-permute-done((bf16[2,160,2688]{2,1,0:T(8,128)(2,1)S(1)}, bf16[2,160,2688]{2,1,0:T(8,128)(2,1)S(1)}, u32[]{:S(2)}, u32[]{:S(2)}) %collective-permute-start.79) | collective-permute-done | bytes 1720352 | tf_op jit(solution)/shard_map/ppermute | solution.py:51
  620.1 25.7 %collective-permute-done.73 = bf16[2,160,2944]{2,1,0:T(8,128)(2,1)S(1)} collective-permute-done((bf16[2,160,2944]{2,1,0:T(8,128)(2,1)S(1)}, bf16[2,160,2944]{2,1,0:T(8,128)(2,1)S(1)}, u32[]{:S(2)}, u32[]{:S(2)}) %collective-permute-start.73) | collective-permute-done | bytes 1884192 | tf_op jit(solution)/shard_map/ppermute | solution.py:51
  648.0 25.0 %collective-permute-done.80 = bf16[1,160,2688]{2,1,0:T(8,128)(2,1)S(1)} collective-permute-done((bf16[1,160,2688]{2,1,0:T(8,128)(2,1)}, bf16[1,160,2688]{2,1,0:T(8,128)(2,1)S(1)}, u32[]{:S(2)}, u32[]{:S(2)}) %collective-permute-start.80) | collective-permute-done | bytes 860192 | tf_op jit(solution)/shard_map/ppermute | solution.py:51
  681.5 46.5 %collective-permute-done.74 = bf16[1,160,2944]{2,1,0:T(8,128)(2,1)} collective-permute-done((bf16[1,160,2944]{2,1,0:T(8,128)(2,1)S(1)}, bf16[1,160,2944]{2,1,0:T(8,128)(2,1)}, u32[]{:S(2)}, u32[]{:S(2)}) %collective-permute-start.74) | collective-permute-done | bytes 942112 | tf_op jit(solution)/shard_map/ppermute | solution.py:51
  779.2 10.5 %collective-permute-done.69 = bf16[40,5248]{1,0:T(8,128)(2,1)S(1)} collective-permute-done((bf16[40,5248]{1,0:T(8,128)(2,1)S(1)}, bf16[40,5248]{1,0:T(8,128)(2,1)S(1)}, u32[]{:S(2)}, u32[]{:S(2)}) %collective-permute-start.69) | collective-permute-done | bytes 419872 | tf_op jit(solution)/shard_map/ppermute | solution.py:56
  791.5 9.9 %collective-permute-done.70 = bf16[40,5248]{1,0:T(8,128)(2,1)S(1)} collective-permute-done((bf16[40,5248]{1,0:T(8,128)(2,1)S(1)}, bf16[40,5248]{1,0:T(8,128)(2,1)S(1)}, u32[]{:S(2)}, u32[]{:S(2)}) %collective-permute-start.70) | collective-permute-done | bytes 419872 | tf_op jit(solution)/shard_map/ppermute | solution.py:56
  (492 shorter events, 274.3 us)
Async XLA Ops:
  5.4 60.3 %collective-permute-start.44 = (bf16[160,2688]{1,0:T(8,128)(2,1)}, bf16[160,2688]{1,0:T(8,128)(2,1)}, u32[]{:S(2)}, u32[]{:S(2)}) collective-permute-start(bf16[160,2688]{1,0:T(8,128)(2,1)} %get-tuple-element.205.refs_0_), channel_id=1, source_target_pairs={{0,8},{4,12},{8,0},{12,4},{16,24},{20,28},{24,16},{28,20},{1,9},{5... | collective-permute-start | bytes 2580488 | tf_op jit(solution)/shard_map/ppermute | solution.py:51
  8.3 64.9 %collective-permute-start.46 = (bf16[160,2688]{1,0:T(8,128)(2,1)}, bf16[160,2688]{1,0:T(8,128)(2,1)}, u32[]{:S(2)}, u32[]{:S(2)}) collective-permute-start(bf16[160,2688]{1,0:T(8,128)(2,1)} %get-tuple-element.205.refs_0_), channel_id=1, source_target_pairs={{0,16},{4,20},{8,24},{12,28},{16,0},{20,4},{24,8},{28,12},{1,17},{... | collective-permute-start | bytes 2580488 | tf_op jit(solution)/shard_map/ppermute | solution.py:51
  74.7 45.1 %collective-permute-start.27 = (bf16[160,3200]{1,0:T(8,128)(2,1)S(1)}, bf16[160,3200]{1,0:T(8,128)(2,1)}, u32[]{:S(2)}, u32[]{:S(2)}) collective-permute-start(bf16[160,3200]{1,0:T(8,128)(2,1)S(1)} %pad_maximum_fusion.11.refs_8_), channel_id=1, source_target_pairs={{0,16},{4,20},{8,24},{12,28},{16,0},{20,4},{24,8},{28,12},{1,17},{... | collective-permute-start | bytes 3072008 | tf_op jit(solution)/shard_map/ppermute | solution.py:51
  222.7 50.8 %collective-permute-start.29 = (bf16[160,3200]{1,0:T(8,128)(2,1)}, bf16[160,3200]{1,0:T(8,128)(2,1)S(1)}, u32[]{:S(2)}, u32[]{:S(2)}) collective-permute-start(bf16[160,3200]{1,0:T(8,128)(2,1)} %collective-permute-done.27.refs_12_), channel_id=1, source_target_pairs={{0,8},{4,12},{8,0},{12,4},{16,24},{20,28},{24,16},{28,20},{1,9},{5... | collective-permute-start | bytes 3072008 | tf_op jit(solution)/shard_map/ppermute | solution.py:51
  273.6 72.2 %collective-permute-start.21 = (bf16[160,2944]{1,0:T(8,128)(2,1)}, bf16[160,2944]{1,0:T(8,128)(2,1)}, u32[]{:S(2)}, u32[]{:S(2)}) collective-permute-start(bf16[160,2944]{1,0:T(8,128)(2,1)} %collective-permute-done.20.refs_4_), channel_id=1, source_target_pairs={{0,4},{4,0},{8,12},{12,8},{16,20},{20,16},{24,28},{28,24},{1,5},{5... | collective-permute-start | bytes 2826248 | tf_op jit(solution)/shard_map/ppermute | solution.py:51
  273.6 72.2 %collective-permute-start.28 = (bf16[160,3200]{1,0:T(8,128)(2,1)}, bf16[160,3200]{1,0:T(8,128)(2,1)}, u32[]{:S(2)}, u32[]{:S(2)}) collective-permute-start(bf16[160,3200]{1,0:T(8,128)(2,1)} %collective-permute-done.27.refs_12_), channel_id=1, source_target_pairs={{0,4},{4,0},{8,12},{12,8},{16,20},{20,16},{24,28},{28,24},{1,5},{5... | collective-permute-start | bytes 3072008 | tf_op jit(solution)/shard_map/ppermute | solution.py:51
  274.1 71.7 %collective-permute-start.26 = (bf16[160,3200]{1,0:T(8,128)(2,1)}, bf16[160,3200]{1,0:T(8,128)(2,1)}, u32[]{:S(2)}, u32[]{:S(2)}) collective-permute-start(bf16[160,3200]{1,0:T(8,128)(2,1)} %copy-done.71), channel_id=1, source_target_pairs={{0,4},{4,0},{8,12},{12,8},{16,20},{20,16},{24,28},{28,24},{1,5},{5... | collective-permute-start | bytes 3072008 | tf_op jit(solution)/shard_map/ppermute | solution.py:51
  278.5 67.3 %collective-permute-start.23 = (bf16[160,2944]{1,0:T(8,128)(2,1)}, bf16[160,2944]{1,0:T(8,128)(2,1)}, u32[]{:S(2)}, u32[]{:S(2)}) collective-permute-start(bf16[160,2944]{1,0:T(8,128)(2,1)} %collective-permute-done.22.refs_6_), channel_id=1, source_target_pairs={{0,4},{4,0},{8,12},{12,8},{16,20},{20,16},{24,28},{28,24},{1,5},{5... | collective-permute-start | bytes 2826248 | tf_op jit(solution)/shard_map/ppermute | solution.py:51
  278.5 67.3 %collective-permute-start.30 = (bf16[160,3200]{1,0:T(8,128)(2,1)S(1)}, bf16[160,3200]{1,0:T(8,128)(2,1)}, u32[]{:S(2)}, u32[]{:S(2)}) collective-permute-start(bf16[160,3200]{1,0:T(8,128)(2,1)S(1)} %collective-permute-done.29.refs_14_), channel_id=1, source_target_pairs={{0,4},{4,0},{8,12},{12,8},{16,20},{20,16},{24,28},{28,24},{1,5},{5... | collective-permute-start | bytes 3072008 | tf_op jit(solution)/shard_map/ppermute | solution.py:51
  418.5 144.3 %collective-permute-start.78 = (bf16[4,160,2688]{2,1,0:T(8,128)(2,1)}, bf16[4,160,2688]{2,1,0:T(8,128)(2,1)}, u32[]{:S(2)}, u32[]{:S(2)}) collective-permute-start(bf16[4,160,2688]{2,1,0:T(8,128)(2,1)} %get-tuple-element.81), channel_id=1, source_target_pairs={{0,4},{4,0},{8,12},{12,8},{16,20},{20,16},{24,28},{28,24},{1,5},{5... | collective-permute-start | bytes 10321928 | tf_op jit(solution)/shard_map/ppermute | solution.py:51
  418.7 146.3 %collective-permute-start.81 = (bf16[4,160,2688]{2,1,0:T(8,128)(2,1)}, bf16[4,160,2688]{2,1,0:T(8,128)(2,1)}, u32[]{:S(2)}, u32[]{:S(2)}) collective-permute-start(bf16[4,160,2688]{2,1,0:T(8,128)(2,1)} %get-tuple-element.83), channel_id=1, source_target_pairs={{0,4},{4,0},{8,12},{12,8},{16,20},{20,16},{24,28},{28,24},{1,5},{5... | collective-permute-start | bytes 10321928 | tf_op jit(solution)/shard_map/ppermute | solution.py:51
  419.1 151.0 %collective-permute-start.72 = (bf16[4,160,2944]{2,1,0:T(8,128)(2,1)}, bf16[4,160,2944]{2,1,0:T(8,128)(2,1)}, u32[]{:S(2)}, u32[]{:S(2)}) collective-permute-start(bf16[4,160,2944]{2,1,0:T(8,128)(2,1)} %get-tuple-element.77), channel_id=1, source_target_pairs={{0,4},{4,0},{8,12},{12,8},{16,20},{20,16},{24,28},{28,24},{1,5},{5... | collective-permute-start | bytes 11304968 | tf_op jit(solution)/shard_map/ppermute | solution.py:51
  481.3 78.0 %collective-permute-start.59 = (bf16[256,1280]{1,0:T(8,128)(2,1)}, bf16[256,1280]{1,0:T(8,128)(2,1)}, u32[]{:S(2)}, u32[]{:S(2)}) collective-permute-start(bf16[256,1280]{1,0:T(8,128)(2,1)} %add_convert_fusion.21), channel_id=1, source_target_pairs={{0,1},{1,2},{2,3},{3,0},{4,5},{5,6},{6,7},{7,4},{8,9},{9,10},{10,1... | collective-permute-start | bytes 1966088 | tf_op jit(solution)/shard_map/ppermute | solution.py:56
  508.4 64.6 %collective-permute-start.75 = (bf16[4,160,3200]{2,1,0:T(8,128)(2,1)}, bf16[4,160,3200]{2,1,0:T(8,128)(2,1)}, u32[]{:S(2)}, u32[]{:S(2)}) collective-permute-start(bf16[4,160,3200]{2,1,0:T(8,128)(2,1)} %get-tuple-element.79), channel_id=1, source_target_pairs={{0,4},{4,0},{8,12},{12,8},{16,20},{20,16},{24,28},{28,24},{1,5},{5... | collective-permute-start | bytes 12288008 | tf_op jit(solution)/shard_map/ppermute | solution.py:51
  559.2 54.8 %collective-permute-start.66 = (bf16[4,160,2560]{2,1,0:T(8,128)(2,1)}, bf16[4,160,2560]{2,1,0:T(8,128)(2,1)S(1)}, u32[]{:S(2)}, u32[]{:S(2)}) collective-permute-start(bf16[4,160,2560]{2,1,0:T(8,128)(2,1)} %get-tuple-element.75), channel_id=1, source_target_pairs={{0,4},{4,0},{8,12},{12,8},{16,20},{20,16},{24,28},{28,24},{1,5},{5... | collective-permute-start | bytes 9830408 | tf_op jit(solution)/shard_map/ppermute | solution.py:51
  562.9 53.7 %collective-permute-start.63 = (bf16[4,160,2688]{2,1,0:T(8,128)(2,1)}, bf16[4,160,2688]{2,1,0:T(8,128)(2,1)S(1)}, u32[]{:S(2)}, u32[]{:S(2)}) collective-permute-start(bf16[4,160,2688]{2,1,0:T(8,128)(2,1)} %get-tuple-element.73), channel_id=1, source_target_pairs={{0,4},{4,0},{8,12},{12,8},{16,20},{20,16},{24,28},{28,24},{1,5},{5... | collective-permute-start | bytes 10321928 | tf_op jit(solution)/shard_map/ppermute | solution.py:51
  573.1 72.7 %collective-permute-start.73 = (bf16[2,160,2944]{2,1,0:T(8,128)(2,1)S(1)}, bf16[2,160,2944]{2,1,0:T(8,128)(2,1)S(1)}, u32[]{:S(2)}, u32[]{:S(2)}) collective-permute-start(bf16[2,160,2944]{2,1,0:T(8,128)(2,1)S(1)} %pad_maximum_fusion.5), channel_id=1, source_target_pairs={{0,16},{4,20},{8,24},{12,28},{16,0},{20,4},{24,8},{28,12},{1,17},{... | collective-permute-start | bytes 5652488 | tf_op jit(solution)/shard_map/ppermute | solution.py:51
  605.4 73.2 %collective-permute-start.76 = (bf16[2,160,3200]{2,1,0:T(8,128)(2,1)S(1)}, bf16[2,160,3200]{2,1,0:T(8,128)(2,1)}, u32[]{:S(2)}, u32[]{:S(2)}) collective-permute-start(bf16[2,160,3200]{2,1,0:T(8,128)(2,1)S(1)} %pad_maximum_fusion.4), channel_id=1, source_target_pairs={{0,8},{4,12},{8,0},{12,4},{16,24},{20,28},{24,16},{28,20},{1,9},{5... | collective-permute-start | bytes 6144008 | tf_op jit(solution)/shard_map/ppermute | solution.py:51
  610.8 62.2 %collective-permute-start.80 = (bf16[1,160,2688]{2,1,0:T(8,128)(2,1)}, bf16[1,160,2688]{2,1,0:T(8,128)(2,1)S(1)}, u32[]{:S(2)}, u32[]{:S(2)}) collective-permute-start(bf16[1,160,2688]{2,1,0:T(8,128)(2,1)} %add_convert_fusion.9), channel_id=1, source_target_pairs={{0,8},{4,12},{8,0},{12,4},{16,24},{20,28},{24,16},{28,20},{1,9},{5... | collective-permute-start | bytes 2580488 | tf_op jit(solution)/shard_map/ppermute | solution.py:51
  614.1 62.4 %collective-permute-start.83 = (bf16[1,160,2688]{2,1,0:T(8,128)(2,1)}, bf16[1,160,2688]{2,1,0:T(8,128)(2,1)S(1)}, u32[]{:S(2)}, u32[]{:S(2)}) collective-permute-start(bf16[1,160,2688]{2,1,0:T(8,128)(2,1)} %add_convert_fusion.6), channel_id=1, source_target_pairs={{0,16},{4,20},{8,24},{12,28},{16,0},{20,4},{24,8},{28,12},{1,17},{... | collective-permute-start | bytes 2580488 | tf_op jit(solution)/shard_map/ppermute | solution.py:51
  616.6 113.6 %collective-permute-start.67 = (bf16[2,160,2560]{2,1,0:T(8,128)(2,1)}, bf16[2,160,2560]{2,1,0:T(8,128)(2,1)}, u32[]{:S(2)}, u32[]{:S(2)}) collective-permute-start(bf16[2,160,2560]{2,1,0:T(8,128)(2,1)} %pad_maximum_fusion.9), channel_id=1, source_target_pairs={{0,8},{4,12},{8,0},{12,4},{16,24},{20,28},{24,16},{28,20},{1,9},{5... | collective-permute-start | bytes 4915208 | tf_op jit(solution)/shard_map/ppermute | solution.py:51
  645.8 87.3 %collective-permute-start.64 = (bf16[2,160,2688]{2,1,0:T(8,128)(2,1)}, bf16[2,160,2688]{2,1,0:T(8,128)(2,1)}, u32[]{:S(2)}, u32[]{:S(2)}) collective-permute-start(bf16[2,160,2688]{2,1,0:T(8,128)(2,1)} %pad_maximum_fusion.6), channel_id=1, source_target_pairs={{0,16},{4,20},{8,24},{12,28},{16,0},{20,4},{24,8},{28,12},{1,17},{... | collective-permute-start | bytes 5160968 | tf_op jit(solution)/shard_map/ppermute | solution.py:51
  673.9 54.1 %collective-permute-start.74 = (bf16[1,160,2944]{2,1,0:T(8,128)(2,1)S(1)}, bf16[1,160,2944]{2,1,0:T(8,128)(2,1)}, u32[]{:S(2)}, u32[]{:S(2)}) collective-permute-start(bf16[1,160,2944]{2,1,0:T(8,128)(2,1)S(1)} %add_convert_fusion.3), channel_id=1, source_target_pairs={{0,8},{4,12},{8,0},{12,4},{16,24},{20,28},{24,16},{28,20},{1,9},{5... | collective-permute-start | bytes 2826248 | tf_op jit(solution)/shard_map/ppermute | solution.py:51
  680.6 55.8 %collective-permute-start.77 = (bf16[1,160,3200]{2,1,0:T(8,128)(2,1)S(1)}, bf16[1,160,3200]{2,1,0:T(8,128)(2,1)}, u32[]{:S(2)}, u32[]{:S(2)}) collective-permute-start(bf16[1,160,3200]{2,1,0:T(8,128)(2,1)S(1)} %add_convert_fusion), channel_id=1, source_target_pairs={{0,16},{4,20},{8,24},{12,28},{16,0},{20,4},{24,8},{28,12},{1,17},{... | collective-permute-start | bytes 3072008 | tf_op jit(solution)/shard_map/ppermute | solution.py:51
  (159 other events, 3281.6 us)

commit v3 on v2

--- a/solution.py
+++ b/solution.py
@@ -64,15 +64,30 @@
     return bits
 
 
-def gather_plane(left, right):
-    halves = []
-    for part, order in ((left, chip_bits()), (right, chip_bits()[::-1])):
-        pieces = {0: part}
-        for bit in order:
-            pieces.update({r | bit: wide_xor(p, bit) for r, p in list(pieces.items())})
-        pieces.update({r | 1: wide_xor(p, 1) for r, p in list(pieces.items())})
-        halves.append([pieces[r] for r in range(lax.axis_size("wide"))])
-    return halves
+def after(value, *others):
+    return lax.optimization_barrier((value, *others))[0]
+
+
+def first_hops(pieces, bit):
+    return {r | bit: wide_xor(p, bit) for r, p in pieces.items()}
+
+
+def core_hops(pieces, pairs=False):
+    full = {r: (p, wide_xor(p, 1)) for r, p in pieces.items()}
+    return full if pairs else [p for r in sorted(full) for p in full[r]]
+
+
+def gather_chips(piece, order, held=None, wait=()):
+    pieces = {0: piece}
+    for number, bit in enumerate(order):
+        if number == 0 and held is not None:
+            pieces.update(held)
+            continue
+        source = dict(pieces)
+        if wait:
+            source = {r: after(p, *wait) for r, p in source.items()}
+        pieces.update(first_hops(source, bit))
+    return pieces
 
 
 def place(pieces):
@@ -84,58 +99,75 @@
     return full
 
 
-def scatter_half(keep, give, order):
+def scatter_core(keep, give):
     arrived = wide_xor(give, 1)
-    terms = {i: [keep[i], arrived[i]] for i in range(keep.shape[0])}
-    for bit in order:
-        sent = [i for i in terms if i & (bit >> 1)]
-        kept = [i for i in terms if not i & (bit >> 1)]
-        outgoing = jnp.stack([sum(t.astype(single) for t in terms[i]).astype(bfloat) for i in sent])
-        incoming = wide_xor(outgoing, bit)
-        terms = {
-            i: [*terms[i], incoming[sent.index(i | (bit >> 1))]]
-            for i in kept
-        }
-    return sum(t.astype(single) for t in terms[0])
-
-
-def scatter_plane(left, right):
-    order = chip_bits()
-    return (
-        scatter_half(*left, order[::-1]),
-        scatter_half(*right, order),
-    )
+    return {i: [(keep, i), (arrived, i)] for i in range(keep.shape[0])}
+
+
+def block_of(term):
+    array, i = term
+    return array[i].astype(single)
+
+
+def blocks_of(places):
+    array, numbers = places[0][0], [i for _, i in places]
+    step = numbers[1] - numbers[0] if len(numbers) > 1 else 1
+    if numbers == list(range(numbers[0], numbers[-1] + 1, step)):
+        return array[numbers[0] : numbers[-1] + 1 : step].astype(single)
+    return jnp.stack([array[i] for i in numbers]).astype(single)
+
+
+def scatter_hop(terms, bit):
+    low = bit >> 1
+    sent = [i for i in terms if i & low]
+    outgoing = sum(blocks_of([t[n] for t in (terms[i] for i in sent)]) for n in range(len(terms[sent[0]])))
+    outgoing = outgoing.astype(bfloat)
+    incoming = wide_xor(outgoing, bit)
+    kept = {i: [*terms[i], (incoming, sent.index(i | low))] for i in terms if not i & low}
+    return kept, outgoing
 
 
 TILE = 256
+
+
+def lasting(micros):
+    return pl.CostEstimate(flops=int(micros * 1.1e9), bytes_accessed=1000, transcendentals=0)
 
 
 def col_tiles(width):
     return [(at, min(TILE, width - at)) for at in range(0, width, TILE)]
 
 
-def expert_body(
-    wide_count, narrow_count, capacity, width, first, buffers, idx, *refs
-):
+def expert_body(wide_count, narrow_count, capacity, width, column, first, last, idx, *refs):
     refs = list(refs)
     take = lambda count: [refs.pop(0) for _ in range(count)]
-    lefts, rights = take(wide_count), take(wide_count)
-    norm_parts, dy_parts = take(narrow_count), take(narrow_count)
-    rank_parts, gate_parts = take(narrow_count), take(narrow_count)
+    pieces = take(wide_count)
+    shared_weights = take(1) if width else []
+    norm_parts, (dy_all,) = take(narrow_count), take(1)
+    if first:
+        router_slots, slot_bias = take(2)
+    else:
+        gates, ranks = take(2)
+    earlier_q = take(EXP_DEV - 1) if last else []
     sums_in = [] if first else take(2)
-    keep_left, give_left, keep_right, give_right, q_ref = take(5)
-    sums_out = take(2) if first else take(2 * narrow_count)
+    keep, give, q_ref = take(3)
+    if first:
+        gates, ranks = take(2)
+    sums_out = take(1 + narrow_count) if last else take(2)
     (w, stage, norm, dy, out_acc, grad_acc, rows, dy_rows, grad_rows, pre, act, grad_pre, sel, sel_t, gate, q_acc, turned) = take(17)
     if width:
         sw, s_stage, s_act, s_pre = take(4)
+    if first:
+        (rank_cols,) = take(1)
+    if last:
+        q_cols, q_low = take(2)
     sems = refs.pop(0)
     assert not refs
-    me, slot = idx[0], idx[1]
+    me, slot, level = idx[0], idx[1], idx[2]
     part = norm_parts[0].shape[0]
     total = part * narrow_count
     shard = D // wide_count
     blocks = total // MB_TOK
-    per_part = part // MB_TOK
 
     def row_of(r):
         return pl.multiple_of((me ^ r) * shard, 16)
@@ -145,63 +177,46 @@
         mine = lax.broadcasted_iota(jnp.int32, tile.shape, 0) == number
         return jnp.sum(jnp.where(mine, tile, 0.0), axis=0, keepdims=True)
 
-    def weight_copies(halves, buffer, sem):
-        return [
-            pltpu.make_async_copy(
-                halves[r].at[:, pl.ds(0, ECOLS)],
-                w.at[buffer, pl.ds(row_of(r), shard), :],
-                sems.at[sem],
-            )
-            for r in range(wide_count)
-        ]
-
-    token_copies = [
-        pltpu.make_async_copy(src, dst.at[pl.ds(s * part, part), :], sems.at[2])
-        for parts, dst in ((norm_parts, norm), (dy_parts, dy))
-        for s, src in enumerate(parts)
+    expert_copies = [
+        pltpu.make_async_copy(
+            pieces[r].at[:, pl.ds(column, ECOLS)], w.at[pl.ds(row_of(r), shard), :], sems.at[0]
+        )
+        for r in range(wide_count)
     ]
+    shared_copies = [pltpu.make_async_copy(ref, sw, sems.at[4]) for ref in shared_weights]
+
+    def from_below(s):
+        return lax.rem(level + (narrow_count - s), narrow_count)
+
+    token_copies = []
+    for s, src in enumerate(norm_parts):
+        here = pl.ds(s * part, part)
+        theirs = dy_all.at[from_below(s)]
+        moves = [(src, norm.at[here, :]), (theirs.at[:, pl.ds(0, D)], dy.at[here, :])]
+        if first:
+            moves.append((theirs.at[:, pl.ds(D, LANES)], rank_cols.at[here, :]))
+        token_copies += [pltpu.make_async_copy(*move, sems.at[2]) for move in moves]
     sum_copies = [
         pltpu.make_async_copy(src, dst, sems.at[3])
         for src, dst in zip(sums_in, (out_acc, grad_acc))
     ]
-    shared_copies = []
-    if width:
-        for r in range(wide_count):
-            shared_copies.append(
-                pltpu.make_async_copy(
-                    lefts[r].at[:, pl.ds(ECOLS, width)],
-                    sw.at[pl.ds(row_of(r), shard), pl.ds(0, width)],
-                    sems.at[4],
-                )
-            )
-            shared_copies.append(
-                pltpu.make_async_copy(
-                    rights[r].at[:, pl.ds(ECOLS, 2 * width)],
-                    sw.at[pl.ds(row_of(r), shard), pl.ds(width, 2 * width)],
-                    sems.at[4],
-                )
-            )
-    expert_copies = [weight_copies(lefts, 0, 0), weight_copies(rights, buffers - 1, 1)]
-    for copy in token_copies + expert_copies[0] + sum_copies:
-        copy.start()
-    if buffers == 2:
-        for copy in expert_copies[1]:
-            copy.start()
-    for copy in shared_copies:
+    for copy in token_copies + expert_copies + sum_copies + shared_copies:
         copy.start()
     for copy in token_copies:
         copy.wait()
 
-    waiting = []
-    for e in range(2):
-        buffer = e if buffers == 2 else 0
-        if e == 1 and buffers == 1:
-            for copy in expert_copies[1]:
-                copy.start()
+    if first:
+        for at in range(0, total, TILE):
+            logits = dot(norm[at : at + TILE, :], router_slots[...]) + slot_bias[...]
+            exp_logits = jnp.exp(logits - jnp.max(logits, axis=-1, keepdims=True))
+            probs = exp_logits / jnp.sum(exp_logits, axis=-1, keepdims=True)
+            gates[:, at : at + TILE] = probs.T[: gates.shape[0], :]
+            numbers = rank_cols[at : at + TILE, :].astype(single)
+            ranks[:, at : at + TILE] = numbers.T[: gates.shape[0], :]
+    if True:
         for b in range(blocks):
-            s, at = b // per_part, (b % per_part) * MB_TOK
-            rank_row = slot_row(rank_parts[s], slot + e, at)
-            gate_row = slot_row(gate_parts[s], slot + e, at)
+            rank_row = slot_row(ranks, slot, b * MB_TOK)
+            gate_row = slot_row(gates, slot, b * MB_TOK)
             place_in = lax.broadcasted_iota(jnp.int32, (capacity, MB_TOK), 0).astype(single)
             hit = jnp.where(place_in == rank_row, 1.0, 0.0)
             here = pl.ds(b * capacity, capacity)
@@ -215,13 +230,13 @@
             picked = dot(hit_low, dy[tokens_here, :])
             dy_rows[here, :] = picked.astype(bfloat)
             grad_rows[here, :] = (gate_col * picked).astype(bfloat)
-        for copy in expert_copies[e]:
+        for copy in expert_copies:
             copy.wait()
 
         @pl.loop(0, 2 * FF // TILE)
         def _(j):
             cols = pl.ds(pl.multiple_of(j * TILE, TILE), TILE)
-            pre[:, cols] = dot(rows[...], w[buffer, :, cols])
+            pre[:, cols] = dot(rows[...], w[:, cols])
 
         @pl.loop(0, rows.shape[0] // 32)
         def _(i):
@@ -233,9 +248,8 @@
             pre[here, :FF] = up_pre * sigma * (1.0 + gate_pre * (1.0 - sigma))
             pre[here, FF:] = silu
 
-        if e == 0:
-            for copy in sum_copies:
-                copy.wait()
+        for copy in sum_copies:
+            copy.wait()
         q_acc[...] = jnp.zeros_like(q_acc)
 
         def add_up(acc, tile, cols, fresh):
@@ -250,20 +264,20 @@
         @pl.loop(0, D // TILE)
         def _(j):
             cols = pl.ds(pl.multiple_of(j * TILE, TILE), TILE)
-            out = dot(act[...], w[buffer, cols, 2 * FF :], NT).astype(bfloat).astype(single)
+            out = dot(act[...], w[cols, 2 * FF :], NT).astype(bfloat).astype(single)
             product = out * dy_rows[:, cols].astype(single)
             q_acc[...] += product[:, :LANES] + product[:, LANES:]
             tile = (out * gate[:, :1]).astype(bfloat)
-            add_up(out_acc, tile, cols, first and e == 0)
+            add_up(out_acc, tile, cols, first)
 
         q_col = jnp.sum(q_acc[...], axis=1, keepdims=True)
         for b in range(blocks):
             here = slice(b * capacity, (b + 1) * capacity)
-            q_ref[e : e + 1, b * MB_TOK : (b + 1) * MB_TOK] = jnp.sum(
+            q_ref[0:1, b * MB_TOK : (b + 1) * MB_TOK] = jnp.sum(
                 sel[here, :].astype(single) * q_col[here], axis=0, keepdims=True
             )
         for at, n in col_tiles(FF):
-            grad_act = dot(grad_rows[...], w[buffer, :, 2 * FF + at : 2 * FF + at + n])
+            grad_act = dot(grad_rows[...], w[:, 2 * FF + at : 2 * FF + at + n])
             grad_pre[:, at : at + n] = (grad_act * pre[:, at : at + n]).astype(bfloat)
             grad_pre[:, FF + at : FF + at + n] = (
                 grad_act * pre[:, FF + at : FF + at + n]
@@ -272,39 +286,8 @@
         @pl.loop(0, D // TILE)
         def _(j):
             cols = pl.ds(pl.multiple_of(j * TILE, TILE), TILE)
-            tile = dot(grad_pre[...], w[buffer, cols, : 2 * FF], NT).astype(bfloat)
-            add_up(grad_acc, tile, cols, first and e == 0)
-
-        for copy in waiting:
-            copy.wait()
-
-        @pl.loop(0, D // TILE)
-        def _(j):
-            cols = pl.ds(pl.multiple_of(j * TILE, TILE), TILE)
-            turned[...] = rows[:, cols].T
-
-            @pl.loop(0, 2 * FF // TILE)
-            def _(k):
-                out_cols = pl.ds(pl.multiple_of(k * TILE, TILE), TILE)
-                stage[cols, out_cols] = dot(turned[...], grad_pre[:, out_cols]).astype(bfloat)
-
-            turned[...] = grad_rows[:, cols].T
-            for at, n in col_tiles(FF):
-                stage[cols, 2 * FF + at : 2 * FF + at + n] = dot(
-                    turned[...], act[:, at : at + n]
-                ).astype(bfloat)
-
-        keep, give = ((keep_left, give_left), (keep_right, give_right))[e]
-        waiting = [
-            pltpu.make_async_copy(
-                stage.at[pl.ds(row_of(r), shard), :],
-                (give if r & 1 else keep).at[r // 2, :, pl.ds(0, ECOLS)],
-                sems.at[5],
-            )
-            for r in range(wide_count)
-        ]
-        for copy in waiting:
-            copy.start()
+            tile = dot(grad_pre[...], w[cols, : 2 * FF], NT).astype(bfloat)
+            add_up(grad_acc, tile, cols, first)
 
     if width:
         for copy in shared_copies:
@@ -334,74 +317,127 @@
             s_stage[cols, : 2 * width] = dot(norm[:, cols], s_pre[...], TN).astype(bfloat)
             s_stage[cols, 2 * width :] = dot(dy[:, cols], s_act[...], TN).astype(bfloat)
 
+    waiting = []
+    if last:
+        slots = EXP_DEV * narrow_count
+        number = lax.broadcasted_iota(jnp.int32, (LANES, MB_TOK), 0)
+        for b in range(blocks):
+            tokens_here = slice(b * MB_TOK, (b + 1) * MB_TOK)
+            table = jnp.zeros((LANES, MB_TOK), single)
+            for e, ref in enumerate([*earlier_q, q_ref]):
+                row = ref[0:1, tokens_here]
+                high = row.astype(bfloat).astype(single)
+                mine = slot - (EXP_DEV - 1) + e
+                table = jnp.where(number == mine, high, table)
+                table = jnp.where(number == slots + mine, row - high, table)
+            q_cols[tokens_here, :] = table.T
+        q_low[...] = q_cols[...].astype(bfloat)
+        for s in range(narrow_count):
+            here = pl.ds(s * part, part)
+            waiting.append(
+                pltpu.make_async_copy(
+                    (q_low if s else q_cols).at[here, :],
+                    sums_out[1 + s].at[:, pl.ds(D, LANES)],
+                    sems.at[3],
+                )
+            )
+            waiting[-1].start()
+    if not last:
+        for src, dst in zip((out_acc, grad_acc), sums_out):
+            waiting.append(pltpu.make_async_copy(src, dst, sems.at[7]))
+            waiting[-1].start()
+    else:
+        for acc, low in ((grad_acc, dy), (out_acc, norm)):
+            for s in range(narrow_count):
+                here = pl.ds(s * part, part)
+                if acc is grad_acc:
+                    target = sums_out[1 + s].at[:, pl.ds(0, D)]
+                else:
+                    target = sums_out[0].at[from_below(s)]
+                source = low
+                if s == 0 and acc is grad_acc:
+                    source = acc
+                else:
+
+                    @pl.loop(0, part // 32)
+                    def _(i):
+                        some = pl.ds(pl.multiple_of(s * part + i * 32, 32), 32)
+                        low[some, :] = acc[some, :].astype(bfloat)
+
+                waiting.append(pltpu.make_async_copy(source.at[here, :], target, sems.at[7]))
+                waiting[-1].start()
+    if width:
         for r in range(wide_count):
-            for ref_pair, at, n in (
-                ((keep_left, give_left), 0, width),
-                ((keep_right, give_right), width, 2 * width),
-            ):
-                copy = pltpu.make_async_copy(
-                    s_stage.at[pl.ds(row_of(r), shard), pl.ds(at, n)],
-                    ref_pair[r & 1].at[r // 2, :, pl.ds(ECOLS, n)],
+            waiting.append(
+                pltpu.make_async_copy(
+                    s_stage.at[pl.ds(row_of(r), shard), :],
+                    (give if r & 1 else keep).at[r // 2, :, pl.ds(ECOLS, 3 * width)],
                     sems.at[6],
                 )
-                copy.start()
-                waiting.append(copy)
-    if first:
-        finals = [
-            pltpu.make_async_copy(src, dst, sems.at[7])
-            for src, dst in zip((out_acc, grad_acc), sums_out)
-        ]
-        for copy in finals:
-            copy.start()
-    else:
-        finals = []
-        for acc, low, outs in (
-            (out_acc, norm, sums_out[:narrow_count]),
-            (grad_acc, dy, sums_out[narrow_count:]),
-        ):
-            finals.append(pltpu.make_async_copy(acc.at[pl.ds(0, part), :], outs[0], sems.at[7]))
-            finals[-1].start()
-            for s in range(1, narrow_count):
-
-                @pl.loop(0, part // 32)
-                def _(i):
-                    here = pl.ds(pl.multiple_of(s * part + i * 32, 32), 32)
-                    low[here, :] = acc[here, :].astype(bfloat)
-
-                finals.append(
-                    pltpu.make_async_copy(low.at[pl.ds(s * part, part), :], outs[s], sems.at[7])
-                )
-                finals[-1].start()
-    for copy in waiting + finals:
+            )
+            waiting[-1].start()
+    if True:
+
+        @pl.loop(0, D // TILE)
+        def _(j):
+            cols = pl.ds(pl.multiple_of(j * TILE, TILE), TILE)
+            turned[...] = rows[:, cols].T
+
+            @pl.loop(0, 2 * FF // TILE)
+            def _(k):
+                out_cols = pl.ds(pl.multiple_of(k * TILE, TILE), TILE)
+                stage[cols, out_cols] = dot(turned[...], grad_pre[:, out_cols]).astype(bfloat)
+
+            turned[...] = grad_rows[:, cols].T
+            for at, n in col_tiles(FF):
+                stage[cols, 2 * FF + at : 2 * FF + at + n] = dot(
+                    turned[...], act[:, at : at + n]
+                ).astype(bfloat)
+
+    for r in range(wide_count):
+        waiting.append(
+            pltpu.make_async_copy(
+                stage.at[pl.ds(row_of(r), shard), :],
+                (give if r & 1 else keep).at[r // 2, :, pl.ds(0, ECOLS)],
+                sems.at[5],
+            )
+        )
+        waiting[-1].start()
+    for copy in waiting:
         copy.wait()
 
 
-def expert_pair(lefts, rights, norm_parts, dy_parts, rank_parts, gate_parts, sums, index, capacity, width):
-    wide_count, narrow_count = len(lefts), len(norm_parts)
+def expert_call(pieces, column, shared_weights, tokens, gating, earlier_q, sums, index, capacity, last):
+    wide_count = len(pieces)
+    norm_parts, dy_all = tokens
+    narrow_count = len(norm_parts)
     shard = D // wide_count
     part = norm_parts[0].shape[0]
+    slots = EXP_DEV * narrow_count
     total = part * narrow_count
     count_rows = total // MB_TOK * capacity
     first = sums is None
-    buffers = 2 if narrow_count <= 4 else 1
-    left_cols, right_cols = lefts[0].shape[1], rights[0].shape[1]
+    width = shared_weights[0].shape[1] // 3 if shared_weights else 0
     grads = lambda cols: jax.ShapeDtypeStruct((wide_count // 2, shard, cols), bfloat)
-    if first:
+    if last:
+        sum_shapes = [jax.ShapeDtypeStruct((narrow_count, part, D), bfloat)] + [
+            jax.ShapeDtypeStruct((part, D + LANES), bfloat if s else single)
+            for s in range(narrow_count)
+        ]
+    else:
         sum_shapes = [jax.ShapeDtypeStruct((total, D), single)] * 2
-    else:
-        sum_shapes = (
-            [jax.ShapeDtypeStruct((part, D), single)]
-            + [jax.ShapeDtypeStruct((part, D), bfloat)] * (narrow_count - 1)
-        ) * 2
     any_space = pl.BlockSpec(memory_space=pl.ANY)
     vmem = pl.BlockSpec(memory_space=pltpu.VMEM)
-    operands = [*lefts, *rights, *norm_parts, *dy_parts, *rank_parts, *gate_parts]
-    specs = [any_space] * (2 * wide_count + 2 * narrow_count) + [vmem] * (2 * narrow_count)
+    operands = [*pieces, *shared_weights, *norm_parts, dy_all]
+    specs = [any_space] * len(operands)
+    operands += [*gating, *earlier_q]
+    specs += [vmem] * (len(operands) - len(specs))
+    gate_shapes = [jax.ShapeDtypeStruct((slots, total), single)] * 2 if first else []
     if not first:
         operands += list(sums)
         specs += [any_space] * 2
     scratch = [
-        pltpu.VMEM((buffers, D, ECOLS), bfloat),
+        pltpu.VMEM((D, ECOLS), bfloat),
         pltpu.VMEM((D, ECOLS), bfloat),
         pltpu.VMEM((total, D), bfloat),
         pltpu.VMEM((total, D), bfloat),
@@ -426,29 +462,128 @@
             pltpu.VMEM((total, width), bfloat),
             pltpu.VMEM((total, 2 * width), bfloat),
         ]
+    if first:
+        scratch.append(pltpu.VMEM((total, LANES), bfloat))
+    if last:
+        scratch += [pltpu.VMEM((total, LANES), single), pltpu.VMEM((total, LANES), bfloat)]
     scratch.append(pltpu.SemaphoreType.DMA((8,)))
-    flops = 2 * 2 * count_rows * 9 * D * FF + 6 * 2 * total * D * width
-    results = pl.pallas_call(
+    keep, give, q_row, *rest = pl.pallas_call(
         functools.partial(
-            expert_body, wide_count, narrow_count, capacity, width, first, buffers
+            expert_body, wide_count, narrow_count, capacity, width, column, first, last
         ),
         out_shape=[
-            grads(left_cols),
-            grads(left_cols),
-            grads(right_cols),
-            grads(right_cols),
-            jax.ShapeDtypeStruct((2, total), single),
+            grads(ECOLS + 3 * width),
+            grads(ECOLS + 3 * width),
+            jax.ShapeDtypeStruct((1, total), single),
+            *gate_shapes,
             *sum_shapes,
         ],
         in_specs=[pl.BlockSpec(memory_space=pltpu.SMEM)] + specs,
-        out_specs=[any_space] * 4 + [vmem] + [any_space] * len(sum_shapes),
+        out_specs=[any_space] * 2
+        + [vmem] * (1 + len(gate_shapes))
+        + [any_space] * len(sum_shapes),
         scratch_shapes=scratch,
         compiler_params=pltpu.CompilerParams(vmem_limit_bytes=60 * 2**20),
-        cost_estimate=pl.CostEstimate(
-            flops=flops, bytes_accessed=4 * D * (left_cols + right_cols), transcendentals=0
-        ),
+        cost_estimate=lasting(36 + 8 * (width > 0)),
     )(index, *operands)
-    return results[:4], results[4], results[5:]
+    if first:
+        gating = [rest.pop(0), rest.pop(0)]
+    return (keep, give), q_row, gating, rest
+
+
+RATES = dict(zip(("attention_in", "attention_out", "shared_in", "shared_out", "router", "gains", "experts_in", "experts_out"), STEP_RATES))
+
+
+def nesterov(grad, master, moment, average, rate):
+    moment_new = MOMENTUM_DECAY * moment + grad
+    master_new = master - rate * (grad + MOMENTUM_DECAY * moment_new)
+    average_new = AVERAGE_DECAY * average + (1.0 - AVERAGE_DECAY) * master_new
+    return moment_new, average_new, master_new
+
+
+def expert_update_body(term_count, rates, *refs):
+    terms = refs[:term_count]
+    states = refs[term_count : term_count + 6]
+    moment_in, state_in, moment_out, state_out = refs[-4:]
+    read = lambda ref, cols: (ref[0, :, cols] if len(ref.shape) == 3 else ref[:, cols]).astype(single)
+    for at, n, which, moment_ref, state_ref in (
+        (0, 2 * FF, 0, moment_in, state_in),
+        (2 * FF, FF, 3, moment_out, state_out),
+    ):
+        grad = sum(read(t, slice(at, at + n)) for t in terms)
+        master, moment, average = (ref[0] for ref in states[which : which + 3])
+        moment_ref[0], state_ref[0, 0], state_ref[1, 0] = nesterov(
+            grad, master, moment, average, rates[which // 3]
+        )
+
+
+def expert_update(terms, states, held, expert, rates):
+    rows = states[0].shape[1]
+    tile = 80 if rows % 80 == 0 else rows
+    specs, operands = [], []
+    for array, block in terms:
+        specs.append(pl.BlockSpec((1, tile, ECOLS), lambda i, block=block: (block, i, 0)))
+        operands.append(array)
+    for number, state in enumerate(states):
+        width = 2 * FF if number < 3 else FF
+        specs.append(pl.BlockSpec((1, tile, width), lambda i: (expert, i, 0)))
+        operands.append(state)
+    shapes, out_specs = [], []
+    for width in (2 * FF, FF):
+        shapes.append(jax.ShapeDtypeStruct((EXP_DEV, rows, width), single))
+        out_specs.append(pl.BlockSpec((1, tile, width), lambda i: (expert, i, 0)))
+        shapes.append(jax.ShapeDtypeStruct((2, EXP_DEV, rows, width), single))
+        out_specs.append(pl.BlockSpec((2, 1, tile, width), lambda i: (0, expert, i, 0)))
+    aliases = {}
+    if held is not None:
+        aliases = {len(operands) + k: k for k in range(4)}
+        operands += held
+        specs += [pl.BlockSpec(memory_space=pl.ANY)] * 4
+    return pl.pallas_call(
+        functools.partial(expert_update_body, len(terms), rates),
+        grid=(rows // tile,),
+        out_shape=shapes,
+        in_specs=specs,
+        out_specs=out_specs,
+        input_output_aliases=aliases,
+        compiler_params=pltpu.CompilerParams(vmem_limit_bytes=48 * 2**20),
+        cost_estimate=lasting(5),
+    )(*operands)
+
+
+def dense_update_body(rates, own, come, *refs):
+    states, outs = refs[:6], refs[6:]
+    moment_in, state_in, moment_out, state_out, tail = outs
+    for at, n, which, moment_ref, state_ref in (
+        (0, 3 * D, 0, moment_in, state_in),
+        (3 * D, D, 3, moment_out, state_out),
+    ):
+        cols = slice(at, at + n)
+        grad = own[:, cols].astype(single) + come[:, cols].astype(single)
+        master, moment, average = (ref[...] for ref in states[which : which + 3])
+        moment_ref[...], state_ref[0], state_ref[1] = nesterov(
+            grad, master, moment, average, rates[which // 3]
+        )
+    tail[...] = own[:, 4 * D :].astype(single) + come[:, 4 * D :].astype(single)
+
+
+def dense_update(own, come, states, rates):
+    rows = own.shape[0]
+    out = lambda *shape: jax.ShapeDtypeStruct(shape, single)
+    vmem = pl.BlockSpec(memory_space=pltpu.VMEM)
+    return pl.pallas_call(
+        functools.partial(dense_update_body, rates),
+        out_shape=[
+            out(rows, 3 * D),
+            out(2, rows, 3 * D),
+            out(rows, D),
+            out(2, rows, D),
+            out(rows, LANES),
+        ],
+        in_specs=[vmem] * 8,
+        out_specs=[vmem] * 5,
+        compiler_params=pltpu.CompilerParams(vmem_limit_bytes=48 * 2**20),
+    )(own, come, *states)
 
 
 def ring_gather(piece):
@@ -459,9 +594,8 @@
 
 
 def ring_scatter(parts):
-    count = lax.axis_size("narrow")
     total = parts[1].astype(bfloat)
-    for step in range(2, count):
+    for step in range(2, lax.axis_size("narrow")):
         total = (ring(total).astype(single) + parts[step].astype(single)).astype(bfloat)
     return parts[0], ring(total)
 
@@ -496,7 +630,7 @@
     take = lambda count: [refs.pop(0) for _ in range(count)]
     lefts, rights = take(wide_count), take(wide_count)
     x, cosines, sines, bias, perm, slot_bias = take(6)
-    hidden, second_norm, first_norm, qkv, attended, router_probs, gates, gain_rows = take(8)
+    hidden, second_norm, first_norm, qkv, attended, router_probs, router_slots, gain_rows = take(8)
     w, projected, sem = refs
     copies = pack_copies(w, lefts, rights, idx[0], sem)
     for copy in copies:
@@ -533,12 +667,11 @@
         )
     rows_mid = hidden[...]
     second_norm[...] = (rows_mid * rms_scale(rows_mid) * gain_rows[1:2, :]).astype(bfloat)
-    router_slots = dot(tail, perm[...]).astype(bfloat)
-    logits = dot(second_norm[...], router_slots) + slot_bias[...]
+    router_slots[...] = dot(tail, perm[...]).astype(bfloat)
+    logits = dot(second_norm[...], router_slots[...]) + slot_bias[...]
     exp_logits = jnp.exp(logits - jnp.max(logits, axis=-1, keepdims=True))
     probs = exp_logits / jnp.sum(exp_logits, axis=-1, keepdims=True)
     router_probs[...] = probs
-    gates[...] = probs.T[: gates.shape[0], :]
 
 
 def attention_backward_body(wide_count, routed, slots, idx, *refs):
@@ -547,7 +680,7 @@
     lefts, rights = take(wide_count), take(wide_count)
     x, cosines, sines, bias, perm = take(5)
     hidden, second_norm, first_norm, qkv, attended, router_probs, gain_rows = take(7)
-    dy, second_own, second_come, q_rows = take(4)
+    dy, second_own, second_come = take(3)
     keep_left, give_left, keep_right, give_right, input_grad = take(5)
     w, stage, grad_second, grad_hidden, grad_branch, grad_attended, grad_projected, turned, tail_rows, sems = refs
     me = idx[0]
@@ -557,8 +690,8 @@
     for copy in copies:
         copy.wait()
     probs = router_probs[...]
-    pad = jnp.zeros((LANES - slots, q_rows.shape[1]), single)
-    q = jnp.concatenate([q_rows[...], pad], axis=0).T
+    q = second_own[:, D:] + second_come[:, D:].astype(single)
+    q = q + pltpu.roll(q, LANES - slots, 1)
     grad_logits = probs * (q - jnp.sum(probs * q, axis=-1, keepdims=True))
     high = grad_logits.astype(bfloat)
     rest = (grad_logits - high.astype(single)).astype(bfloat)
@@ -684,7 +817,7 @@
             out((part, 3 * D), bfloat),
             out((part, D), bfloat),
             out((part, LANES), single),
-            out((slots, part), single),
+            out((D, LANES), bfloat),
             out((2, D), single),
         ],
         in_specs=[pl.BlockSpec(memory_space=pltpu.SMEM)]
@@ -697,9 +830,7 @@
             pltpu.SemaphoreType.DMA,
         ],
         compiler_params=pltpu.CompilerParams(vmem_limit_bytes=60 * 2**20),
-        cost_estimate=pl.CostEstimate(
-            flops=8 * part * D * D, bytes_accessed=2 * D * ACOLS, transcendentals=0
-        ),
+        cost_estimate=lasting(24),
     )(index, *lefts, *rights, *operands)
 
 
@@ -738,9 +869,7 @@
             pltpu.SemaphoreType.DMA((2,)),
         ],
         compiler_params=pltpu.CompilerParams(vmem_limit_bytes=60 * 2**20),
-        cost_estimate=pl.CostEstimate(
-            flops=16 * part * D * D, bytes_accessed=6 * D * ACOLS, transcendentals=0
-        ),
+        cost_estimate=lasting(50),
     )(index, *lefts, *rights, *operands)
 
 
@@ -799,24 +928,25 @@
         ],
         axis=1,
     )
-    shared_pack = jnp.concatenate([shared_in, shared_out.T], axis=1).astype(bfloat)
-    shared_pack = shared_pack.reshape(rows_dense, 3, narrow_count, quarter)
-    shared_pack = jnp.pad(shared_pack, ((0, 0), (0, 0), (0, 0), (0, shared_width - quarter)))
-    shared_pack = shared_pack.transpose(2, 0, 1, 3).reshape(
-        narrow_count, rows_dense, 3 * shared_width
-    )
-    shared_piece = lax.all_to_all(
-        shared_pack, "narrow", split_axis=0, concat_axis=0, tiled=True
-    ).reshape(rows_plane, 3 * shared_width)
-    expert_pack = jnp.concatenate(
-        [experts_in, experts_out.transpose(0, 2, 1)], axis=2
-    ).astype(bfloat)
-    expert_halves = [
-        (expert_pack[0], expert_pack[1]),
-        (
-            jnp.concatenate([expert_pack[2], shared_piece[:, :shared_width]], axis=1),
-            jnp.concatenate([expert_pack[3], shared_piece[:, shared_width:]], axis=1),
-        ),
+    late_in, late_out, late_shared_in, late_shared_out = lax.optimization_barrier(
+        (experts_in, experts_out, shared_in, shared_out, attention_pack)
+    )[:4]
+    expert_pack = [
+        jnp.concatenate(
+            [part for e in (h, h + 2) for part in (late_in[e], late_out[e].T)], axis=1
+        ).astype(bfloat)
+        for h in range(2)
+    ]
+    orders = [chip_bits(), chip_bits()[::-1]]
+    early = [first_hops({0: expert_pack[e]}, orders[e][0]) for e in range(2)]
+
+    attention_parts = [attention_pack]
+    for _ in range(narrow_count - 1):
+        attention_parts.append(ring(attention_parts[-1]))
+    cut = split_cols(ACOLS)
+    attention_pieces = [
+        place([p[:, :cut] for p in attention_parts]).reshape(rows_plane, cut),
+        place([p[:, cut:] for p in attention_parts]).reshape(rows_plane, ACOLS - cut),
     ]
 
     route_hot = (routes[..., None] == jnp.arange(routed, dtype=jnp.int32)).astype(single).sum(axis=2)
@@ -829,17 +959,38 @@
     ranks = jnp.einsum(
         "tu,bue->bte", below, chosen.reshape(MB, MB_TOK, slots).astype(bfloat), preferred_element_type=single
     ).reshape(own_tokens, slots)
-    rank_parts = ring_gather(jnp.where(chosen > 0.5, ranks, -1.0).T)
+    rank_own = jnp.where(chosen > 0.5, ranks, -1.0).astype(bfloat)
     grad_out = cotangent.reshape(own_tokens, D)
-    dy_parts = ring_gather(grad_out)
-
-    attention_parts = ring_gather(attention_pack)
-    attention_piece = place(attention_parts).reshape(rows_plane, ACOLS)
-    cut = split_cols(ACOLS)
-    attention_halves = gather_plane(attention_piece[:, :cut], attention_piece[:, cut:])
-    expert_full = [gather_plane(*halves) for halves in expert_halves]
-
-    wide_index = lax.axis_index("wide").reshape(1)
+    token_pack = jnp.concatenate(
+        [grad_out, jnp.pad(rank_own, ((0, 0), (0, LANES - slots)))], axis=1
+    )
+    dy_all = lax.all_gather(after(token_pack, attention_parts[-1]), "narrow")
+    early_done = [p for pieces in early for p in pieces.values()]
+    attention_chips = [
+        gather_chips(p, order, first_hops({0: p}, order[0]), early_done)
+        for p, order in zip(attention_pieces, orders)
+    ]
+    attention_halves = [core_hops(chips) for chips in attention_chips]
+
+    shared_pack = jnp.concatenate([late_shared_in, late_shared_out.T], axis=1).astype(bfloat)
+    shared_pack = shared_pack.reshape(rows_dense, 3, narrow_count, quarter)
+    shared_pack = jnp.pad(shared_pack, ((0, 0), (0, 0), (0, 0), (0, shared_width - quarter)))
+    shared_pack = shared_pack.transpose(2, 0, 1, 3).reshape(
+        narrow_count, rows_dense, 3 * shared_width
+    )
+    shared_piece = lax.all_to_all(
+        shared_pack, "narrow", split_axis=0, concat_axis=0, tiled=True
+    ).reshape(rows_plane, 3 * shared_width)
+
+    first_last = [chips[max(chips)] for chips in attention_chips]
+    own_hops = [
+        first_hops({0: after(expert_pack[h], *first_last)}, bit)
+        for h in range(2)
+        for bit in orders[h][1:2]
+    ]
+    shared_weights = lax.all_gather(shared_piece, "wide", axis=0, tiled=True)
+
+    wide_index = after(lax.axis_index("wide").reshape(1), dy_all, shared_weights)
     perm = jnp.pad(
         slot_hot_of_expert, ((0, LANES - routed), (0, LANES - slots))
     ).astype(bfloat)
@@ -856,35 +1007,58 @@
     bias = jnp.where(allowed, 0.0, MASKED).reshape(own_tokens, MB_TOK)
     rows_in = block_in.reshape(own_tokens, D)
     tables = (cosines, sines, bias, perm)
-    hidden, second_norm, first_norm, qkv, attended, router_probs, gates, gain_rows = attention_forward(
+    hidden, second_norm, first_norm, qkv, attended, router_probs, router_slots, gain_rows = attention_forward(
         *attention_halves, (rows_in, *tables, slot_bias), wide_index, routed, slots
     )
 
     norm_parts = ring_gather(second_norm)
-    gate_parts = ring_gather(gates)
-    sums = None
-    expert_grads, q_rows = [], []
-    for pair in range(2):
-        index = jnp.stack([lax.axis_index("wide"), level * EXP_DEV + 2 * pair])
-        grads, q_pair, sums = expert_pair(
-            *expert_full[pair],
-            norm_parts,
-            dy_parts,
-            rank_parts,
-            gate_parts,
+    expert_pieces = []
+    for h in range(2):
+        chips = {0: expert_pack[h], **early[h]}
+        swapped = core_hops({r: after(p, second_norm) for r, p in chips.items()}, pairs=True)
+        for number, bit in enumerate(orders[h][1:]):
+            source = {r: after(p, second_norm) for r, p in chips.items() if r or number}
+            if number == 0:
+                chips.update(own_hops[h])
+            chips.update(first_hops(source, bit))
+        late = {r: after(p, norm_parts[-1]) for r, p in chips.items() if r not in swapped}
+        swapped.update(core_hops(late, pairs=True))
+        expert_pieces.append([p for r in sorted(swapped) for p in swapped[r]])
+    tokens_in = (norm_parts, dy_all)
+    gating = [router_slots, slot_bias]
+    sums, q_rows = None, []
+    terms, bits_left = [], [order[::-1] for order in orders] * 2
+
+    def hop(e):
+        bit, bits_left[e] = bits_left[e][0], bits_left[e][1:]
+        terms[e], outgoing = scatter_hop(terms[e], bit)
+        return outgoing
+
+    for e in range(EXP_DEV):
+        index = jnp.stack([lax.axis_index("wide"), level * EXP_DEV + e, level])
+        if e == EXP_DEV - 2:
+            index = after(index, *[hop(n) for n in range(2)])
+        if e == EXP_DEV - 1:
+            index = after(index, *[hop(n) for n in range(2)])
+        grads, q_row, gating, sums = expert_call(
+            expert_pieces[e % 2],
+            e // 2 * ECOLS,
+            [shared_weights] if e == 2 else [],
+            tokens_in,
+            gating,
+            q_rows if e == EXP_DEV - 1 else [],
             sums,
             index,
             capacity,
-            shared_width if pair else 0,
+            e == EXP_DEV - 1,
         )
-        expert_grads.append(grads)
-        q_rows.append(q_pair)
-    out_parts, grad_parts = sums[:narrow_count], sums[narrow_count:]
-    q_sent = jnp.concatenate(q_rows, axis=0).reshape(EXP_DEV, narrow_count, own_tokens)
-    q_sent = place([q_sent[:, s] for s in range(narrow_count)])
-    q_back = lax.all_to_all(q_sent, "narrow", split_axis=0, concat_axis=0, tiled=True)
-    q_back = q_back.reshape(slots, own_tokens)
+        terms.append(scatter_core(*grads))
+        q_rows.append(q_row)
+    out_parts, grad_parts = sums[0], sums[1:]
     second_own, second_come = ring_scatter(grad_parts)
+    sent = [hop(e) for e in range(2) for _ in range(len(bits_left[e]))]
+    sent += [hop(e) for e in range(2, EXP_DEV)]
+    wide_index = after(wide_index, *sent)
     *attention_grads, input_grad = attention_backward(
         *attention_halves,
         (
@@ -900,93 +1074,117 @@
             grad_out,
             second_own,
             second_come,
-            q_back,
         ),
         wide_index,
         routed,
         slots,
     )
     input_grad = input_grad.reshape(MB, MB_TOK, D)
-
-    out_own, out_come = ring_scatter(out_parts)
-    block_out = hidden + out_own + out_come.astype(single)
+    attention_terms = [
+        scatter_core(*attention_grads[:2]),
+        scatter_core(*attention_grads[2:]),
+    ]
+
+    out_come = lax.psum_scatter(after(out_parts, second_come), "narrow", scatter_dimension=0)
+    block_out = hidden + out_come.astype(single)
     block_out = block_out.astype(bfloat).reshape(MB, MB_TOK, D)
 
-    shares = [scatter_plane(grads[:2], grads[2:]) for grads in expert_grads]
+    first_sent, second_sent = [], []
+    for level_bit in range(len(orders[0])):
+        for h in range(2):
+            attention_terms[h], outgoing = scatter_hop(attention_terms[h], orders[h][::-1][level_bit])
+            (second_sent if level_bit else first_sent).append(outgoing)
     attention_share = jnp.concatenate(
-        scatter_plane(attention_grads[:2], attention_grads[2:]),
-        axis=1,
-    ).reshape(narrow_count, rows_dense, ACOLS)
+        [sum(block_of(t) for t in attention_terms[h][0]) for h in range(2)], axis=1
+    ).astype(bfloat)
+    attention_share = attention_share.reshape(narrow_count, rows_dense, ACOLS)
     attention_own, attention_come = ring_scatter(
         [
             lax.dynamic_index_in_dim(attention_share, (level - s) % narrow_count, 0, False)
             for s in range(narrow_count)
         ]
     )
-    attention_share = attention_own + attention_come.astype(single)
-    shared_share = (
-        jnp.concatenate([shares[1][0][:, ECOLS:], shares[1][1][:, ECOLS:]], axis=1)
-        .astype(bfloat)
-        .reshape(narrow_count, rows_dense, 3 * shared_width)
-    )
-    expert_shares = [half[:, :ECOLS] for pair in shares for half in pair]
+    for e in range(2, EXP_DEV):
+        for _ in range(len(bits_left[e])):
+            terms[e] = {i: [(after(a, *second_sent), n) for a, n in ts] for i, ts in terms[e].items()}
+            hop(e)
+    shared_terms = [after(array[block, :, ECOLS:], *second_sent) for array, block in terms[2][0]]
+    shared_share = sum(term.astype(single) for term in shared_terms)
+    shared_share = shared_share.astype(bfloat).reshape(narrow_count, rows_dense, 3 * shared_width)
     shared_share = lax.all_to_all(
         shared_share, "narrow", split_axis=0, concat_axis=0, tiled=True
     ).reshape(narrow_count, rows_dense, 3, shared_width)[..., :quarter]
     shared_share = shared_share.transpose(1, 2, 0, 3).reshape(rows_dense, 3 * FF).astype(single)
 
-    summed = (
-        attention_share[:, : 3 * D],
-        attention_share[:, 3 * D : 4 * D],
-        shared_share[:, : 2 * FF],
-        shared_share[:, 2 * FF :].T,
-        attention_share[:, 4 * D : 4 * D + routed],
-        attention_share[:, 4 * D + routed : 4 * D + routed + 2].T,
-        jnp.stack([share[:, : 2 * FF] for share in expert_shares]),
-        jnp.stack([share[:, 2 * FF :].T for share in expert_shares]),
-    )
-    masters = (
-        attention_in,
-        attention_out,
-        shared_in,
-        shared_out,
-        router,
-        gains,
+    base_rate = 1.0 / math.sqrt(tokens)
+    rate = {name: value * base_rate for name, value in RATES.items()}
+    turn_out = lambda array: array.transpose(0, 2, 1)
+    states = (
         experts_in,
-        experts_out,
-    )
-    moments = (
-        attention_in_moment,
-        attention_out_moment,
-        shared_in_moment,
-        shared_out_moment,
-        router_moment,
-        gains_moment,
         experts_in_moment,
-        experts_out_moment,
-    )
-    averages = (
-        attention_in_average,
-        attention_out_average,
-        shared_in_average,
-        shared_out_average,
-        router_average,
-        gains_average,
         experts_in_average,
-        experts_out_average,
-    )
-    base_rate = 1.0 / math.sqrt(tokens)
-    moment_outs = []
-    states = []
-    for master, moment, average, grad_share, step_rate in zip(
-        masters, moments, averages, summed, STEP_RATES
-    ):
-        moment_new = MOMENTUM_DECAY * moment + grad_share
-        master_new = master - step_rate * base_rate * (grad_share + MOMENTUM_DECAY * moment_new)
-        average_new = AVERAGE_DECAY * average + (1.0 - AVERAGE_DECAY) * master_new
-        moment_outs.append(moment_new)
-        states.append(jnp.stack([average_new, master_new]))
-    return (block_out, input_grad, *moment_outs, *states)
+        turn_out(experts_out),
+        turn_out(experts_out_moment),
+        turn_out(experts_out_average),
+    )
+    held = None
+    for e in range(EXP_DEV):
+        held = expert_update(
+            [(after(array, *first_sent, *([out_come] if e == 2 else [])), block) for array, block in terms[e][0]],
+            states,
+ held, e, (rate["experts_in"], rate["experts_out"])
+        )
+    experts_in_new, experts_in_state, experts_out_new, experts_out_state = held
+    attention_in_new, attention_in_state, attention_out_new, attention_out_state, tail = dense_update(
+        attention_own,
+        attention_come,
+        (
+            attention_in,
+            attention_in_moment,
+            attention_in_average,
+            attention_out,
+            attention_out_moment,
+            attention_out_average,
+        ),
+        (rate["attention_in"], rate["attention_out"]),
+    )
+
+    def plain(name, grad, *old):
+        moment_new, average_new, master_new = nesterov(grad, *old, rate[name])
+        return moment_new, jnp.stack([average_new, master_new])
+
+    shared_in_new, shared_in_state = plain(
+        "shared_in", shared_share[:, : 2 * FF], shared_in, shared_in_moment, shared_in_average
+    )
+    shared_out_new, shared_out_state = plain(
+        "shared_out", shared_share[:, 2 * FF :].T, shared_out, shared_out_moment, shared_out_average
+    )
+    router_new, router_state = plain(
+        "router", tail[:, :routed], router, router_moment, router_average
+    )
+    gains_new, gains_state = plain(
+        "gains", tail[:, routed : routed + 2].T, gains, gains_moment, gains_average
+    )
+    return (
+        block_out,
+        input_grad,
+        attention_in_new,
+        attention_out_new,
+        shared_in_new,
+        shared_out_new,
+        router_new,
+        gains_new,
+        experts_in_new,
+        turn_out(experts_out_new),
+        attention_in_state,
+        attention_out_state,
+        shared_in_state,
+        shared_out_state,
+        router_state,
+        gains_state,
+        experts_in_state,
+        experts_out_state.transpose(0, 1, 3, 2),
+    )
 
 
 def solution(mesh):

time: 854 us -> 750 us (0.88)
  waiting for transfers between devices: 406 us -> 332 us
  other arithmetic: 104 us -> 67.6 us
  Pallas kernels: 214 us -> 248 us
  local copies, waits for them, and re-layouts: 58.4 us -> 31.8 us
  starting transfers between devices: 59.3 us -> 45.8 us
  between operations: 2.66 us -> 14.8 us
    ppermute x24 -> x12, waiting for transfers between devices: 197 us -> 122 us  [ring(): lax.ppermute(piece, 'narrow', [(i, (i + 1) % count) for i in range(count)])]
    pallas_call x2 -> x9, Pallas kernels: 139 us -> 174 us  [the longest x4 153 us: expert_call(): pl.pallas_call(functools.partial(expert_body, wide_count, narrow_count, c...]
    another operation x34 -> x19, other arithmetic: 46.3 us -> 14.4 us  [the longest x24 37.7 us: local(): states.append(jnp.stack([average_new, master_new]))]
    add x7 -> x1, other arithmetic: 15.4 us -> 0.08 us  [nesterov(): average_new = AVERAGE_DECAY * average + (1.0 - AVERAGE_DECAY) * master_new]
    unnamed x203 -> x128, local copies, waits for them, and re-layouts: 28.8 us -> 14.7 us
    convert_element_type x13 -> x14, other arithmetic: 22.6 us -> 35.6 us  [the longest x12 33.8 us: scatter_hop(): outgoing = outgoing.astype(bfloat)]
    reduce_scatter x0 -> x1, waiting for transfers between devices: none -> 12.8 us  [local(): lax.psum_scatter(after(out_parts, second_come), 'narrow', scatter_dimensi...]
    ppermute x60 -> x46, waiting for transfers between devices: 198 us -> 187 us  [wide_xor(): return lax.ppermute(piece, 'wide', [(i, i ^ bit) for i in range(count)])]
  transfers between devices with their start and end apart: 87 -> 63, of which waited for: 33 -> 31; matrix products, arithmetic and copies ran while one was open for 14% -> 11% of each run, Pallas kernels for 17% -> 18%
where the time goes in v3:
time: 750 us; the launch traced here: 741 us
  waiting for transfers between devices  332 us (44%)
  Pallas kernels  248 us (33%)
  other arithmetic  67.6 us (9%)
  starting transfers between devices  45.8 us (6%)
  local copies, waits for them, and re-layouts  31.8 us (4%)
  between operations  14.8 us (2%)
    ppermute x46, waiting for transfers between devices, wide_xor(): return lax.ppermute(piece, 'wide', [(i, i ^ bit) for i in range(count)])  187 us
    pallas_call x4, Pallas kernels, expert_call(): pl.pallas_call(functools.partial(expert_body, wide_count, narrow_count, c...  153 us
    ppermute x12, waiting for transfers between devices, ring(): lax.ppermute(piece, 'narrow', [(i, (i + 1) % count) for i in range(count)])  122 us
    pallas_call x1, Pallas kernels, attention_backward(): pl.pallas_call(functools.partial(attention_backward_body, wide_count, rou...  50.8 us
    convert_element_type x12, other arithmetic, scatter_hop(): outgoing = outgoing.astype(bfloat)  33.8 us
    ppermute x46, starting transfers between devices, wide_xor(): return lax.ppermute(piece, 'wide', [(i, i ^ bit) for i in range(count)])  30.7 us
    pallas_call x1, Pallas kernels, attention_forward(): pl.pallas_call(functools.partial(attention_forward_body, wide_count, rout...  23.7 us
    pallas_call x4, Pallas kernels, expert_update(): pl.pallas_call(functools.partial(expert_update_body, len(terms), rates),...  19.3 us
  transfers between devices with their start and end apart: 63, of which 31 were waited for; matrix products, arithmetic and copies ran while one was open for 11% of the time, Pallas kernels for 18%

profile of v3, /device:TPU:0, one launch (start us, length us, event | category | flops | bytes accessed | tf_op | source)
XLA Modules:
  0.0 741.1 jit_solution(17822137236980077255)
XLA Ops:
  51.3 9.0 %collective-permute-done.2 = bf16[40,5248]{1,0:T(8,128)(2,1)S(1)} collective-permute-done((bf16[40,5248]{1,0:T(8,128)(2,1)S(1)}, bf16[40,5248]{1,0:T(8,128)(2,1)S(1)}, u32[]{:S(2)}, u32[]{:S(2)}) %collective-permute-start.2) | collective-permute-done | bytes 419872 | tf_op jit(solution)/shard_map/ppermute | solution.py:56
  71.2 14.1 %collective-permute-done.4.refs_2_ = bf16[160,2688]{1,0:T(8,128)(2,1)S(1)} collective-permute-done((bf16[160,2688]{1,0:T(8,128)(2,1)}, bf16[160,2688]{1,0:T(8,128)(2,1)S(1)}, u32[]{:S(2)}, u32[]{:S(2)}) %collective-permute-start.4) | collective-permute-done | bytes 860192 | tf_op jit(solution)/shard_map/ppermute | solution.py:51
  90.1 18.2 %collective-permute-done.13.refs_10_ = bf16[160,2560]{1,0:T(8,128)(2,1)} collective-permute-done((bf16[160,2560]{1,0:T(8,128)(2,1)}, bf16[160,2560]{1,0:T(8,128)(2,1)}, u32[]{:S(2)}, u32[]{:S(2)}) %collective-permute-start.13) | collective-permute-done | bytes 819232 | tf_op jit(solution)/shard_map/ppermute | solution.py:51
  108.8 14.5 %collective-permute-done.17.refs_14_ = bf16[160,2560]{1,0:T(8,128)(2,1)} collective-permute-done((bf16[160,2560]{1,0:T(8,128)(2,1)S(1)}, bf16[160,2560]{1,0:T(8,128)(2,1)}, u32[]{:S(2)}, u32[]{:S(2)}) %collective-permute-start.17) | collective-permute-done | bytes 819232 | tf_op jit(solution)/shard_map/ppermute | solution.py:51
  131.8 23.7 %shard_map.412 = (f32[256,1280]{1,0:T(8,128)}, bf16[256,1280]{1,0:T(8,128)(2,1)}, bf16[256,1280]{1,0:T(8,128)(2,1)}, bf16[256,3840]{1,0:T(8,128)(2,1)}, bf16[256...) custom-call(s32[1]{0:T(128)} %bitcast.idx, ...), custom_call_target="tpu_custom_call" | custom-call | flops 26400000000 | bytes 1000 | tf_op jit(solution)/shard_map/pallas_call | solution.py:811
  159.1 14.9 %collective-permute-done.22.refs_9_.refs_10_ = bf16[256,1280]{1,0:T(8,128)(2,1)S(1)} collective-permute-done((bf16[256,1280]{1,0:T(8,128)(2,1)}, bf16[256,1280]{1,0:T(8,128)(2,1)S(1)}, u32[]{:S(2)}, u32[]{:S(2)}) %collective-permute-start.22) | collective-permute-done | bytes 655392 | tf_op jit(solution)/shard_map/ppermute | solution.py:56
  173.9 17.3 %collective-permute-done.23.refs_10_.refs_11_ = bf16[256,1280]{1,0:T(8,128)(2,1)S(1)} collective-permute-done((bf16[256,1280]{1,0:T(8,128)(2,1)S(1)}, bf16[256,1280]{1,0:T(8,128)(2,1)S(1)}, u32[]{:S(2)}, u32[]{:S(2)}) %collective-permute-start.23) | collective-permute-done | bytes 655392 | tf_op jit(solution)/shard_map/ppermute | solution.py:56
  196.4 11.4 %collective-permute-done.24.refs_11_.refs_12_ = bf16[256,1280]{1,0:T(8,128)(2,1)S(1)} collective-permute-done((bf16[256,1280]{1,0:T(8,128)(2,1)S(1)}, bf16[256,1280]{1,0:T(8,128)(2,1)S(1)}, u32[]{:S(2)}, u32[]{:S(2)}) %collective-permute-start.24) | collective-permute-done | bytes 655392 | tf_op jit(solution)/shard_map/ppermute | solution.py:56
  208.6 23.5 %collective-permute-done.21.refs_4_ = bf16[160,5376]{1,0:T(8,128)(2,1)} collective-permute-done((bf16[160,5376]{1,0:T(8,128)(2,1)}, bf16[160,5376]{1,0:T(8,128)(2,1)}, u32[]{:S(2)}, u32[]{:S(2)}) %collective-permute-start.21) | collective-permute-done | bytes 1720352 | tf_op jit(solution)/shard_map/ppermute | solution.py:51
  240.9 35.9 %shard_map.413 = (bf16[4,160,2688]{2,1,0:T(8,128)(2,1)}, bf16[4,160,2688]{2,1,0:T(8,128)(2,1)}, f32[1,1024]{1,0:T(1,128)}, f32[16,1024]{1,0:T(8,128)}, f32[16,10...) custom-call(s32[3]{0:T(128)} %add_add_fusion.1.idx, bf16[160,5376]{1,0:T(8,128)(2,1)} %pad_maximum_fusion.refs_0_, ...), custom_call_target="tpu_custom_call" | custom-call | flops 39600001024 | bytes 1000 | tf_op jit(solution)/shard_map/pallas_call | solution.py:470
  276.9 35.7 %shard_map.414 = (bf16[4,160,2688]{2,1,0:T(8,128)(2,1)}, bf16[4,160,2688]{2,1,0:T(8,128)(2,1)}, f32[1,1024]{1,0:T(1,128)}, f32[1024,1280]{1,0:T(8,128)}, f32[1024,1280]{1,0:T(8,128)}) custom-call(s32[3]{0:T(128)} %add_add_fusion.2.idx, bf16[160,5376]{1,0:T(8,128)(2,1)} %copy-done.28, bf16[160,5376]{1,0:T(8,128)(2,1)} %collective-permute-done.30.refs_1_, ...), custom_call_target="tpu_custom_call" | custom-call | flops 39600001024 | bytes 1000 | tf_op jit(solution)/shard_map/pallas_call | solution.py:470
  314.4 8.0 %collective-permute-done.36.refs_1_ = bf16[4,160,2688]{2,1,0:T(8,128)(2,1)S(1)} collective-permute-done((bf16[4,160,2688]{2,1,0:T(8,128)(2,1)}, bf16[4,160,2688]{2,1,0:T(8,128)(2,1)S(1)}, u32[]{:S(2)}, u32[]{:S(2)}) %collective-permute-start.36) | collective-permute-done | bytes 3440672 | tf_op jit(solution)/shard_map/ppermute | solution.py:51
  333.5 44.6 %shard_map.415 = (bf16[4,160,3456]{2,1,0:T(8,128)(2,1)}, bf16[4,160,3456]{2,1,0:T(8,128)(2,1)}, f32[1,1024]{1,0:T(1,128)}, f32[1024,1280]{1,0:T(8,128)}, f32[1024,1280]{1,0:T(8,128)}) custom-call(s32[3]{0:T(128)} %add_add_fusion.3.idx, bf16[160,5376]{1,0:T(8,128)(2,1)} %pad_maximum_fusion.refs_0_, bf16[160,5376]{1,0:T(8,128)(2,1)} %collective-permute-done.19.refs_1_, ...), custom_call_target="tpu_custom_call" | custom-call | flops 48399998976 | bytes 1000 | tf_op jit(solution)/shard_map/pallas_call | solution.py:470
  384.8 36.6 %shard_map.416 = (bf16[4,160,2688]{2,1,0:T(8,128)(2,1)}, bf16[4,160,2688]{2,1,0:T(8,128)(2,1)}, f32[1,1024]{1,0:T(1,128)}, bf16[4,256,1280]{2,1,0:T(8,128)(2,1)}...) custom-call(s32[3]{0:T(128)} %add_add_fusion.idx, ...), custom_call_target="tpu_custom_call" | custom-call | flops 39600001024 | bytes 1000 | tf_op jit(solution)/shard_map/pallas_call | solution.py:470
  423.0 19.0 %collective-permute-done.38 = bf16[256,1408]{1,0:T(8,128)(2,1)S(1)} collective-permute-done((bf16[256,1408]{1,0:T(8,128)(2,1)}, bf16[256,1408]{1,0:T(8,128)(2,1)S(1)}, u32[]{:S(2)}, u32[]{:S(2)}) %collective-permute-start.38) | collective-permute-done | bytes 720928 | tf_op jit(solution)/shard_map/ppermute | solution.py:56
  443.4 19.5 %collective-permute-done.39 = bf16[256,1408]{1,0:T(8,128)(2,1)S(1)} collective-permute-done((bf16[256,1408]{1,0:T(8,128)(2,1)S(1)}, bf16[256,1408]{1,0:T(8,128)(2,1)S(1)}, u32[]{:S(2)}, u32[]{:S(2)}) %collective-permute-start.39) | collective-permute-done | bytes 720928 | tf_op jit(solution)/shard_map/ppermute | solution.py:56
  469.7 12.1 %collective-permute-done.40.refs_30_ = bf16[256,1408]{1,0:T(8,128)(2,1)S(1)} collective-permute-done((bf16[256,1408]{1,0:T(8,128)(2,1)S(1)}, bf16[256,1408]{1,0:T(8,128)(2,1)S(1)}, u32[]{:S(2)}, u32[]{:S(2)}) %collective-permute-start.40) | collective-permute-done | bytes 720928 | tf_op jit(solution)/shard_map/ppermute | solution.py:56
  482.7 50.8 %shard_map.417 = (bf16[4,160,2688]{2,1,0:T(8,128)(2,1)}, bf16[4,160,2688]{2,1,0:T(8,128)(2,1)}, bf16[4,160,2560]{2,1,0:T(8,128)(2,1)}, bf16[4,160,2560]{2,1,0:T(8,128)(2,1)}, bf16[256,1280]{1,0:T(8,128)(2,1)}) custom-call(s32[1]{0:T(128)} %bitcast.idx, bf16[160,2688]{1,0:T(8,128)(2,1)} %bitcast.206, bf16[160,2688]{1,0:T(8,128)(2,1)} %copy-done.52, ...), custom_call_target="tpu_custom_call" | custom-call | flops 54999998464 | bytes 1000 | tf_op jit(solution)/shard_map/pallas_call | solution.py:846
  569.9 12.8 %reduce-scatter.2.cloned.1.call-done = bf16[1,256,1280]{2,1,0:T(8,128)(2,1)} async-done(((bf16[4,256,1280]{2,1,0:T(8,128)(2,1)}), bf16[1,256,1280]{2,1,0:T(8,128)(2,1)}) %reduce-scatter.2.cloned.1.call-update) | async-done | bytes 655376 | tf_op jit(solution)/shard_map/reduce_scatter | solution.py:1088
  585.4 45.8 %collective-permute-done.47 = bf16[2,160,2560]{2,1,0:T(8,128)(2,1)} collective-permute-done((bf16[2,160,2560]{2,1,0:T(8,128)(2,1)}, bf16[2,160,2560]{2,1,0:T(8,128)(2,1)}, u32[]{:S(2)}, u32[]{:S(2)}) %collective-permute-start.47) | collective-permute-done | bytes 1638432 | tf_op jit(solution)/shard_map/ppermute | solution.py:51
  633.7 11.2 %collective-permute-done.44 = bf16[2,160,2688]{2,1,0:T(8,128)(2,1)} collective-permute-done((bf16[2,160,2688]{2,1,0:T(8,128)(2,1)}, bf16[2,160,2688]{2,1,0:T(8,128)(2,1)}, u32[]{:S(2)}, u32[]{:S(2)}) %collective-permute-start.44) | collective-permute-done | bytes 1720352 | tf_op jit(solution)/shard_map/ppermute | solution.py:51
  671.7 7.8 %collective-permute-done.55.refs_3_ = bf16[1,160,2688]{2,1,0:T(8,128)(2,1)S(1)} collective-permute-done((bf16[1,160,2688]{2,1,0:T(8,128)(2,1)S(1)}, bf16[1,160,2688]{2,1,0:T(8,128)(2,1)S(1)}, u32[]{:S(2)}, u32[]{:S(2)}) %collective-permute-start.55) | collective-permute-done | bytes 860192 | tf_op jit(solution)/shard_map/ppermute | solution.py:51
  680.4 8.7 %collective-permute-done.53.refs_3_ = bf16[1,160,3456]{2,1,0:T(8,128)(2,1)S(1)} collective-permute-done((bf16[1,160,3456]{2,1,0:T(8,128)(2,1)S(1)}, bf16[1,160,3456]{2,1,0:T(8,128)(2,1)S(1)}, u32[]{:S(2)}, u32[]{:S(2)}) %collective-permute-start.53) | collective-permute-done | bytes 1105952 | tf_op jit(solution)/shard_map/ppermute | solution.py:51
  721.5 8.2 %collective-permute-done.51.come = bf16[40,5248]{1,0:T(8,128)(2,1)S(1)} collective-permute-done((bf16[40,5248]{1,0:T(8,128)(2,1)S(1)}, bf16[40,5248]{1,0:T(8,128)(2,1)S(1)}, u32[]{:S(2)}, u32[]{:S(2)}) %collective-permute-start.51) | collective-permute-done | bytes 419872 | tf_op jit(solution)/shard_map/ppermute | solution.py:56
  (344 shorter events, 222.9 us)
Async XLA Ops:
  19.7 48.4 %collective-permute-start.6 = (bf16[160,5376]{1,0:T(8,128)(2,1)}, bf16[160,5376]{1,0:T(8,128)(2,1)}, u32[]{:S(2)}, u32[]{:S(2)}) collective-permute-start(bf16[160,5376]{1,0:T(8,128)(2,1)} %pad_maximum_fusion.refs_0_), channel_id=1, source_target_pairs={{0,8},{4,12},{8,0},{12,4},{16,24},{20,28},{24,16},{28,20},{1,9},{5... | collective-permute-start | bytes 5160968 | tf_op jit(solution)/shard_map/ppermute | solution.py:51
  21.4 47.8 %collective-permute-start.7 = (bf16[160,5376]{1,0:T(8,128)(2,1)S(1)}, bf16[160,5376]{1,0:T(8,128)(2,1)}, u32[]{:S(2)}, u32[]{:S(2)}) collective-permute-start(bf16[160,5376]{1,0:T(8,128)(2,1)S(1)} %pad_maximum_fusion.1.refs_0_), channel_id=1, source_target_pairs={{0,16},{4,20},{8,24},{12,28},{16,0},{20,4},{24,8},{28,12},{1,17},{... | collective-permute-start | bytes 5160968 | tf_op jit(solution)/shard_map/ppermute | solution.py:51
  28.5 98.4 %all-gather.4.cloned.1.call-start = ((), (), s32[]{:S(2)}) async-start(), calls=%async_computation.3 | async-start | bytes 2211840 | tf_op jit(solution)/shard_map/all_gather | solution.py:991
  37.1 94.6 %all-gather.6.cloned.1.call-start = ((), (), s32[]{:S(2)}) async-start(), calls=%async_computation.5 | async-start | bytes 3604480 | tf_op jit(solution)/shard_map/all_gather | solution.py:967
  60.3 522.5 %reduce-scatter.2.cloned.1.call-start = ((), (), s32[]{:S(2)}) async-start(), calls=%async_computation.4 | async-start | bytes 3276800 | tf_op jit(solution)/shard_map/reduce_scatter | solution.py:1088
  69.2 39.2 %collective-permute-start.8 = (bf16[160,2688]{1,0:T(8,128)(2,1)}, bf16[160,2688]{1,0:T(8,128)(2,1)}, u32[]{:S(2)}, u32[]{:S(2)}) collective-permute-start(bf16[160,2688]{1,0:T(8,128)(2,1)} %bitcast.204), channel_id=1, source_target_pairs={{0,16},{4,20},{8,24},{12,28},{16,0},{20,4},{24,8},{28,12},{1,17},{... | collective-permute-start | bytes 2580488 | tf_op jit(solution)/shard_map/ppermute | solution.py:51
  85.3 38.5 %collective-permute-start.10 = (bf16[160,2688]{1,0:T(8,128)(2,1)S(1)}, bf16[160,2688]{1,0:T(8,128)(2,1)}, u32[]{:S(2)}, u32[]{:S(2)}) collective-permute-start(bf16[160,2688]{1,0:T(8,128)(2,1)S(1)} %collective-permute-done.4.refs_2_), channel_id=1, source_target_pairs={{0,16},{4,20},{8,24},{12,28},{16,0},{20,4},{24,8},{28,12},{1,17},{... | collective-permute-start | bytes 2580488 | tf_op jit(solution)/shard_map/ppermute | solution.py:51
  155.5 40.8 %collective-permute-start.26 = (bf16[160,5376]{1,0:T(8,128)(2,1)}, bf16[160,5376]{1,0:T(8,128)(2,1)}, u32[]{:S(2)}, u32[]{:S(2)}) collective-permute-start(bf16[160,5376]{1,0:T(8,128)(2,1)} %collective-permute-done.6.refs_2_), channel_id=1, source_target_pairs={{0,16},{4,20},{8,24},{12,28},{16,0},{20,4},{24,8},{28,12},{1,17},{... | collective-permute-start | bytes 5160968 | tf_op jit(solution)/shard_map/ppermute | solution.py:51
  157.1 74.9 %collective-permute-start.21 = (bf16[160,5376]{1,0:T(8,128)(2,1)}, bf16[160,5376]{1,0:T(8,128)(2,1)}, u32[]{:S(2)}, u32[]{:S(2)}) collective-permute-start(bf16[160,5376]{1,0:T(8,128)(2,1)} %pad_maximum_fusion.refs_0_), channel_id=1, source_target_pairs={{0,16},{4,20},{8,24},{12,28},{16,0},{20,4},{24,8},{28,12},{1,17},{... | collective-permute-start | bytes 5160968 | tf_op jit(solution)/shard_map/ppermute | solution.py:51
  157.6 74.4 %collective-permute-start.34 = (bf16[160,5376]{1,0:T(8,128)(2,1)}, bf16[160,5376]{1,0:T(8,128)(2,1)}, u32[]{:S(2)}, u32[]{:S(2)}) collective-permute-start(bf16[160,5376]{1,0:T(8,128)(2,1)} %collective-permute-done.7.refs_4_), channel_id=1, source_target_pairs={{0,8},{4,12},{8,0},{12,4},{16,24},{20,28},{24,16},{28,20},{1,9},{5... | collective-permute-start | bytes 5160968 | tf_op jit(solution)/shard_map/ppermute | solution.py:51
  191.3 42.4 %collective-permute-start.31 = (bf16[160,5376]{1,0:T(8,128)(2,1)S(1)}, bf16[160,5376]{1,0:T(8,128)(2,1)}, u32[]{:S(2)}, u32[]{:S(2)}) collective-permute-start(bf16[160,5376]{1,0:T(8,128)(2,1)S(1)} %pad_maximum_fusion.1.refs_0_), channel_id=1, source_target_pairs={{0,8},{4,12},{8,0},{12,4},{16,24},{20,28},{24,16},{28,20},{1,9},{5... | collective-permute-start | bytes 5160968 | tf_op jit(solution)/shard_map/ppermute | solution.py:51
  196.4 37.4 %collective-permute-start.20 = (bf16[160,5376]{1,0:T(8,128)(2,1)}, bf16[160,5376]{1,0:T(8,128)(2,1)}, u32[]{:S(2)}, u32[]{:S(2)}) collective-permute-start(bf16[160,5376]{1,0:T(8,128)(2,1)} %collective-permute-done.6.refs_2_), channel_id=1, source_target_pairs={{0,4},{4,0},{8,12},{12,8},{16,20},{20,16},{24,28},{28,24},{1,5},{5... | collective-permute-start | bytes 5160968 | tf_op jit(solution)/shard_map/ppermute | solution.py:51
  233.7 43.1 %collective-permute-start.33 = (bf16[160,5376]{1,0:T(8,128)(2,1)}, bf16[160,5376]{1,0:T(8,128)(2,1)}, u32[]{:S(2)}, u32[]{:S(2)}) collective-permute-start(bf16[160,5376]{1,0:T(8,128)(2,1)} %collective-permute-done.7.refs_4_), channel_id=1, source_target_pairs={{0,4},{4,0},{8,12},{12,8},{16,20},{20,16},{24,28},{28,24},{1,5},{5... | collective-permute-start | bytes 5160968 | tf_op jit(solution)/shard_map/ppermute | solution.py:51
  233.7 43.1 %collective-permute-start.30 = (bf16[160,5376]{1,0:T(8,128)(2,1)S(1)}, bf16[160,5376]{1,0:T(8,128)(2,1)}, u32[]{:S(2)}, u32[]{:S(2)}) collective-permute-start(bf16[160,5376]{1,0:T(8,128)(2,1)S(1)} %pad_maximum_fusion.1.refs_0_), channel_id=1, source_target_pairs={{0,4},{4,0},{8,12},{12,8},{16,20},{20,16},{24,28},{28,24},{1,5},{5... | collective-permute-start | bytes 5160968 | tf_op jit(solution)/shard_map/ppermute | solution.py:51
  234.2 42.6 %collective-permute-start.35 = (bf16[160,5376]{1,0:T(8,128)(2,1)}, bf16[160,5376]{1,0:T(8,128)(2,1)}, u32[]{:S(2)}, u32[]{:S(2)}) collective-permute-start(bf16[160,5376]{1,0:T(8,128)(2,1)} %collective-permute-done.34.refs_6_), channel_id=1, source_target_pairs={{0,4},{4,0},{8,12},{12,8},{16,20},{20,16},{24,28},{28,24},{1,5},{5... | collective-permute-start | bytes 5160968 | tf_op jit(solution)/shard_map/ppermute | solution.py:51
  236.0 40.9 %collective-permute-start.32 = (bf16[160,5376]{1,0:T(8,128)(2,1)}, bf16[160,5376]{1,0:T(8,128)(2,1)}, u32[]{:S(2)}, u32[]{:S(2)}) collective-permute-start(bf16[160,5376]{1,0:T(8,128)(2,1)} %collective-permute-done.31.refs_2_), channel_id=1, source_target_pairs={{0,4},{4,0},{8,12},{12,8},{16,20},{20,16},{24,28},{28,24},{1,5},{5... | collective-permute-start | bytes 5160968 | tf_op jit(solution)/shard_map/ppermute | solution.py:51
  327.4 50.8 %collective-permute-start.37 = (bf16[2,160,2688]{2,1,0:T(8,128)(2,1)}, bf16[2,160,2688]{2,1,0:T(8,128)(2,1)S(1)}, u32[]{:S(2)}, u32[]{:S(2)}) collective-permute-start(bf16[2,160,2688]{2,1,0:T(8,128)(2,1)} %add_convert_fusion.3), channel_id=1, source_target_pairs={{0,8},{4,12},{8,0},{12,4},{16,24},{20,28},{24,16},{28,20},{1,9},{5... | collective-permute-start | bytes 5160968 | tf_op jit(solution)/shard_map/ppermute | solution.py:51
  332.0 49.5 %collective-permute-start.29 = (bf16[2,160,2688]{2,1,0:T(8,128)(2,1)}, bf16[2,160,2688]{2,1,0:T(8,128)(2,1)S(1)}, u32[]{:S(2)}, u32[]{:S(2)}) collective-permute-start(bf16[2,160,2688]{2,1,0:T(8,128)(2,1)} %add_convert_fusion.4), channel_id=1, source_target_pairs={{0,16},{4,20},{8,24},{12,28},{16,0},{20,4},{24,8},{28,12},{1,17},{... | collective-permute-start | bytes 5160968 | tf_op jit(solution)/shard_map/ppermute | solution.py:51
  378.1 85.1 %collective-permute-start.41 = (bf16[4,160,3456]{2,1,0:T(8,128)(2,1)}, bf16[4,160,3456]{2,1,0:T(8,128)(2,1)}, u32[]{:S(2)}, u32[]{:S(2)}) collective-permute-start(bf16[4,160,3456]{2,1,0:T(8,128)(2,1)} %get-tuple-element.172), channel_id=1, source_target_pairs={{0,4},{4,0},{8,12},{12,8},{16,20},{20,16},{24,28},{28,24},{1,5},{5... | collective-permute-start | bytes 13271048 | tf_op jit(solution)/shard_map/ppermute | solution.py:51
  422.8 44.6 %collective-permute-start.42 = (bf16[4,160,2688]{2,1,0:T(8,128)(2,1)}, bf16[4,160,2688]{2,1,0:T(8,128)(2,1)S(1)}, u32[]{:S(2)}, u32[]{:S(2)}) collective-permute-start(bf16[4,160,2688]{2,1,0:T(8,128)(2,1)} %get-tuple-element.174), channel_id=1, source_target_pairs={{0,4},{4,0},{8,12},{12,8},{16,20},{20,16},{24,28},{28,24},{1,5},{5... | collective-permute-start | bytes 10321928 | tf_op jit(solution)/shard_map/ppermute | solution.py:51
  538.8 109.4 %collective-permute-start.52 = (bf16[2,160,3456]{2,1,0:T(8,128)(2,1)}, bf16[2,160,3456]{2,1,0:T(8,128)(2,1)}, u32[]{:S(2)}, u32[]{:S(2)}) collective-permute-start(bf16[2,160,3456]{2,1,0:T(8,128)(2,1)} %add_convert_fusion), channel_id=1, source_target_pairs={{0,16},{4,20},{8,24},{12,28},{16,0},{20,4},{24,8},{28,12},{1,17},{... | collective-permute-start | bytes 6635528 | tf_op jit(solution)/shard_map/ppermute | solution.py:51
  543.7 108.8 %collective-permute-start.54 = (bf16[2,160,2688]{2,1,0:T(8,128)(2,1)}, bf16[2,160,2688]{2,1,0:T(8,128)(2,1)}, u32[]{:S(2)}, u32[]{:S(2)}) collective-permute-start(bf16[2,160,2688]{2,1,0:T(8,128)(2,1)} %add_convert_fusion.2), channel_id=1, source_target_pairs={{0,8},{4,12},{8,0},{12,4},{16,24},{20,28},{24,16},{28,20},{1,9},{5... | collective-permute-start | bytes 5160968 | tf_op jit(solution)/shard_map/ppermute | solution.py:51
  547.8 83.3 %collective-permute-start.47 = (bf16[2,160,2560]{2,1,0:T(8,128)(2,1)}, bf16[2,160,2560]{2,1,0:T(8,128)(2,1)}, u32[]{:S(2)}, u32[]{:S(2)}) collective-permute-start(bf16[2,160,2560]{2,1,0:T(8,128)(2,1)} %add_convert_fusion.5), channel_id=1, source_target_pairs={{0,8},{4,12},{8,0},{12,4},{16,24},{20,28},{24,16},{28,20},{1,9},{5... | collective-permute-start | bytes 4915208 | tf_op jit(solution)/shard_map/ppermute | solution.py:51
  559.9 84.9 %collective-permute-start.44 = (bf16[2,160,2688]{2,1,0:T(8,128)(2,1)}, bf16[2,160,2688]{2,1,0:T(8,128)(2,1)}, u32[]{:S(2)}, u32[]{:S(2)}) collective-permute-start(bf16[2,160,2688]{2,1,0:T(8,128)(2,1)} %add_convert_fusion.1), channel_id=1, source_target_pairs={{0,16},{4,20},{8,24},{12,28},{16,0},{20,4},{24,8},{28,12},{1,17},{... | collective-permute-start | bytes 5160968 | tf_op jit(solution)/shard_map/ppermute | solution.py:51
  (99 other events, 1626.1 us)
Sparse Core Ops, SparseCore 0:
  37.2 33.3 all-gather.3
  72.8 58.9 all-gather.5
  534.3 48.4 reduce-scatter.1
